TPU v7x, 512 devices: a whole 4x8x8 slice. The times are simulated.
512 devices in a mesh: fx: 16 (over x, y_lo), fy: 16 (over z, core), sec: 2 (over y_hi).
Axes of the slice: x: 4, y: 8 (y_hi: 2, y_lo: 4; y = y_hi * 4 + y_lo), z: 8, core: 2. Of those that a mesh axis runs over, the one named last changes fastest.
Arguments:
- state: float32 [5, 32, 512, 256], P(None, 'fx', 'fy', 'sec'), may hold values from -6 to 6
- mixing: float32 [5, 5], replicated, may hold values from -2.5 to 2.5
- wall_weight: float32 [32, 16, 256], P('fx', 'fy', 'sec'), may hold values from 0.05 to 0.4
- patch_map: int32 [32, 16, 2, 1], P('fx', 'fy', 'sec'), may hold values from 0 to 15
- block_map: int32 [32, 16, 2, 1], P('fx', 'fy', 'sec'), may hold values from 0 to 31
- shell_disp: float32 [16, 4096], P('fx'), may hold values from -6 to 6
- shell_vel: float32 [16, 4096], P('fx'), may hold values from -6 to 6
- connect: int32 [16, 64, 2], P('fx'), may hold values from 0 to 31
- stiffness: float32 [16, 64, 128], P('fx'), may hold values from 0.25 to 1
Outputs:
- new_state: float32 [5, 32, 512, 256], P(None, 'fx', 'fy', 'sec')
- new_disp: float32 [16, 4096], P('fx')
- new_vel: float32 [16, 4096], P('fx')
Inputs may be any that keep to these rules, and one draw needn't show every extreme that they name: `patch_map`: every patch is named by some tile; some patches are named far more often than others. `connect`: block indices within one patch.
All inputs are finite; a program needn't handle non-finite values.
Results may differ from a plain program's by a relative error of at most 0.0001.
Values sent between devices are 32-bit elements; how exact they have to be, the bound alone decides.
No kernel may reach another device: no remote copies, remote signals or barrier semaphores. Data moves between devices by JAX's collectives and lax.ppermute only.
A program may use at most 64 MiB of HBM per device.

v0:
```python
import jax
import jax.numpy as jnp
from jax import lax
from jax.sharding import PartitionSpec as P

NB = 32
SUBCYCLES = 4


DIFFUSION = 0.25
TRANSPORT = 0.5
TIME_STEP = 0.2
SHELL_STEP = 0.25
DAMPING = 0.1


def extended(block, sides, width):
    for axis, dim in sides:
        count = lax.axis_size(axis)
        forward = [(i, i + 1) for i in range(count - 1)]
        backward = [(target, source) for source, target in forward]
        low = lax.ppermute(
            lax.slice_in_dim(block, block.shape[dim] - width, None, axis=dim), axis, forward
        )
        high = lax.ppermute(lax.slice_in_dim(block, 0, width, axis=dim), axis, backward)
        block = jnp.concatenate([low, block, high], axis=dim)
    return block


def rate_of(padded, mixing):
    center = padded[:, 1:-1, 1:-1, 1:-1]
    ahead = padded[:, 2:, 1:-1, 1:-1]
    behind = padded[:, :-2, 1:-1, 1:-1]
    beside = ahead + behind + padded[:, 1:-1, 2:, 1:-1] + padded[:, 1:-1, :-2, 1:-1]
    beside = beside + padded[:, 1:-1, 1:-1, 2:] + padded[:, 1:-1, 1:-1, :-2]
    mixed = jnp.einsum("vw,wxyz->vxyz", mixing, center, precision=lax.Precision.HIGHEST)
    return DIFFUSION * (beside - 6.0 * center) - TRANSPORT * 0.5 * (ahead - behind) + mixed


def fluid_rate(field, mixing):
    padded = extended(field, (("fx", 1), ("fy", 2), ("sec", 3)), 1)
    return rate_of(padded, mixing)


def shell_cycles(load, disp, vel, pairs, stiff):
    first = pairs[:, 0]
    second = pairs[:, 1]
    width = stiff.shape[1]
    count = disp.shape[0] // width
    load = load.reshape(count, width)
    disp = disp.reshape(count, width)
    vel = vel.reshape(count, width)
    samples = []
    for cycle in range(SUBCYCLES):
        stretch = stiff * (disp[first] - disp[second])
        inner = jax.ops.segment_sum(stretch, first, num_segments=count) - jax.ops.segment_sum(
            stretch, second, num_segments=count
        )
        vel = vel + SHELL_STEP * (load - inner - DAMPING * vel)
        disp = disp + SHELL_STEP * vel
        samples.append(disp.reshape(-1))
    return (disp.reshape(-1), vel.reshape(-1), jnp.stack(samples))


def shards(
    state, mixing, wall_weight, patch_map, block_map, shell_disp, shell_vel, connect, stiffness
):
    blocks = NB
    length = state.shape[3]
    patches = lax.axis_size("fx")
    weights = wall_weight[:, 0, :]
    tile_load = weights * state[4, :, 0, :]
    patch_of = patch_map[:, 0, 0, 0]
    block_of = block_map[:, 0, 0, 0]
    target = patch_of * blocks + block_of
    owner = lax.axis_index("fx")
    dense = jax.ops.segment_sum(tile_load, target, num_segments=patches * blocks).reshape(
        patches, blocks * length
    )
    summed = lax.psum(dense, ("fx", "fy", "sec"))
    load = lax.dynamic_index_in_dim(summed, owner, 0, keepdims=False)
    new_disp, new_vel, samples = shell_cycles(
        load, shell_disp[0], shell_vel[0], connect[0], stiffness[0]
    )
    first_rate = fluid_rate(state, mixing)
    section = state + TIME_STEP * first_rate
    second_rate = fluid_rate(section, mixing)
    new_state = state + 0.5 * TIME_STEP * (first_rate + second_rate)
    gathered = lax.all_gather(samples[None], "fx", axis=0, tiled=True)
    wall = jnp.mean(gathered, 1)
    wall_tiles = wall.reshape(patches * blocks, length)[target]
    new_state = new_state.at[2, :, 0, :].add(weights * wall_tiles)
    return (new_state, new_disp[None], new_vel[None])


def solution(mesh):
    return jax.shard_map(
        shards,
        mesh=mesh,
        in_specs=(
            P(None, "fx", "fy", "sec"),
            P(),
            P("fx", "fy", "sec"),
            P("fx", "fy", "sec", None),
            P("fx", "fy", "sec", None),
            P("fx", None),
            P("fx", None),
            P("fx", None, None),
            P("fx", None, None),
        ),
        out_specs=(P(None, "fx", "fy", "sec"), P("fx", None), P("fx", None)),
        check_vma=False,
    )
```

profile of v0, /device:TPU:8, one launch (start us, length us, event | category | flops | bytes accessed | tf_op | source)
XLA Modules:
  0.0 393.4 jit_solution(133905889582724776)
XLA Ops:
  7.2 1.0 copy.39
  8.3 3.6 collective-permute-start.1
  11.9 5.5 %collective-permute-start = (f32[5,1,32,128]{3,0,2,1:T(8,128)S(1)}, f32[5,1,32,128]{3,0,2,1:T(8,128)S(1)}, u32[]{:S(2)}, u32[]{:S(2)}) collective-permute-start(f32[5,1,32,128]{3,0,2,1:T(8,128)S(1)} %get-tuple-element.37), channel_id=1, source_target_pairs={{32,0},{64,32},{96,64},{128,96},{160,128},{192,160},{224,192},{256... | collective-permute-start | bytes 245768 | tf_op jit(solution)/shard_map/ppermute | solution.py:25
  17.6 0.7 copy-done.6
  18.2 0.7 scatter_custom_fusion
  18.9 0.7 reshape.107
  19.7 0.0 all-gather.4.cloned.1.call-start
  19.8 0.6 copy-done.7
  20.4 0.1 copy-done.1
  20.4 0.6 gather_fusion
  21.0 0.6 gather_fusion.1
  21.6 0.2 copy-done.3
  21.8 0.8 scatter_custom_fusion.1
  22.6 0.8 scatter_custom_fusion.2
  23.4 0.1 copy_dynamic-update-slice_fusion
  23.6 1.3 collective-permute-start.2
  24.9 3.0 collective-permute-start.3
  27.9 262.5 %all-reduce.2.cloned.1.call-done = f32[16,4096]{1,0:T(8,128)} async-done(((f32[16,4096]{1,0:T(8,128)}), f32[16,4096]{1,0:T(8,128)}) %all-reduce.2.cloned.1.call-update) | async-done | bytes 262160 | tf_op jit(solution)/shard_map/psum | solution.py:80
  290.5 0.9 constant_dynamic-slice_fusion
  291.4 0.6 gather_fusion.2
  292.0 0.6 gather_fusion.3
  292.6 0.8 scatter_custom_fusion.3
  293.4 0.8 scatter_custom_fusion.4
  294.3 0.6 gather_fusion.4
  294.9 0.6 gather_fusion.5
  295.5 0.8 scatter_custom_fusion.5
  296.3 0.8 scatter_custom_fusion.6
  297.1 0.6 gather_fusion.6
  297.7 0.6 gather_fusion.7
  298.3 0.8 scatter_custom_fusion.7
  299.1 0.8 scatter_custom_fusion.8
  299.9 0.6 multiply_add_fusion.1
  300.6 0.7 maximum_bitcast_fusion
  301.3 0.1 pad_maximum_fusion
  301.4 0.2 fusion.51
  301.6 0.3 copy.30
  301.8 4.7 %collective-permute-start.5 = (f32[5,4,34,1]{2,1,3,0:T(4,128)S(1)}, f32[5,4,34,1]{2,1,3,0:T(4,128)S(1)}, u32[]{:S(2)}, u32[]{:S(2)}) collective-permute-start(f32[5,4,34,1]{2,1,3,0:T(4,128)S(1)} %copy.30), channel_id=1, source_target_pairs={{0,1},{2,3},{4,5},{6,7},{8,9},{10,11},{12,13},{14,15},{16,17},{18,... | collective-permute-start | bytes 8168 | tf_op jit(solution)/shard_map/ppermute | solution.py:22
  306.6 0.3 copy.28
  306.8 1.3 collective-permute-start.4
  308.1 0.3 copy.31
  308.5 7.9 %collective-permute-done.4 = f32[5,4,34,1]{2,1,3,0:T(4,128)S(1)} collective-permute-done((f32[5,4,34,1]{2,1,3,0:T(4,128)S(1)}, f32[5,4,34,1]{2,1,3,0:T(4,128)S(1)}, u32[]{:S(2)}, u32[]{:S(2)}) %collective-permute-start.4) | collective-permute-done | bytes 2752 | tf_op jit(solution)/shard_map/ppermute | solution.py:25
  316.4 0.3 copy.29
  316.8 0.7 multiply_add_fusion
  317.4 4.5 %collective-permute-start.6 = (f32[5,1,32,128]{3,0,2,1:T(8,128)S(1)}, f32[5,1,32,128]{3,0,2,1:T(8,128)S(1)}, u32[]{:S(2)}, u32[]{:S(2)}) collective-permute-start(f32[5,1,32,128]{3,0,2,1:T(8,128)S(1)} %get-tuple-element.36), channel_id=1, source_target_pairs={{32,0},{64,32},{96,64},{128,96},{160,128},{192,160},{224,192},{256... | collective-permute-start | bytes 245768 | tf_op jit(solution)/shard_map/ppermute | solution.py:25
  322.0 1.9 collective-permute-start.7
  323.9 2.5 collective-permute-done.6
  326.4 2.9 collective-permute-done.7
  329.3 1.3 collective-permute-start.8
  330.6 3.0 collective-permute-start.9
  333.6 0.8 collective-permute-done.9
  334.4 0.1 pad_maximum_fusion.1
  334.5 0.2 fusion.50
  334.7 0.3 copy.37
  334.9 1.7 collective-permute-start.11
  336.7 0.3 copy.35
  336.9 1.3 collective-permute-start.10
  338.3 0.3 copy.38
  338.6 8.1 %collective-permute-done.10 = f32[5,4,34,1]{2,1,3,0:T(4,128)S(1)} collective-permute-done((f32[5,4,34,1]{2,1,3,0:T(4,128)S(1)}, f32[5,4,34,1]{2,1,3,0:T(4,128)S(1)}, u32[]{:S(2)}, u32[]{:S(2)}) %collective-permute-start.10) | collective-permute-done | bytes 2752 | tf_op jit(solution)/shard_map/ppermute | solution.py:25
  346.7 0.3 copy.36
  347.0 0.6 fusion.7
  347.6 35.7 %all-gather.4.cloned.1.call-done = f32[16,4,4096]{2,1,0:T(4,128)} async-done(((f32[1,4,4096]{2,1,0:T(4,128)}), f32[16,4,4096]{2,1,0:T(4,128)}) %all-gather.4.cloned.1.call-update) | async-done | bytes 1048592 | tf_op jit(solution)/shard_map/all_gather | solution.py:89
  383.3 1.9 reduce_sum.9
  385.3 0.6 gather_fusion.8
  385.9 0.7 copy.41
  (45 shorter events, 0.4 us)
Async XLA Ops:
  7.2 309.6 %copy-start = (f32[5,5]{1,0:T(8,128)S(1)}, f32[5,5]{1,0:T(8,128)}, u32[]{:S(2)}) copy-start(f32[5,5]{1,0:T(8,128)} %param.12) | copy-start | bytes 304
  7.2 283.3 %all-reduce.2.cloned.1.call-start = ((), (), s32[]{:S(2)}) async-start(), calls=%async_computation | async-start | bytes 524288 | tf_op jit(solution)/shard_map/psum | solution.py:80
  8.2 9.2 %copy-start.2 = (f32[5,2,32,128]{3,2,1,0:T(8,128)S(1)}, f32[5,2,32,128]{3,2,1,0:T(8,128)}, u32[]{:S(2)}) copy-start(f32[5,2,32,128]{3,2,1,0:T(8,128)} %param.11) | copy-start | bytes 491524
  8.3 15.1 %collective-permute-start.1 = (f32[5,1,32,128]{3,0,2,1:T(8,128)S(1)}, f32[5,1,32,128]{3,0,2,1:T(8,128)S(1)}, u32[]{:S(2)}, u32[]{:S(2)}) collective-permute-start(f32[5,1,32,128]{3,0,2,1:T(8,128)S(1)} %get-tuple-element.38), channel_id=1, source_target_pairs={{0,32},{32,64},{64,96},{96,128},{128,160},{160,192},{192,224},{224... | collective-permute-start | bytes 245768 | tf_op jit(solution)/shard_map/ppermute | solution.py:22
  11.9 5.6 %copy-start.8 = (s32[2,1,1,1]{0,3,2,1:T(1,128)S(1)}, s32[2,1,1,1]{0,3,2,1:T(1,128)}, u32[]{:S(2)}) copy-start(s32[2,1,1,1]{0,3,2,1:T(1,128)} %param.15) | copy-start | bytes 28
  11.9 5.6 %copy-start.9 = (s32[2,1,1,1]{0,3,2,1:T(1,128)S(1)}, s32[2,1,1,1]{0,3,2,1:T(1,128)}, u32[]{:S(2)}) copy-start(s32[2,1,1,1]{0,3,2,1:T(1,128)} %param.14) | copy-start | bytes 28
  11.9 11.6 %collective-permute-start = (f32[5,1,32,128]{3,0,2,1:T(8,128)S(1)}, f32[5,1,32,128]{3,0,2,1:T(8,128)S(1)}, u32[]{:S(2)}, u32[]{:S(2)}) collective-permute-start(f32[5,1,32,128]{3,0,2,1:T(8,128)S(1)} %get-tuple-element.37), channel_id=1, source_target_pairs={{32,0},{64,32},{96,64},{128,96},{160,128},{192,160},{224,192},{256... | collective-permute-start | bytes 245768 | tf_op jit(solution)/shard_map/ppermute | solution.py:25
  17.5 0.7 copy-start.6
  19.7 0.7 copy-start.7
  19.7 0.7 copy-start.1
  19.7 363.6 %all-gather.4.cloned.1.call-start = ((), (), s32[]{:S(2)}) async-start(), calls=%async_computation.1 | async-start | bytes 1114112 | tf_op jit(solution)/shard_map/all_gather | solution.py:89
  21.0 0.8 copy-start.3
  23.6 277.7 %collective-permute-start.2 = (f32[5,4,1,128]{3,0,2,1:T(8,128)S(1)}, f32[5,4,1,128]{3,0,2,1:T(8,128)S(1)}, u32[]{:S(2)}, u32[]{:S(2)}) collective-permute-start(f32[5,4,1,128]{3,0,2,1:T(8,128)S(1)} %get-tuple-element.34), channel_id=1, source_target_pairs={{2,0},{4,2},{6,4},{8,6},{10,8},{12,10},{14,12},{16,14},{18,16},{20... | collective-permute-start | bytes 30728 | tf_op jit(solution)/shard_map/ppermute | solution.py:25
  24.9 266.5 %copy-start.5 = (f32[1,4096]{1,0:T(1,128)S(1)}, f32[1,4096]{1,0:T(1,128)}, u32[]{:S(2)}) copy-start(f32[1,4096]{1,0:T(1,128)} %param.17) | copy-start | bytes 49156
  24.9 276.4 %collective-permute-start.3 = (f32[5,4,1,128]{3,0,2,1:T(8,128)S(1)}, f32[5,4,1,128]{3,0,2,1:T(8,128)S(1)}, u32[]{:S(2)}, u32[]{:S(2)}) collective-permute-start(f32[5,4,1,128]{3,0,2,1:T(8,128)S(1)} %get-tuple-element.33), channel_id=1, source_target_pairs={{0,2},{2,4},{4,6},{6,8},{8,10},{10,12},{12,14},{14,16},{16,18},{18... | collective-permute-start | bytes 30728 | tf_op jit(solution)/shard_map/ppermute | solution.py:22
  300.6 0.7 copy-start.4
  301.8 6.3 %collective-permute-start.5 = (f32[5,4,34,1]{2,1,3,0:T(4,128)S(1)}, f32[5,4,34,1]{2,1,3,0:T(4,128)S(1)}, u32[]{:S(2)}, u32[]{:S(2)}) collective-permute-start(f32[5,4,34,1]{2,1,3,0:T(4,128)S(1)} %copy.30), channel_id=1, source_target_pairs={{0,1},{2,3},{4,5},{6,7},{8,9},{10,11},{12,13},{14,15},{16,17},{18,... | collective-permute-start | bytes 8168 | tf_op jit(solution)/shard_map/ppermute | solution.py:22
  306.8 9.6 %collective-permute-start.4 = (f32[5,4,34,1]{2,1,3,0:T(4,128)S(1)}, f32[5,4,34,1]{2,1,3,0:T(4,128)S(1)}, u32[]{:S(2)}, u32[]{:S(2)}) collective-permute-start(f32[5,4,34,1]{2,1,3,0:T(4,128)S(1)} %copy.28), channel_id=1, source_target_pairs={{1,0},{3,2},{5,4},{7,6},{9,8},{11,10},{13,12},{15,14},{17,16},{19,... | collective-permute-start | bytes 8168 | tf_op jit(solution)/shard_map/ppermute | solution.py:25
  317.4 9.0 %collective-permute-start.6 = (f32[5,1,32,128]{3,0,2,1:T(8,128)S(1)}, f32[5,1,32,128]{3,0,2,1:T(8,128)S(1)}, u32[]{:S(2)}, u32[]{:S(2)}) collective-permute-start(f32[5,1,32,128]{3,0,2,1:T(8,128)S(1)} %get-tuple-element.36), channel_id=1, source_target_pairs={{32,0},{64,32},{96,64},{128,96},{160,128},{192,160},{224,192},{256... | collective-permute-start | bytes 245768 | tf_op jit(solution)/shard_map/ppermute | solution.py:25
  322.0 7.3 %collective-permute-start.7 = (f32[5,1,32,128]{3,0,2,1:T(8,128)S(1)}, f32[5,1,32,128]{3,0,2,1:T(8,128)S(1)}, u32[]{:S(2)}, u32[]{:S(2)}) collective-permute-start(f32[5,1,32,128]{3,0,2,1:T(8,128)S(1)} %get-tuple-element.35), channel_id=1, source_target_pairs={{0,32},{32,64},{64,96},{96,128},{128,160},{160,192},{192,224},{224... | collective-permute-start | bytes 245768 | tf_op jit(solution)/shard_map/ppermute | solution.py:22
  329.3 4.3 %collective-permute-start.8 = (f32[5,4,1,128]{3,0,2,1:T(8,128)S(1)}, f32[5,4,1,128]{3,0,2,1:T(8,128)S(1)}, u32[]{:S(2)}, u32[]{:S(2)}) collective-permute-start(f32[5,4,1,128]{3,0,2,1:T(8,128)S(1)} %get-tuple-element.32), channel_id=1, source_target_pairs={{2,0},{4,2},{6,4},{8,6},{10,8},{12,10},{14,12},{16,14},{18,16},{20... | collective-permute-start | bytes 30728 | tf_op jit(solution)/shard_map/ppermute | solution.py:25
  330.6 3.9 collective-permute-start.9
  334.9 3.3 collective-permute-start.11
  336.9 9.7 %collective-permute-start.10 = (f32[5,4,34,1]{2,1,3,0:T(4,128)S(1)}, f32[5,4,34,1]{2,1,3,0:T(4,128)S(1)}, u32[]{:S(2)}, u32[]{:S(2)}) collective-permute-start(f32[5,4,34,1]{2,1,3,0:T(4,128)S(1)} %copy.35), channel_id=1, source_target_pairs={{1,0},{3,2},{5,4},{7,6},{9,8},{11,10},{13,12},{15,14},{17,16},{19,... | collective-permute-start | bytes 8168 | tf_op jit(solution)/shard_map/ppermute | solution.py:25
Sparse Core Ops, SparseCore 0:
  19.8 270.6 all-reduce.1
  301.4 81.8 all-gather.3
where the time goes:
time: 394 us; the launch traced here: 393 us
  waiting for transfers between devices  320 us (81%)
  starting transfers between devices  33.3 us (8%)
  between operations  14.5 us (4%)
  local copies, waits for them, and re-layouts  13.3 us (3%)
  other arithmetic  10.5 us (3%)
    psum x1, waiting for transfers between devices, shards(): summed = lax.psum(dense, ('fx', 'fy', 'sec'))  263 us
    all_gather x1, waiting for transfers between devices, shards(): gathered = lax.all_gather(samples[None], 'fx', axis=0, tiled=True)  35.7 us
    ppermute x6, waiting for transfers between devices, extended(): lax.ppermute(lax.slice_in_dim(block, 0, width, axis=dim), axis, backward)  18.5 us
    ppermute x6, starting transfers between devices, extended(): lax.ppermute(lax.slice_in_dim(block, block.shape[dim] - width, None, axis...  18 us
    ppermute x6, starting transfers between devices, extended(): lax.ppermute(lax.slice_in_dim(block, 0, width, axis=dim), axis, backward)  15.2 us
  transfers between devices with their start and end apart: 14, of which 7 were waited for; matrix products, arithmetic and copies ran while one was open for 5% of the time, Pallas kernels for 0%

commit v1 on v0

v1 whole, which is shorter than its diff:
```python
import jax
import jax.numpy as jnp
from jax import lax
from jax.experimental import pallas as pl
from jax.experimental.pallas import tpu as pltpu
from jax.sharding import PartitionSpec as P

NV = 5
NB = 32
SUBCYCLES = 4
LANES = 128

DIFFUSION = 0.25
TRANSPORT = 0.5
TIME_STEP = 0.2
SHELL_STEP = 0.25
DAMPING = 0.1

TOP = 8
ROWS = 48

VM = pl.BlockSpec(memory_space=pltpu.VMEM)
SM = pl.BlockSpec(memory_space=pltpu.SMEM)


def kernel_call(body, outs, ins, scratch=(), cost=20000):
    return pl.pallas_call(
        body,
        out_shape=outs,
        in_specs=ins,
        out_specs=jax.tree.map(lambda _: VM, outs),
        scratch_shapes=scratch,
        cost_estimate=pl.CostEstimate(flops=cost, bytes_accessed=cost, transcendentals=0),
    )


def f32(*shape):
    return jax.ShapeDtypeStruct(shape, jnp.float32)


def offer_body(patch_ref, block_ref, weight_ref, state_ref, out_ref):
    rows = []
    for tile in range(2):
        rows.append(weight_ref[tile] * state_ref[0, tile, 0:1, :])
    for tile in range(2):
        target = patch_ref[tile, 0, 0, 0] * NB + block_ref[tile, 0, 0, 0]
        rows.append(jnp.full((1, LANES), target.astype(jnp.float32)))
    rows = jnp.concatenate(rows, axis=0)
    for receiver in range(out_ref.shape[0]):
        out_ref[receiver] = rows


def offer(patch_map, block_map, weight, state, receivers):
    return pl.pallas_call(
        offer_body,
        grid=(1,),
        out_shape=f32(receivers, 4, LANES),
        in_specs=[
            SM,
            SM,
            pl.BlockSpec((2, 1, LANES), lambda i: (0, 0, 0)),
            pl.BlockSpec((1, 2, 8, LANES), lambda i: (4, 0, 0, 0)),
        ],
        out_specs=pl.BlockSpec((receivers, 4, LANES), lambda i: (0, 0, 0)),
        cost_estimate=pl.CostEstimate(flops=4096, bytes_accessed=65536, transcendentals=0),
    )(patch_map, block_map, weight, state)


def collect_body(tiles_ref, out_ref):
    base = (lax.axis_index("fx") * NB).astype(jnp.float32)
    block = lax.broadcasted_iota(jnp.int32, (NB, LANES), 0).astype(jnp.float32) + base
    sums = [jnp.zeros((NB, LANES), jnp.float32) for _ in range(4)]
    for sender in range(tiles_ref.shape[0]):
        for tile in range(2):
            load = tiles_ref[sender, tile : tile + 1, :]
            target = tiles_ref[sender, 2 + tile : 3 + tile, :]
            slot = (2 * sender + tile) % 4
            sums[slot] = sums[slot] + jnp.where(block == target, load, 0.0)
    total = (sums[0] + sums[1]) + (sums[2] + sums[3])
    for receiver in range(out_ref.shape[0]):
        out_ref[receiver] = total


def pieces(x):
    high = x.astype(jnp.bfloat16)
    rest = x - high.astype(jnp.float32)
    middle = rest.astype(jnp.bfloat16)
    low = (rest - middle.astype(jnp.float32)).astype(jnp.bfloat16)
    return jnp.concatenate([high, middle, low], axis=0)


def thrice(select):
    select = select.astype(jnp.bfloat16)
    return jnp.concatenate([select, select, select], axis=1)


def picked(select3, x):
    return jnp.dot(select3, pieces(x), preferred_element_type=jnp.float32)


def shell_body(
    loads_ref, tiles_ref, disp_ref, vel_ref, connect_ref, stiff_ref, disp_out, vel_out, wall_out
):
    elements = stiff_ref.shape[0]
    lane = lax.broadcasted_iota(jnp.int32, (elements, LANES), 1)
    first = connect_ref[:, 0:1]
    second = connect_ref[:, 1:2]
    ends = (lane == first).astype(jnp.float32) - (lane == second).astype(jnp.float32)
    gather = thrice(ends[:, :NB])
    scatter = thrice(ends.T[:NB, :])

    base = (lax.axis_index("fx") * NB).astype(jnp.float32)
    sec = lax.axis_index("sec")
    peers = wall_out.shape[0]
    targets = [
        tiles_ref[2 * peer + sec, 2 + tile : 3 + tile, :]
        for peer in range(peers)
        for tile in range(2)
    ]
    targets = jnp.concatenate(targets, axis=0)[:, :NB]
    block = lax.broadcasted_iota(jnp.int32, (2 * peers, NB), 1).astype(jnp.float32) + base
    wanted = thrice((block == targets).astype(jnp.float32))

    stiff = stiff_ref[...]
    disp = disp_ref[...]
    vel = vel_ref[...]
    load = loads_ref[0]
    for sender in range(1, loads_ref.shape[0]):
        load = load + loads_ref[sender]
    total = jnp.zeros_like(disp)
    for _ in range(SUBCYCLES):
        stretch = stiff * picked(gather, disp)
        inner = picked(scatter, stretch)
        vel = vel + SHELL_STEP * (load - inner - DAMPING * vel)
        disp = disp + SHELL_STEP * vel
        total = total + disp
    disp_out[...] = disp
    vel_out[...] = vel
    wall = picked(wanted, total * (1.0 / SUBCYCLES))
    for peer in range(peers):
        wall_out[peer] = wall[2 * peer : 2 * peer + 2, :]


def finish_body(walls_ref, weight_ref, state_ref, out_ref):
    wall = walls_ref[0]
    for owner in range(1, walls_ref.shape[0]):
        wall = wall + walls_ref[owner]
    row = lax.broadcasted_iota(jnp.int32, (8, LANES), 0)
    for tile in range(2):
        gain = weight_ref[tile] * wall[tile : tile + 1, :]
        out_ref[0, tile] = state_ref[0, tile] + jnp.where(row == 0, gain, 0.0)


def finish(walls, weight, state):
    owners = walls.shape[0]
    part = pl.BlockSpec((1, 2, 8, LANES), lambda i: (2, 0, 0, 0))
    return pl.pallas_call(
        finish_body,
        grid=(1,),
        out_shape=f32(*state.shape),
        in_specs=[
            pl.BlockSpec((owners, 2, LANES), lambda i: (0, 0, 0)),
            pl.BlockSpec((2, 1, LANES), lambda i: (0, 0, 0)),
            part,
        ],
        out_specs=part,
        input_output_aliases={2: 0},
        cost_estimate=pl.CostEstimate(flops=4096, bytes_accessed=65536, transcendentals=0),
    )(walls, weight, state)


def slab(low_ref, state_ref, high_ref, v, xi):
    if xi == 0:
        return low_ref.at[v, 1]
    if xi == 3:
        return high_ref.at[v, 0]
    return state_ref.at[v, xi - 1]


def pack_sec_body(low_ref, state_ref, high_ref, out_ref):
    sec = lax.axis_index("sec")
    lane = lax.broadcasted_iota(jnp.int32, (32, LANES), 1)
    packed = jnp.zeros((32, LANES), jnp.float32)
    for v in range(NV):
        for xi in range(4):
            first = 8 * v + 2 * xi
            moved = pltpu.roll(
                slab(low_ref, state_ref, high_ref, v, xi)[...], first + 2 * (1 - sec), axis=1
            )
            packed = jnp.where((lane == first) | (lane == first + 1), moved, packed)
    out_ref[...] = packed


def pack_span_body(low_ref, state_ref, high_ref, beyond_ref, top_ref, bottom_ref):
    last = state_ref.shape[2] - 1
    for out, rows in ((top_ref, (0, 1)), (bottom_ref, (last, last - 1))):
        for place, y in enumerate(rows):
            for v in range(NV):
                for xi in range(4):
                    spot = 8 * v + 4 * place + xi
                    out[spot : spot + 1, :] = slab(low_ref, state_ref, high_ref, v, xi)[
                        y : y + 1, :
                    ]
            out[8 * NV + place : 8 * NV + place + 1, :] = beyond_ref[y : y + 1, :]
        out[8 * NV + 2 :, :] = jnp.zeros((6, LANES), jnp.float32)


def stencil(center, ahead, behind, others, mixed):
    beside = ahead + behind + others
    return DIFFUSION * (beside - 6.0 * center) - TRANSPORT * 0.5 * (ahead - behind) + mixed


def fluid_body(
    mixing_ref,
    low_ref,
    state_ref,
    high_ref,
    edge_ref,
    beyond_ref,
    top_ref,
    bottom_ref,
    before_ref,
    after_ref,
    out_ref,
    field,
    section,
    packed,
):
    size = state_ref.shape[2]
    end = TOP + size
    sec = lax.axis_index("sec")
    fx = lax.axis_index("fx")
    fy = lax.axis_index("fy")
    inside_low = (fx > 0).astype(jnp.float32)
    inside_high = (fx < lax.axis_size("fx") - 1).astype(jnp.float32)
    inside_before = (fy > 0).astype(jnp.float32)
    inside_after = (fy < lax.axis_size("fy") - 1).astype(jnp.float32)
    mix = [[mixing_ref[v, w] for w in range(NV)] for v in range(NV)]

    lane = lax.broadcasted_iota(jnp.int32, (1, LANES), 1)
    open_lane = (LANES - 1) * (1 - sec)
    keep_low = (lane != 0).astype(jnp.float32)
    keep_high = (lane != LANES - 1).astype(jnp.float32)
    at_open = (lane == open_lane).astype(jnp.float32)

    def along_z(cells, columns, v, xi):
        moved = pltpu.roll(columns, LANES - 1 - (8 * v + 2 * xi), axis=1)
        return (
            keep_low * pltpu.roll(cells, 1, axis=1)
            + keep_high * pltpu.roll(cells, LANES - 1, axis=1)
            + at_open * moved
        )

    def mixed(cells, v):
        total = mix[v][0] * cells[0]
        for w in range(1, NV):
            total = total + mix[v][w] * cells[w]
        return total

    packed[TOP:end, :] = beyond_ref[...]
    packed[TOP - 1 : TOP, :] = before_ref[8 * NV : 8 * NV + 1, :]
    packed[end : end + 1, :] = after_ref[8 * NV : 8 * NV + 1, :]
    beyond = beyond_ref[...]
    group = lane // 8
    mixed_columns = jnp.zeros((size, LANES), jnp.float32)
    for shift in range(1 - NV, NV):
        factor = jnp.zeros((1, LANES), jnp.float32)
        for v in range(NV):
            if 0 <= v - shift < NV:
                factor = jnp.where(group == v, mix[v][v - shift], factor)
        source = beyond if shift == 0 else pltpu.roll(beyond, (8 * shift) % LANES, axis=1)
        mixed_columns = mixed_columns + factor * source
    column_rate = stencil(
        beyond,
        pltpu.roll(beyond, LANES - 2, axis=1),
        pltpu.roll(beyond, 2, axis=1),
        packed[TOP - 1 : end - 1, :]
        + packed[TOP + 1 : end + 1, :]
        + pltpu.roll(beyond + edge_ref[...], 1 + (LANES - 2) * (1 - sec), axis=1),
        mixed_columns,
    )
    column_section = beyond + TIME_STEP * column_rate

    row = lax.broadcasted_iota(jnp.int32, (8, LANES), 0)
    inside_rows = jnp.where(row < 4, inside_before, inside_after)
    row_cells = []
    row_others = []
    row_columns = jnp.where(
        row < 4, before_ref[8 * NV : 8 * NV + 1, :], after_ref[8 * NV : 8 * NV + 1, :]
    )
    for v in range(NV):
        cells = jnp.concatenate(
            [before_ref[8 * v : 8 * v + 4, :], after_ref[8 * v : 8 * v + 4, :]], axis=0
        )
        outer = jnp.concatenate(
            [before_ref[8 * v + 4 : 8 * v + 8, :], after_ref[8 * v + 4 : 8 * v + 8, :]], axis=0
        )
        inner = jnp.concatenate(
            [top_ref[8 * v : 8 * v + 4, :], bottom_ref[8 * v : 8 * v + 4, :]], axis=0
        )
        columns = jnp.zeros((8, LANES), jnp.float32)
        for xi in (1, 2):
            moved = pltpu.roll(row_columns, LANES - 1 - (8 * v + 2 * xi), axis=1)
            columns = jnp.where((row == xi) | (row == 4 + xi), moved, columns)
        across = (
            keep_low * pltpu.roll(cells, 1, axis=1)
            + keep_high * pltpu.roll(cells, LANES - 1, axis=1)
            + at_open * columns
        )
        row_cells.append(cells)
        row_others.append(outer + inner + across)
    for v in range(NV):
        cells = row_cells[v]
        rate = stencil(
            cells,
            pltpu.roll(cells, 7, axis=0),
            pltpu.roll(cells, 1, axis=0),
            row_others[v],
            mixed(row_cells, v),
        )
        after = inside_rows * (cells + TIME_STEP * rate)
        for xi in (1, 2):
            section[v, xi, TOP - 1 : TOP, :] = after[xi : xi + 1, :]
            section[v, xi, end : end + 1, :] = after[4 + xi : 5 + xi, :]

    for v in range(NV):
        for xi in range(4):
            field[v, xi, TOP:end, :] = slab(low_ref, state_ref, high_ref, v, xi)[...]
            field[v, xi, TOP - 1 : TOP, :] = before_ref[8 * v + xi : 8 * v + xi + 1, :]
            field[v, xi, end : end + 1, :] = after_ref[8 * v + xi : 8 * v + xi + 1, :]

    def center(v, x):
        if x < 0:
            return low_ref[v, 0]
        if x > 3:
            return high_ref[v, 1]
        return field[v, x, TOP:end, :]

    for xi in range(4):
        cells = [center(w, xi) for w in range(NV)]
        for v in range(NV):
            others = (
                field[v, xi, TOP - 1 : end - 1, :]
                + field[v, xi, TOP + 1 : end + 1, :]
                + along_z(cells[v], beyond, v, xi)
            )
            rate = stencil(
                cells[v], center(v, xi + 1), center(v, xi - 1), others, mixed(cells, v)
            )
            after = cells[v] + TIME_STEP * rate
            if xi == 0:
                after = inside_low * after
            if xi == 3:
                after = inside_high * after
            section[v, xi, TOP:end, :] = after
            if xi in (1, 2):
                out_ref[v, xi - 1] = cells[v] + 0.5 * TIME_STEP * rate

    for xi in (1, 2):
        cells = [section[w, xi, TOP:end, :] for w in range(NV)]
        for v in range(NV):
            others = (
                section[v, xi, TOP - 1 : end - 1, :]
                + section[v, xi, TOP + 1 : end + 1, :]
                + along_z(cells[v], column_section, v, xi)
            )
            rate = stencil(
                cells[v],
                section[v, xi + 1, TOP:end, :],
                section[v, xi - 1, TOP:end, :],
                others,
                mixed(cells, v),
            )
            out_ref[v, xi - 1] = out_ref[v, xi - 1] + 0.5 * TIME_STEP * rate


def shards(
    state, mixing, wall_weight, patch_map, block_map, shell_disp, shell_vel, connect, stiffness
):
    nfx, nfy, nsec = (lax.axis_size(axis) for axis in ("fx", "fy", "sec"))
    up_x = [(i, i + 1) for i in range(nfx - 1)]
    down_x = [(i + 1, i) for i in range(nfx - 1)]
    up_y = [(i, i + 1) for i in range(nfy - 1)]
    down_y = [(i + 1, i) for i in range(nfy - 1)]

    offered = offer(patch_map, block_map, wall_weight, state, nfx * nsec)
    tiles = lax.all_to_all(offered, ("fx", "sec"), 0, 0, tiled=True)

    low = lax.ppermute(state, "fx", up_x)
    high = lax.ppermute(state, "fx", down_x)

    partial = kernel_call(collect_body, f32(nfy, NB, LANES), [VM])(tiles)
    loads = lax.all_to_all(partial, "fy", 0, 0, tiled=True)

    edge = kernel_call(pack_sec_body, f32(32, LANES), [VM] * 3)(low, state, high)
    beyond = lax.ppermute(edge, "sec", [(0, 1), (1, 0)])
    span = f32(8 * NV + 8, LANES)
    top, bottom = kernel_call(pack_span_body, (span, span), [VM] * 4)(low, state, high, beyond)
    before = lax.ppermute(bottom, "fy", up_y)
    after = lax.ppermute(top, "fy", down_y)

    new_disp, new_vel, walls = kernel_call(
        shell_body, (f32(NB, LANES), f32(NB, LANES), f32(nfx, 2, LANES)), [VM] * 6
    )(
        loads,
        tiles,
        shell_disp.reshape(NB, LANES),
        shell_vel.reshape(NB, LANES),
        connect[0],
        stiffness[0],
    )
    walls = lax.all_to_all(walls, "fx", 0, 0, tiled=True)

    fluid = kernel_call(
        fluid_body,
        f32(*state.shape),
        [SM] + [VM] * 9,
        scratch=[
            pltpu.VMEM((NV, 4, ROWS, LANES), jnp.float32),
            pltpu.VMEM((NV, 4, ROWS, LANES), jnp.float32),
            pltpu.VMEM((ROWS, LANES), jnp.float32),
        ],
    )(mixing, low, state, high, edge, beyond, top, bottom, before, after)
    new_state = finish(walls, wall_weight, fluid)
    return (new_state, new_disp.reshape(1, -1), new_vel.reshape(1, -1))


def solution(mesh):
    return jax.shard_map(
        shards,
        mesh=mesh,
        in_specs=(
            P(None, "fx", "fy", "sec"),
            P(),
            P("fx", "fy", "sec"),
            P("fx", "fy", "sec", None),
            P("fx", "fy", "sec", None),
            P("fx", None),
            P("fx", None),
            P("fx", None, None),
            P("fx", None, None),
        ),
        out_specs=(P(None, "fx", "fy", "sec"), P("fx", None), P("fx", None)),
        check_vma=False,
    )
```

time: 394 us -> 84.9 us (0.22)
  the two profiles are of different devices: /device:TPU:8 before, /device:TPU:57 now
where the time goes in v1:
time: 84.9 us; the launch traced here: 84.3 us
  starting transfers between devices  37.6 us (44%)
  blocking collectives  15.8 us (19%)
  Pallas kernels  13.3 us (16%)
  waiting for transfers between devices  10.8 us (13%)
  local copies, waits for them, and re-layouts  5.85 us (7%)
    all_to_all x1, blocking collectives, shards(): tiles = lax.all_to_all(offered, ('fx', 'sec'), 0, 0, tiled=True)  15.8 us
    all_to_all x1, starting transfers between devices, shards(): loads = lax.all_to_all(partial, 'fy', 0, 0, tiled=True)  12.4 us
    ppermute x1, starting transfers between devices, shards(): beyond = lax.ppermute(edge, 'sec', [(0, 1), (1, 0)])  6.84 us
    all_to_all x1, starting transfers between devices, shards(): walls = lax.all_to_all(walls, 'fx', 0, 0, tiled=True)  6.03 us
    ppermute x1, starting transfers between devices, shards(): before = lax.ppermute(bottom, 'fy', up_y)  5.17 us
    unnamed x22, local copies, waits for them, and re-layouts  5.14 us
    ppermute x1, waiting for transfers between devices, shards(): high = lax.ppermute(state, 'fx', down_x)  5.09 us
    ppermute x1, waiting for transfers between devices, shards(): after = lax.ppermute(top, 'fy', down_y)  3.41 us
  transfers between devices with their start and end apart: 7, of which 3 were waited for; matrix products, arithmetic and copies ran while one was open for 1% of the time, Pallas kernels for 11%

profile of v1, /device:TPU:57, one launch (start us, length us, event | category | flops | bytes accessed | tf_op | source)
XLA Modules:
  0.0 84.3 jit_solution(16851359720460645912)
XLA Ops:
  0.6 0.0 copy-start.9
  0.6 1.3 %copy.13.patch_ref = s32[2,1,1,1]{3,2,1,0:T(1,128)} copy(s32[2,1,1,1]{0,3,2,1:T(1,128)} %param.12) | data formatting | bytes 16 | tf_op args[3]
  1.9 0.0 copy-done.9
  1.9 0.6 copy.14.block_ref
  2.6 1.4 %shard_map.112 = f32[32,4,128]{2,1,0:T(4,128)} custom-call(s32[2,1,1,1]{3,2,1,0:T(1,128)} %copy.13.patch_ref, s32[2,1,1,1]{3,2,1,0:T(1,128)} %copy.14.block_ref, f32[2,1,128]{2,1,0:T(1,128)} %weight_ref.3, f32[5,2,32,128]{3,2,1,0:T(8,128)} %state_ref.7), custom_call_target="tpu_custom_call" | custom-call | flops 4096 | bytes 65536 | tf_op jit(solution)/shard_map/pallas_call | solution.py:54
  4.0 15.8 %all_to_all.15.tiles_ref = f32[32,4,128]{2,1,0:T(4,128)} all-to-all(f32[32,4,128]{2,1,0:T(4,128)} %shard_map.112), channel_id=1, replica_groups=mesh['fx'=16,'fy'=16,'sec'=2] {'fx','sec'}, dimensions={0} | all-to-all | bytes 131072 | tf_op jit(solution)/shard_map/all_to_all | solution.py:387
  19.8 1.7 %shard_map.113 = f32[16,32,128]{2,1,0:T(8,128)} custom-call(f32[32,4,128]{2,1,0:T(4,128)} %all_to_all.15.tiles_ref), custom_call_target="tpu_custom_call" | custom-call | flops 20000 | bytes 20000 | tf_op jit(solution)/shard_map/pallas_call | solution.py:392
  21.5 0.0 copy-start
  21.5 12.4 %all-to-all-start.1 = ((f32[16,32,128]{2,1,0:T(8,128)}), f32[16,32,128]{2,1,0:T(8,128)S(1)}, u32[]{:S(2)}, u32[]{:S(2)}) async-start(f32[16,32,128]{2,1,0:T(8,128)} %shard_map.113), calls=%async_computation.1 | async-start | bytes 524288 | tf_op jit(solution)/shard_map/all_to_all | solution.py:393
  33.8 0.0 copy-done
  33.8 2.7 %collective-permute-start = (f32[5,2,32,128]{3,2,1,0:T(8,128)S(1)}, f32[5,2,32,128]{3,2,1,0:T(8,128)S(1)}, u32[]{:S(2)}, u32[]{:S(2)}) collective-permute-start(f32[5,2,32,128]{3,2,1,0:T(8,128)S(1)} %copy-done), channel_id=1, source_target_pairs={{0,32},{32,64},{64,96},{96,128},{128,160},{160,192},{192,224},{224... | collective-permute-start | bytes 491528 | tf_op jit(solution)/shard_map/ppermute | solution.py:389
  36.6 2.6 %collective-permute-start.1 = (f32[5,2,32,128]{3,2,1,0:T(8,128)S(1)}, f32[5,2,32,128]{3,2,1,0:T(8,128)S(1)}, u32[]{:S(2)}, u32[]{:S(2)}) collective-permute-start(f32[5,2,32,128]{3,2,1,0:T(8,128)S(1)} %copy-done), channel_id=1, source_target_pairs={{32,0},{64,32},{96,64},{128,96},{160,128},{192,160},{224,192},{256... | collective-permute-start | bytes 491528 | tf_op jit(solution)/shard_map/ppermute | solution.py:390
  39.2 2.3 %collective-permute-done.low_ref = f32[5,2,32,128]{3,2,1,0:T(8,128)S(1)} collective-permute-done((f32[5,2,32,128]{3,2,1,0:T(8,128)S(1)}, f32[5,2,32,128]{3,2,1,0:T(8,128)S(1)}, u32[]{:S(2)}, u32[]{:S(2)}) %collective-permute-start) | collective-permute-done | bytes 163872 | tf_op jit(solution)/shard_map/ppermute | solution.py:389
  41.5 0.0 copy-start.1
  41.5 5.1 %collective-permute-done.1.high_ref = f32[5,2,32,128]{3,2,1,0:T(8,128)S(1)} collective-permute-done((f32[5,2,32,128]{3,2,1,0:T(8,128)S(1)}, f32[5,2,32,128]{3,2,1,0:T(8,128)S(1)}, u32[]{:S(2)}, u32[]{:S(2)}) %collective-permute-start.1) | collective-permute-done | bytes 163872 | tf_op jit(solution)/shard_map/ppermute | solution.py:390
  46.6 0.0 copy-done.1
  46.6 0.0 copy-start.2
  46.6 0.7 copy-done.2
  47.3 1.8 %shard_map.115.edge_ref = f32[32,128]{1,0:T(8,128)} custom-call(f32[5,2,32,128]{3,2,1,0:T(8,128)} %copy-done.1, f32[5,2,32,128]{3,2,1,0:T(8,128)} %state_ref.7, f32[5,2,32,128]{3,2,1,0:T(8,128)} %copy-done.2), custom_call_target="tpu_custom_call" | custom-call | flops 20000 | bytes 20000 | tf_op jit(solution)/shard_map/pallas_call | solution.py:395
  49.1 0.0 copy-start.8
  49.1 6.8 %collective-permute-start.2 = (f32[32,128]{1,0:T(8,128)}, f32[32,128]{1,0:T(8,128)S(1)}, u32[]{:S(2)}, u32[]{:S(2)}) collective-permute-start(f32[32,128]{1,0:T(8,128)} %shard_map.115.edge_ref), channel_id=1, source_target_pairs={{0,1},{1,0},{2,3},{3,2},{4,5},{5,4},{6,7},{7,6},{8,9},{9,8},{10,11... | collective-permute-start | bytes 49160 | tf_op jit(solution)/shard_map/ppermute | solution.py:396
  56.0 0.0 copy-done.8
  56.0 0.7 copy.15.connect_ref
  56.7 0.0 all-to-all-done.1.loads_ref
  56.7 0.0 copy-start.3
  56.7 0.7 copy-done.3
  57.4 3.0 %shard_map.114 = (f32[32,128]{1,0:T(8,128)}, f32[32,128]{1,0:T(8,128)}, f32[16,2,128]{2,1,0:T(2,128)}) custom-call(f32[16,32,128]{2,1,0:T(8,128)} %copy-done.3, f32[32,4,128]{2,1,0:T(4,128)} %all_to_all.15.tiles_ref, f32[32,128]{1,0:T(8,128)} %bitcast.7, f32[32,128]{1,0:T(8,128)} %bitcast.8, s32[64,2]{1,0:T(8,128)} %copy.15.connect_ref, f32[64,128]{1,0:T(8,128)} %bitcast.6), custom_call_target="tpu_custom_call" | custom-call | flops 20000 | bytes 20000 | tf_op jit(solution)/shard_map/pallas_call | solution.py:402
  60.4 6.0 %all-to-all-start.2 = ((f32[16,2,128]{2,1,0:T(2,128)}), f32[16,2,128]{2,1,0:T(2,128)S(1)}, u32[]{:S(2)}, u32[]{:S(2)}) async-start(f32[16,2,128]{2,1,0:T(2,128)} %get-tuple-element.8), calls=%async_computation.2 | async-start | bytes 32768 | tf_op jit(solution)/shard_map/all_to_all | solution.py:412
  66.4 0.0 collective-permute-done.2.beyond_ref
  66.4 0.0 copy-start.4
  66.5 0.6 copy-done.4
  67.0 1.7 %shard_map.116 = (f32[48,128]{1,0:T(8,128)}, f32[48,128]{1,0:T(8,128)}) custom-call(f32[5,2,32,128]{3,2,1,0:T(8,128)} %copy-done.1, f32[5,2,32,128]{3,2,1,0:T(8,128)} %state_ref.7, f32[5,2,32,128]{3,2,1,0:T(8,128)} %copy-done.2, f32[32,128]{1,0:T(8,128)} %copy-done.4), custom_call_target="tpu_custom_call" | custom-call | flops 20000 | bytes 20000 | tf_op jit(solution)/shard_map/pallas_call | solution.py:398
  68.8 5.2 %collective-permute-start.3 = (f32[48,128]{1,0:T(8,128)}, f32[48,128]{1,0:T(8,128)S(1)}, u32[]{:S(2)}, u32[]{:S(2)}) collective-permute-start(f32[48,128]{1,0:T(8,128)} %get-tuple-element.10.bottom_ref), channel_id=1, source_target_pairs={{0,2},{2,4},{4,6},{6,8},{8,10},{10,12},{12,14},{14,16},{16,18},{18... | collective-permute-start | bytes 73736 | tf_op jit(solution)/shard_map/ppermute | solution.py:399
  73.9 1.9 %collective-permute-start.4 = (f32[48,128]{1,0:T(8,128)}, f32[48,128]{1,0:T(8,128)S(1)}, u32[]{:S(2)}, u32[]{:S(2)}) collective-permute-start(f32[48,128]{1,0:T(8,128)} %get-tuple-element.9.top_ref), channel_id=1, source_target_pairs={{2,0},{4,2},{6,4},{8,6},{10,8},{12,10},{14,12},{16,14},{18,16},{20... | collective-permute-start | bytes 73736 | tf_op jit(solution)/shard_map/ppermute | solution.py:400
  75.9 0.0 collective-permute-done.3.before_ref
  75.9 0.0 copy-start.6
  75.9 3.4 %collective-permute-done.4.after_ref = f32[48,128]{1,0:T(8,128)S(1)} collective-permute-done((f32[48,128]{1,0:T(8,128)}, f32[48,128]{1,0:T(8,128)S(1)}, u32[]{:S(2)}, u32[]{:S(2)}) %collective-permute-start.4) | collective-permute-done | bytes 24608 | tf_op jit(solution)/shard_map/ppermute | solution.py:400
  79.3 0.0 copy-done.6
  79.3 0.0 copy-start.7
  79.3 0.6 copy-done.7
  79.9 2.4 %shard_map.117.state_ref = f32[5,2,32,128]{3,2,1,0:T(8,128)} custom-call(f32[5,5]{1,0:T(8,128)} %mixing_ref.1, f32[5,2,32,128]{3,2,1,0:T(8,128)} %copy-done.1, f32[5,2,32,128]{3,2,1,0:T(8,128)} %state_ref.7, f32[5,2,32,128]{3,2,1,0:T(8,128)} %copy-done.2, f32[32,128]{1,0:T(8,128)} %shard_map.115.edge_ref, f32[32,128]{1,0:T(8,128)} %copy-done.4, ...), custom_call_target="tpu_custom_call" | custom-call | flops 20000 | bytes 20000 | tf_op jit(solution)/shard_map/pallas_call | solution.py:414
  82.3 0.0 all-to-all-done.2.walls_ref
  82.3 0.0 copy-start.5
  82.3 0.6 copy-done.5
  82.9 1.4 %shard_map.118 = f32[5,2,32,128]{3,2,1,0:T(8,128)} custom-call(f32[16,2,128]{2,1,0:T(2,128)} %copy-done.5, f32[2,1,128]{2,1,0:T(1,128)} %weight_ref.3, f32[5,2,32,128]{3,2,1,0:T(8,128)} %shard_map.117.state_ref), custom_call_target="tpu_custom_call", output_to_operand_aliasing={{}: (2, {})} | custom-call | flops 4096 | bytes 65536 | tf_op jit(solution)/shard_map/pallas_call | solution.py:157
Async XLA Ops:
  0.6 1.3 %copy-start.9 = (s32[2,1,1,1]{0,3,2,1:T(1,128)S(1)}, s32[2,1,1,1]{0,3,2,1:T(1,128)}, u32[]{:S(2)}) copy-start(s32[2,1,1,1]{0,3,2,1:T(1,128)} %param.13) | copy-start | bytes 28
  21.5 12.4 %copy-start = (f32[5,2,32,128]{3,2,1,0:T(8,128)S(1)}, f32[5,2,32,128]{3,2,1,0:T(8,128)}, u32[]{:S(2)}) copy-start(f32[5,2,32,128]{3,2,1,0:T(8,128)} %state_ref.7) | copy-start | bytes 491524
  21.5 35.2 %all-to-all-start.1 = ((f32[16,32,128]{2,1,0:T(8,128)}), f32[16,32,128]{2,1,0:T(8,128)S(1)}, u32[]{:S(2)}, u32[]{:S(2)}) async-start(f32[16,32,128]{2,1,0:T(8,128)} %shard_map.113), calls=%async_computation.1 | async-start | bytes 524288 | tf_op jit(solution)/shard_map/all_to_all | solution.py:393
  33.8 7.7 %collective-permute-start = (f32[5,2,32,128]{3,2,1,0:T(8,128)S(1)}, f32[5,2,32,128]{3,2,1,0:T(8,128)S(1)}, u32[]{:S(2)}, u32[]{:S(2)}) collective-permute-start(f32[5,2,32,128]{3,2,1,0:T(8,128)S(1)} %copy-done), channel_id=1, source_target_pairs={{0,32},{32,64},{64,96},{96,128},{128,160},{160,192},{192,224},{224... | collective-permute-start | bytes 491528 | tf_op jit(solution)/shard_map/ppermute | solution.py:389
  36.6 10.0 %collective-permute-start.1 = (f32[5,2,32,128]{3,2,1,0:T(8,128)S(1)}, f32[5,2,32,128]{3,2,1,0:T(8,128)S(1)}, u32[]{:S(2)}, u32[]{:S(2)}) collective-permute-start(f32[5,2,32,128]{3,2,1,0:T(8,128)S(1)} %copy-done), channel_id=1, source_target_pairs={{32,0},{64,32},{96,64},{128,96},{160,128},{192,160},{224,192},{256... | collective-permute-start | bytes 491528 | tf_op jit(solution)/shard_map/ppermute | solution.py:390
  41.5 5.1 %copy-start.1 = (f32[5,2,32,128]{3,2,1,0:T(8,128)}, f32[5,2,32,128]{3,2,1,0:T(8,128)S(1)}, u32[]{:S(2)}) copy-start(f32[5,2,32,128]{3,2,1,0:T(8,128)S(1)} %collective-permute-done.low_ref) | copy-start | bytes 491524
  46.6 0.7 copy-start.2
  49.1 6.9 %copy-start.8 = (s32[1,64,2]{1,2,0:T(2,128)S(1)}, s32[1,64,2]{1,2,0:T(2,128)}, u32[]{:S(2)}) copy-start(s32[1,64,2]{1,2,0:T(2,128)} %param.16) | copy-start | bytes 1540
  49.1 17.3 %collective-permute-start.2 = (f32[32,128]{1,0:T(8,128)}, f32[32,128]{1,0:T(8,128)S(1)}, u32[]{:S(2)}, u32[]{:S(2)}) collective-permute-start(f32[32,128]{1,0:T(8,128)} %shard_map.115.edge_ref), channel_id=1, source_target_pairs={{0,1},{1,0},{2,3},{3,2},{4,5},{5,4},{6,7},{7,6},{8,9},{9,8},{10,11... | collective-permute-start | bytes 49160 | tf_op jit(solution)/shard_map/ppermute | solution.py:396
  56.7 0.7 copy-start.3
  60.4 21.9 %all-to-all-start.2 = ((f32[16,2,128]{2,1,0:T(2,128)}), f32[16,2,128]{2,1,0:T(2,128)S(1)}, u32[]{:S(2)}, u32[]{:S(2)}) async-start(f32[16,2,128]{2,1,0:T(2,128)} %get-tuple-element.8), calls=%async_computation.2 | async-start | bytes 32768 | tf_op jit(solution)/shard_map/all_to_all | solution.py:412
  66.4 0.6 copy-start.4
  68.8 7.1 %collective-permute-start.3 = (f32[48,128]{1,0:T(8,128)}, f32[48,128]{1,0:T(8,128)S(1)}, u32[]{:S(2)}, u32[]{:S(2)}) collective-permute-start(f32[48,128]{1,0:T(8,128)} %get-tuple-element.10.bottom_ref), channel_id=1, source_target_pairs={{0,2},{2,4},{4,6},{6,8},{8,10},{10,12},{12,14},{14,16},{16,18},{18... | collective-permute-start | bytes 73736 | tf_op jit(solution)/shard_map/ppermute | solution.py:399
  73.9 5.4 %collective-permute-start.4 = (f32[48,128]{1,0:T(8,128)}, f32[48,128]{1,0:T(8,128)S(1)}, u32[]{:S(2)}, u32[]{:S(2)}) collective-permute-start(f32[48,128]{1,0:T(8,128)} %get-tuple-element.9.top_ref), channel_id=1, source_target_pairs={{2,0},{4,2},{6,4},{8,6},{10,8},{12,10},{14,12},{16,14},{18,16},{20... | collective-permute-start | bytes 73736 | tf_op jit(solution)/shard_map/ppermute | solution.py:400
  75.9 3.4 %copy-start.6 = (f32[48,128]{1,0:T(8,128)}, f32[48,128]{1,0:T(8,128)S(1)}, u32[]{:S(2)}) copy-start(f32[48,128]{1,0:T(8,128)S(1)} %collective-permute-done.3.before_ref) | copy-start | bytes 73732
  79.3 0.6 copy-start.7
  82.3 0.6 copy-start.5

commit v2 on v1

--- a/solution.py
+++ b/solution.py
@@ -21,6 +21,8 @@
 
 VM = pl.BlockSpec(memory_space=pltpu.VMEM)
 SM = pl.BlockSpec(memory_space=pltpu.SMEM)
+ANY = pl.BlockSpec(memory_space=pl.ANY)
+SMALL = pltpu.CompilerParams(vmem_limit_bytes=8 * 1024 * 1024)
 
 
 def kernel_call(body, outs, ins, scratch=(), cost=20000):
@@ -30,6 +32,7 @@
         in_specs=ins,
         out_specs=jax.tree.map(lambda _: VM, outs),
         scratch_shapes=scratch,
+        compiler_params=SMALL,
         cost_estimate=pl.CostEstimate(flops=cost, bytes_accessed=cost, transcendentals=0),
     )
 
@@ -43,7 +46,7 @@
     for tile in range(2):
         rows.append(weight_ref[tile] * state_ref[0, tile, 0:1, :])
     for tile in range(2):
-        target = patch_ref[tile, 0, 0, 0] * NB + block_ref[tile, 0, 0, 0]
+        target = patch_ref[tile] * NB + block_ref[tile]
         rows.append(jnp.full((1, LANES), target.astype(jnp.float32)))
     rows = jnp.concatenate(rows, axis=0)
     for receiver in range(out_ref.shape[0]):
@@ -58,15 +61,16 @@
         in_specs=[
             SM,
             SM,
-            pl.BlockSpec((2, 1, LANES), lambda i: (0, 0, 0)),
+            VM,
             pl.BlockSpec((1, 2, 8, LANES), lambda i: (4, 0, 0, 0)),
         ],
-        out_specs=pl.BlockSpec((receivers, 4, LANES), lambda i: (0, 0, 0)),
+        out_specs=VM,
+        compiler_params=SMALL,
         cost_estimate=pl.CostEstimate(flops=4096, bytes_accessed=65536, transcendentals=0),
     )(patch_map, block_map, weight, state)
 
 
-def collect_body(tiles_ref, out_ref):
+def collect_body(tiles_ref, _, out_ref):
     base = (lax.axis_index("fx") * NB).astype(jnp.float32)
     block = lax.broadcasted_iota(jnp.int32, (NB, LANES), 0).astype(jnp.float32) + base
     sums = [jnp.zeros((NB, LANES), jnp.float32) for _ in range(4)]
@@ -81,47 +85,29 @@
         out_ref[receiver] = total
 
 
-def pieces(x):
-    high = x.astype(jnp.bfloat16)
-    rest = x - high.astype(jnp.float32)
-    middle = rest.astype(jnp.bfloat16)
-    low = (rest - middle.astype(jnp.float32)).astype(jnp.bfloat16)
-    return jnp.concatenate([high, middle, low], axis=0)
-
-
-def thrice(select):
-    select = select.astype(jnp.bfloat16)
-    return jnp.concatenate([select, select, select], axis=1)
-
-
-def picked(select3, x):
-    return jnp.dot(select3, pieces(x), preferred_element_type=jnp.float32)
+def couple_body(connect_ref, stiff_ref, out_ref):
+    elements = stiff_ref.shape[0]
+    block = lax.broadcasted_iota(jnp.int32, (NB, elements), 0)
+    first = connect_ref[0:1, :]
+    second = connect_ref[1:2, :]
+    ends = (block == first).astype(jnp.float32) - (block == second).astype(jnp.float32)
+    pairs = [(ends * ends[a : a + 1, :]).astype(jnp.bfloat16) for a in range(NB)]
+    pairs = jnp.concatenate(pairs, axis=0)
+    rest = stiff_ref[...]
+    total = None
+    for _ in range(3):
+        term = rest.astype(jnp.bfloat16)
+        rest = rest - term.astype(jnp.float32)
+        product = jnp.dot(pairs, term, preferred_element_type=jnp.float32)
+        total = product if total is None else total + product
+    out_ref[...] = total.reshape(NB, NB, LANES)
 
 
 def shell_body(
-    loads_ref, tiles_ref, disp_ref, vel_ref, connect_ref, stiff_ref, disp_out, vel_out, wall_out
+    loads_ref, tiles_ref, couple_ref, disp_ref, vel_ref, _, disp_out, vel_out, wall_out
 ):
-    elements = stiff_ref.shape[0]
-    lane = lax.broadcasted_iota(jnp.int32, (elements, LANES), 1)
-    first = connect_ref[:, 0:1]
-    second = connect_ref[:, 1:2]
-    ends = (lane == first).astype(jnp.float32) - (lane == second).astype(jnp.float32)
-    gather = thrice(ends[:, :NB])
-    scatter = thrice(ends.T[:NB, :])
-
     base = (lax.axis_index("fx") * NB).astype(jnp.float32)
     sec = lax.axis_index("sec")
-    peers = wall_out.shape[0]
-    targets = [
-        tiles_ref[2 * peer + sec, 2 + tile : 3 + tile, :]
-        for peer in range(peers)
-        for tile in range(2)
-    ]
-    targets = jnp.concatenate(targets, axis=0)[:, :NB]
-    block = lax.broadcasted_iota(jnp.int32, (2 * peers, NB), 1).astype(jnp.float32) + base
-    wanted = thrice((block == targets).astype(jnp.float32))
-
-    stiff = stiff_ref[...]
     disp = disp_ref[...]
     vel = vel_ref[...]
     load = loads_ref[0]
@@ -129,44 +115,45 @@
         load = load + loads_ref[sender]
     total = jnp.zeros_like(disp)
     for _ in range(SUBCYCLES):
-        stretch = stiff * picked(gather, disp)
-        inner = picked(scatter, stretch)
+        inner = [jnp.zeros_like(disp) for _ in range(4)]
+        for a in range(NB):
+            inner[a % 4] = inner[a % 4] + couple_ref[a] * disp[a : a + 1, :]
+        inner = (inner[0] + inner[1]) + (inner[2] + inner[3])
         vel = vel + SHELL_STEP * (load - inner - DAMPING * vel)
         disp = disp + SHELL_STEP * vel
         total = total + disp
+    wall = total * (1.0 / SUBCYCLES)
+    block = lax.broadcasted_iota(jnp.int32, (NB, LANES), 0).astype(jnp.float32) + base
+    for peer in range(wall_out.shape[0]):
+        for tile in range(2):
+            target = tiles_ref[2 * peer + sec, 2 + tile : 3 + tile, :]
+            wanted = jnp.where(block == target, wall, 0.0)
+            wall_out[peer, tile : tile + 1, :] = jnp.sum(wanted, axis=0, keepdims=True)
     disp_out[...] = disp
     vel_out[...] = vel
-    wall = picked(wanted, total * (1.0 / SUBCYCLES))
-    for peer in range(peers):
-        wall_out[peer] = wall[2 * peer : 2 * peer + 2, :]
-
-
-def finish_body(walls_ref, weight_ref, state_ref, out_ref):
+
+
+def finish_body(walls_ref, weight_ref, part_ref, _, out_ref):
     wall = walls_ref[0]
     for owner in range(1, walls_ref.shape[0]):
         wall = wall + walls_ref[owner]
     row = lax.broadcasted_iota(jnp.int32, (8, LANES), 0)
     for tile in range(2):
         gain = weight_ref[tile] * wall[tile : tile + 1, :]
-        out_ref[0, tile] = state_ref[0, tile] + jnp.where(row == 0, gain, 0.0)
-
-
-def finish(walls, weight, state):
-    owners = walls.shape[0]
-    part = pl.BlockSpec((1, 2, 8, LANES), lambda i: (2, 0, 0, 0))
+        out_ref[0, tile] = part_ref[tile] + jnp.where(row == 0, gain, 0.0)
+
+
+def finish(walls, weight, part, state):
     return pl.pallas_call(
         finish_body,
         grid=(1,),
         out_shape=f32(*state.shape),
-        in_specs=[
-            pl.BlockSpec((owners, 2, LANES), lambda i: (0, 0, 0)),
-            pl.BlockSpec((2, 1, LANES), lambda i: (0, 0, 0)),
-            part,
-        ],
-        out_specs=part,
-        input_output_aliases={2: 0},
+        in_specs=[VM, VM, VM, ANY],
+        out_specs=pl.BlockSpec((1, 2, 8, LANES), lambda i: (2, 0, 0, 0)),
+        input_output_aliases={3: 0},
+        compiler_params=SMALL,
         cost_estimate=pl.CostEstimate(flops=4096, bytes_accessed=65536, transcendentals=0),
-    )(walls, weight, state)
+    )(walls, weight, part, state)
 
 
 def slab(low_ref, state_ref, high_ref, v, xi):
@@ -180,15 +167,19 @@
 def pack_sec_body(low_ref, state_ref, high_ref, out_ref):
     sec = lax.axis_index("sec")
     lane = lax.broadcasted_iota(jnp.int32, (32, LANES), 1)
-    packed = jnp.zeros((32, LANES), jnp.float32)
-    for v in range(NV):
-        for xi in range(4):
-            first = 8 * v + 2 * xi
-            moved = pltpu.roll(
-                slab(low_ref, state_ref, high_ref, v, xi)[...], first + 2 * (1 - sec), axis=1
-            )
-            packed = jnp.where((lane == first) | (lane == first + 1), moved, packed)
-    out_ref[...] = packed
+
+    def pack(shift):
+        packed = jnp.zeros((32, LANES), jnp.float32)
+        for v in range(NV):
+            for xi in range(4):
+                first = 8 * v + 2 * xi
+                cells = slab(low_ref, state_ref, high_ref, v, xi)[...]
+                moved = pltpu.roll(cells, first + shift, axis=1) if first + shift else cells
+                packed = jnp.where((lane == first) | (lane == first + 1), moved, packed)
+        out_ref[...] = packed
+
+    pl.when(sec == 0)(lambda: pack(2))
+    pl.when(sec == 1)(lambda: pack(0))
 
 
 def pack_span_body(low_ref, state_ref, high_ref, beyond_ref, top_ref, bottom_ref):
@@ -222,6 +213,7 @@
     before_ref,
     after_ref,
     out_ref,
+    part_ref,
     field,
     section,
     packed,
@@ -371,7 +363,10 @@
                 others,
                 mixed(cells, v),
             )
-            out_ref[v, xi - 1] = out_ref[v, xi - 1] + 0.5 * TIME_STEP * rate
+            final = out_ref[v, xi - 1] + 0.5 * TIME_STEP * rate
+            out_ref[v, xi - 1] = final
+            if v == 2:
+                part_ref[xi - 1] = final[:8, :]
 
 
 def shards(
@@ -383,37 +378,36 @@
     up_y = [(i, i + 1) for i in range(nfy - 1)]
     down_y = [(i + 1, i) for i in range(nfy - 1)]
 
-    offered = offer(patch_map, block_map, wall_weight, state, nfx * nsec)
-    tiles = lax.all_to_all(offered, ("fx", "sec"), 0, 0, tiled=True)
-
     low = lax.ppermute(state, "fx", up_x)
     high = lax.ppermute(state, "fx", down_x)
 
-    partial = kernel_call(collect_body, f32(nfy, NB, LANES), [VM])(tiles)
-    loads = lax.all_to_all(partial, "fy", 0, 0, tiled=True)
+    offered = offer(
+        patch_map.reshape(2), block_map.reshape(2), wall_weight, state, nfx * nsec
+    )
+    tiles = lax.all_to_all(offered, ("fx", "sec"), 0, 0, tiled=True)
 
     edge = kernel_call(pack_sec_body, f32(32, LANES), [VM] * 3)(low, state, high)
     beyond = lax.ppermute(edge, "sec", [(0, 1), (1, 0)])
+    couple = kernel_call(couple_body, f32(NB, NB, LANES), [VM] * 2)(
+        connect[0].T, stiffness[0]
+    )
+
+    partial = kernel_call(collect_body, f32(nfy, NB, LANES), [VM, ANY])(tiles, edge)
+    loads = lax.all_to_all(partial, "fy", 0, 0, tiled=True)
+
     span = f32(8 * NV + 8, LANES)
     top, bottom = kernel_call(pack_span_body, (span, span), [VM] * 4)(low, state, high, beyond)
     before = lax.ppermute(bottom, "fy", up_y)
     after = lax.ppermute(top, "fy", down_y)
 
     new_disp, new_vel, walls = kernel_call(
-        shell_body, (f32(NB, LANES), f32(NB, LANES), f32(nfx, 2, LANES)), [VM] * 6
-    )(
-        loads,
-        tiles,
-        shell_disp.reshape(NB, LANES),
-        shell_vel.reshape(NB, LANES),
-        connect[0],
-        stiffness[0],
-    )
+        shell_body, (f32(NB, LANES), f32(NB, LANES), f32(nfx, 2, LANES)), [VM] * 5 + [ANY]
+    )(loads, tiles, couple, shell_disp.reshape(NB, LANES), shell_vel.reshape(NB, LANES), top)
     walls = lax.all_to_all(walls, "fx", 0, 0, tiled=True)
 
-    fluid = kernel_call(
+    fluid, part = kernel_call(
         fluid_body,
-        f32(*state.shape),
+        (f32(*state.shape), f32(2, 8, LANES)),
         [SM] + [VM] * 9,
         scratch=[
             pltpu.VMEM((NV, 4, ROWS, LANES), jnp.float32),
@@ -421,7 +415,7 @@
             pltpu.VMEM((ROWS, LANES), jnp.float32),
         ],
     )(mixing, low, state, high, edge, beyond, top, bottom, before, after)
-    new_state = finish(walls, wall_weight, fluid)
+    new_state = finish(walls, wall_weight, part, fluid)
     return (new_state, new_disp.reshape(1, -1), new_vel.reshape(1, -1))
 
 

time: 84.9 us -> 69.2 us (0.82)
  the two profiles are of different devices: /device:TPU:57 before, /device:TPU:1 now
where the time goes in v2:
time: 69.2 us; the launch traced here: 68.6 us
  starting transfers between devices  39.6 us (57%)
  waiting for transfers between devices  20 us (29%)
  Pallas kernels  5.91 us (9%)
  local copies, waits for them, and re-layouts  2.27 us (3%)
  between operations  0.79 us (1%)
    all_to_all x1, starting transfers between devices, shards(): loads = lax.all_to_all(partial, 'fy', 0, 0, tiled=True)  13 us
    all_to_all x1, starting transfers between devices, shards(): tiles = lax.all_to_all(offered, ('fx', 'sec'), 0, 0, tiled=True)  10.3 us
    all_to_all x1, waiting for transfers between devices, shards(): tiles = lax.all_to_all(offered, ('fx', 'sec'), 0, 0, tiled=True)  8.83 us
    ppermute x1, waiting for transfers between devices, shards(): beyond = lax.ppermute(edge, 'sec', [(0, 1), (1, 0)])  5.3 us
    ppermute x1, starting transfers between devices, shards(): low = lax.ppermute(state, 'fx', up_x)  4.67 us
    all_to_all x1, starting transfers between devices, shards(): walls = lax.all_to_all(walls, 'fx', 0, 0, tiled=True)  3.48 us
    ppermute x1, waiting for transfers between devices, shards(): after = lax.ppermute(top, 'fy', down_y)  3.07 us
    all_to_all x1, waiting for transfers between devices, shards(): loads = lax.all_to_all(partial, 'fy', 0, 0, tiled=True)  2.79 us
  transfers between devices with their start and end apart: 8, of which 4 were waited for; matrix products, arithmetic and copies ran while one was open for 0% of the time, Pallas kernels for 5%

profile of v2, /device:TPU:1, one launch (start us, length us, event | category | flops | bytes accessed | tf_op | source)
XLA Modules:
  0.0 68.6 jit_solution(5776780229183408003)
XLA Ops:
  0.6 1.3 %collective-permute-start.1 = (f32[5,2,32,128]{3,2,1,0:T(8,128)}, f32[5,2,32,128]{3,2,1,0:T(8,128)S(1)}, u32[]{:S(2)}, u32[]{:S(2)}) collective-permute-start(f32[5,2,32,128]{3,2,1,0:T(8,128)} %state_ref.7), channel_id=1, source_target_pairs={{32,0},{64,32},{96,64},{128,96},{160,128},{192,160},{224,192},{256... | collective-permute-start | bytes 491528 | tf_op jit(solution)/shard_map/ppermute | solution.py:382
  1.9 4.7 %collective-permute-start = (f32[5,2,32,128]{3,2,1,0:T(8,128)}, f32[5,2,32,128]{3,2,1,0:T(8,128)S(1)}, u32[]{:S(2)}, u32[]{:S(2)}) collective-permute-start(f32[5,2,32,128]{3,2,1,0:T(8,128)} %state_ref.7), channel_id=1, source_target_pairs={{0,32},{32,64},{64,96},{96,128},{128,160},{160,192},{192,224},{224... | collective-permute-start | bytes 491528 | tf_op jit(solution)/shard_map/ppermute | solution.py:381
  6.6 0.0 copy-start.9
  6.6 0.0 copy-start.6
  6.6 0.0 copy-start.8
  6.6 0.6 copy-done.9
  7.3 0.0 copy-done.6
  7.3 0.0 copy-done.8
  7.3 0.0 copy-start
  7.3 0.9 %copy-done = f32[5,2,32,128]{3,2,1,0:T(8,128)S(1)} copy-done((f32[5,2,32,128]{3,2,1,0:T(8,128)S(1)}, f32[5,2,32,128]{3,2,1,0:T(8,128)}, u32[]{:S(2)}) %copy-start) | copy-done | bytes 163864
  8.2 0.0 copy-start.1
  8.2 1.2 %shard_map.112 = f32[32,4,128]{2,1,0:T(4,128)} custom-call(s32[2]{0:T(128)S(1)} %bitcast.14, s32[2]{0:T(128)S(1)} %bitcast.15, f32[2,1,128]{2,1,0:T(1,128)S(1)} %copy-done.6, f32[5,2,32,128]{3,2,1,0:T(8,128)S(1)} %copy-done), custom_call_target="tpu_custom_call" | custom-call | flops 4096 | bytes 65536 | tf_op jit(solution)/shard_map/pallas_call | solution.py:57
  9.4 10.3 %all-to-all-start = ((f32[32,4,128]{2,1,0:T(4,128)}), f32[32,4,128]{2,1,0:T(4,128)S(1)}, u32[]{:S(2)}, u32[]{:S(2)}) async-start(f32[32,4,128]{2,1,0:T(4,128)} %shard_map.112), calls=%async_computation | async-start | bytes 131072 | tf_op jit(solution)/shard_map/all_to_all | solution.py:387
  19.7 0.0 collective-permute-done.1.high_ref
  19.7 0.0 collective-permute-done.low_ref
  19.7 0.0 copy-done.1
  19.7 0.2 shard_map.113._.edge_ref
  19.9 8.8 %all-to-all-done.tiles_ref = f32[32,4,128]{2,1,0:T(4,128)S(1)} async-done(((f32[32,4,128]{2,1,0:T(4,128)}), f32[32,4,128]{2,1,0:T(4,128)S(1)}, u32[]{:S(2)}, u32[]{:S(2)}) %all-to-all-start) | async-done | bytes 65568 | tf_op jit(solution)/shard_map/all_to_all | solution.py:387
  28.7 0.8 %shard_map.114 = f32[16,32,128]{2,1,0:T(8,128)} custom-call(f32[32,4,128]{2,1,0:T(4,128)S(1)} %all-to-all-done.tiles_ref, f32[32,128]{1,0:T(8,128)S(1)} %shard_map.113._.edge_ref), custom_call_target="tpu_custom_call" | custom-call | flops 20000 | bytes 20000 | tf_op jit(solution)/shard_map/pallas_call | solution.py:395
  29.6 0.0 copy-start.2
  29.6 13.0 %all-to-all-start.1 = ((f32[16,32,128]{2,1,0:T(8,128)}), f32[16,32,128]{2,1,0:T(8,128)S(1)}, u32[]{:S(2)}, u32[]{:S(2)}) async-start(f32[16,32,128]{2,1,0:T(8,128)} %shard_map.114), calls=%async_computation.1 | async-start | bytes 524288 | tf_op jit(solution)/shard_map/all_to_all | solution.py:396
  42.6 2.5 %collective-permute-start.2 = (f32[32,128]{1,0:T(8,128)S(1)}, f32[32,128]{1,0:T(8,128)S(1)}, u32[]{:S(2)}, u32[]{:S(2)}) collective-permute-start(f32[32,128]{1,0:T(8,128)S(1)} %shard_map.113._.edge_ref), channel_id=1, source_target_pairs={{0,1},{1,0},{2,3},{3,2},{4,5},{5,4},{6,7},{7,6},{8,9},{9,8},{10,11... | collective-permute-start | bytes 49160 | tf_op jit(solution)/shard_map/ppermute | solution.py:390
  45.2 0.0 copy-start.7
  45.2 0.0 copy-done.2
  45.2 0.7 copy-done.7
  45.8 0.3 shard_map.115.couple_ref
  46.2 5.3 %collective-permute-done.2.beyond_ref = f32[32,128]{1,0:T(8,128)S(1)} collective-permute-done((f32[32,128]{1,0:T(8,128)S(1)}, f32[32,128]{1,0:T(8,128)S(1)}, u32[]{:S(2)}, u32[]{:S(2)}) %collective-permute-start.2) | collective-permute-done | bytes 16416 | tf_op jit(solution)/shard_map/ppermute | solution.py:390
  51.5 0.0 copy-start.3
  51.5 0.0 copy-start.4
  51.5 2.8 %all-to-all-done.1.loads_ref = f32[16,32,128]{2,1,0:T(8,128)S(1)} async-done(((f32[16,32,128]{2,1,0:T(8,128)}), f32[16,32,128]{2,1,0:T(8,128)S(1)}, u32[]{:S(2)}, u32[]{:S(2)}) %all-to-all-start.1) | async-done | bytes 262176 | tf_op jit(solution)/shard_map/all_to_all | solution.py:396
  54.3 0.0 copy-done.3
  54.3 0.0 copy-done.4
  54.3 0.0 copy-start.5
  54.3 0.9 %shard_map.117 = (f32[32,128]{1,0:T(8,128)}, f32[32,128]{1,0:T(8,128)}, f32[16,2,128]{2,1,0:T(2,128)}) custom-call(f32[16,32,128]{2,1,0:T(8,128)S(1)} %all-to-all-done.1.loads_ref, f32[32,4,128]{2,1,0:T(4,128)S(1)} %all-to-all-done.tiles_ref, f32[32,32,128]{2,1,0:T(8,128)S(1)} %shard_map.115.couple_ref, f32[32,128]{1,0:T(8,128)S(1)} %bitcast.11, ...), custom_call_target="tpu_custom_call" | custom-call | flops 20000 | bytes 20000 | tf_op jit(solution)/shard_map/pallas_call | solution.py:403
  55.2 3.5 %all-to-all-start.2 = ((f32[16,2,128]{2,1,0:T(2,128)}), f32[16,2,128]{2,1,0:T(2,128)S(1)}, u32[]{:S(2)}, u32[]{:S(2)}) async-start(f32[16,2,128]{2,1,0:T(2,128)} %get-tuple-element.11), calls=%async_computation.2 | async-start | bytes 32768 | tf_op jit(solution)/shard_map/all_to_all | solution.py:406
  58.7 2.3 %collective-permute-start.3 = (f32[48,128]{1,0:T(8,128)S(1)}, f32[48,128]{1,0:T(8,128)S(1)}, u32[]{:S(2)}, u32[]{:S(2)}) collective-permute-start(f32[48,128]{1,0:T(8,128)S(1)} %get-tuple-element.12.bottom_ref), channel_id=1, source_target_pairs={{0,2},{2,4},{4,6},{6,8},{8,10},{10,12},{12,14},{14,16},{16,18},{18... | collective-permute-start | bytes 73736 | tf_op jit(solution)/shard_map/ppermute | solution.py:400
  61.0 2.1 %collective-permute-start.4 = (f32[48,128]{1,0:T(8,128)S(1)}, f32[48,128]{1,0:T(8,128)S(1)}, u32[]{:S(2)}, u32[]{:S(2)}) collective-permute-start(f32[48,128]{1,0:T(8,128)S(1)} %get-tuple-element.10._.top_ref), channel_id=1, source_target_pairs={{2,0},{4,2},{6,4},{8,6},{10,8},{12,10},{14,12},{16,14},{18,16},{20... | collective-permute-start | bytes 73736 | tf_op jit(solution)/shard_map/ppermute | solution.py:401
  63.0 0.0 collective-permute-done.3.before_ref
  63.0 3.1 %collective-permute-done.4.after_ref = f32[48,128]{1,0:T(8,128)S(1)} collective-permute-done((f32[48,128]{1,0:T(8,128)S(1)}, f32[48,128]{1,0:T(8,128)S(1)}, u32[]{:S(2)}, u32[]{:S(2)}) %collective-permute-start.4) | collective-permute-done | bytes 24608 | tf_op jit(solution)/shard_map/ppermute | solution.py:401
  66.1 0.0 copy-done.5
  66.1 1.8 %shard_map.118 = (f32[5,2,32,128]{3,2,1,0:T(8,128)}, f32[2,8,128]{2,1,0:T(8,128)S(1)}) custom-call(f32[5,5]{1,0:T(8,128)S(1)} %copy-done.5, f32[5,2,32,128]{3,2,1,0:T(8,128)S(1)} %collective-permute-done.low_ref, f32[5,2,32,128]{3,2,1,0:T(8,128)S(1)} %copy-done.1, f32[5,2,32,128]{3,2,1,0:T(8,128)S(1)} %collective-permute-done.1.high_ref, ...), custom_call_target="tpu_custom_call" | custom-call | flops 20000 | bytes 20000 | tf_op jit(solution)/shard_map/pallas_call | solution.py:408
  68.0 0.0 all-to-all-done.2.walls_ref
  68.0 0.6 shard_map.119
  (1 shorter events, 0.0 us)
Async XLA Ops:
  0.6 19.1 %collective-permute-start.1 = (f32[5,2,32,128]{3,2,1,0:T(8,128)}, f32[5,2,32,128]{3,2,1,0:T(8,128)S(1)}, u32[]{:S(2)}, u32[]{:S(2)}) collective-permute-start(f32[5,2,32,128]{3,2,1,0:T(8,128)} %state_ref.7), channel_id=1, source_target_pairs={{32,0},{64,32},{96,64},{128,96},{160,128},{192,160},{224,192},{256... | collective-permute-start | bytes 491528 | tf_op jit(solution)/shard_map/ppermute | solution.py:382
  1.9 17.8 %collective-permute-start = (f32[5,2,32,128]{3,2,1,0:T(8,128)}, f32[5,2,32,128]{3,2,1,0:T(8,128)S(1)}, u32[]{:S(2)}, u32[]{:S(2)}) collective-permute-start(f32[5,2,32,128]{3,2,1,0:T(8,128)} %state_ref.7), channel_id=1, source_target_pairs={{0,32},{32,64},{64,96},{96,128},{128,160},{160,192},{192,224},{224... | collective-permute-start | bytes 491528 | tf_op jit(solution)/shard_map/ppermute | solution.py:381
  6.6 0.7 copy-start.9
  6.6 0.7 copy-start.6
  6.6 0.7 copy-start.8
  7.3 0.9 %copy-start = (f32[5,2,32,128]{3,2,1,0:T(8,128)S(1)}, f32[5,2,32,128]{3,2,1,0:T(8,128)}, u32[]{:S(2)}) copy-start(f32[5,2,32,128]{3,2,1,0:T(8,128)} %state_ref.7) | copy-start | bytes 491524
  8.2 11.5 %copy-start.1 = (f32[5,2,32,128]{3,2,1,0:T(8,128)S(1)}, f32[5,2,32,128]{3,2,1,0:T(8,128)}, u32[]{:S(2)}) copy-start(f32[5,2,32,128]{3,2,1,0:T(8,128)} %state_ref.7) | copy-start | bytes 491524
  9.4 19.3 %all-to-all-start = ((f32[32,4,128]{2,1,0:T(4,128)}), f32[32,4,128]{2,1,0:T(4,128)S(1)}, u32[]{:S(2)}, u32[]{:S(2)}) async-start(f32[32,4,128]{2,1,0:T(4,128)} %shard_map.112), calls=%async_computation | async-start | bytes 131072 | tf_op jit(solution)/shard_map/all_to_all | solution.py:387
  29.6 15.6 %copy-start.2 = (f32[1,64,128]{2,1,0:T(8,128)S(1)}, f32[1,64,128]{2,1,0:T(8,128)}, u32[]{:S(2)}) copy-start(f32[1,64,128]{2,1,0:T(8,128)} %param.17) | copy-start | bytes 98308
  29.6 24.7 %all-to-all-start.1 = ((f32[16,32,128]{2,1,0:T(8,128)}), f32[16,32,128]{2,1,0:T(8,128)S(1)}, u32[]{:S(2)}, u32[]{:S(2)}) async-start(f32[16,32,128]{2,1,0:T(8,128)} %shard_map.114), calls=%async_computation.1 | async-start | bytes 524288 | tf_op jit(solution)/shard_map/all_to_all | solution.py:396
  42.6 8.9 %collective-permute-start.2 = (f32[32,128]{1,0:T(8,128)S(1)}, f32[32,128]{1,0:T(8,128)S(1)}, u32[]{:S(2)}, u32[]{:S(2)}) collective-permute-start(f32[32,128]{1,0:T(8,128)S(1)} %shard_map.113._.edge_ref), channel_id=1, source_target_pairs={{0,1},{1,0},{2,3},{3,2},{4,5},{5,4},{6,7},{7,6},{8,9},{9,8},{10,11... | collective-permute-start | bytes 49160 | tf_op jit(solution)/shard_map/ppermute | solution.py:390
  45.2 0.7 copy-start.7
  51.5 2.8 %copy-start.3 = (f32[1,4096]{1,0:T(1,128)S(1)}, f32[1,4096]{1,0:T(1,128)}, u32[]{:S(2)}) copy-start(f32[1,4096]{1,0:T(1,128)} %param.14) | copy-start | bytes 49156
  51.5 2.8 %copy-start.4 = (f32[1,4096]{1,0:T(1,128)S(1)}, f32[1,4096]{1,0:T(1,128)}, u32[]{:S(2)}) copy-start(f32[1,4096]{1,0:T(1,128)} %param.15) | copy-start | bytes 49156
  54.3 11.8 %copy-start.5 = (f32[5,5]{1,0:T(8,128)S(1)}, f32[5,5]{1,0:T(8,128)}, u32[]{:S(2)}) copy-start(f32[5,5]{1,0:T(8,128)} %mixing_ref.1) | copy-start | bytes 304
  55.2 12.8 %all-to-all-start.2 = ((f32[16,2,128]{2,1,0:T(2,128)}), f32[16,2,128]{2,1,0:T(2,128)S(1)}, u32[]{:S(2)}, u32[]{:S(2)}) async-start(f32[16,2,128]{2,1,0:T(2,128)} %get-tuple-element.11), calls=%async_computation.2 | async-start | bytes 32768 | tf_op jit(solution)/shard_map/all_to_all | solution.py:406
  58.7 4.3 %collective-permute-start.3 = (f32[48,128]{1,0:T(8,128)S(1)}, f32[48,128]{1,0:T(8,128)S(1)}, u32[]{:S(2)}, u32[]{:S(2)}) collective-permute-start(f32[48,128]{1,0:T(8,128)S(1)} %get-tuple-element.12.bottom_ref), channel_id=1, source_target_pairs={{0,2},{2,4},{4,6},{6,8},{8,10},{10,12},{12,14},{14,16},{16,18},{18... | collective-permute-start | bytes 73736 | tf_op jit(solution)/shard_map/ppermute | solution.py:400
  61.0 5.1 %collective-permute-start.4 = (f32[48,128]{1,0:T(8,128)S(1)}, f32[48,128]{1,0:T(8,128)S(1)}, u32[]{:S(2)}, u32[]{:S(2)}) collective-permute-start(f32[48,128]{1,0:T(8,128)S(1)} %get-tuple-element.10._.top_ref), channel_id=1, source_target_pairs={{2,0},{4,2},{6,4},{8,6},{10,8},{12,10},{14,12},{16,14},{18,16},{20... | collective-permute-start | bytes 73736 | tf_op jit(solution)/shard_map/ppermute | solution.py:401

commit v3 on v2

--- a/solution.py
+++ b/solution.py
@@ -19,20 +19,24 @@
 TOP = 8
 ROWS = 48
 
+LONG = 3_800_000_000
+LONG_SEC = 1_300_000_000
+
 VM = pl.BlockSpec(memory_space=pltpu.VMEM)
 SM = pl.BlockSpec(memory_space=pltpu.SMEM)
 ANY = pl.BlockSpec(memory_space=pl.ANY)
+HBM = pl.BlockSpec(memory_space=pltpu.HBM)
 SMALL = pltpu.CompilerParams(vmem_limit_bytes=8 * 1024 * 1024)
 
 
-def kernel_call(body, outs, ins, scratch=(), cost=20000):
+def kernel_call(body, outs, ins, scratch=(), cost=20000, params=SMALL):
     return pl.pallas_call(
         body,
         out_shape=outs,
         in_specs=ins,
         out_specs=jax.tree.map(lambda _: VM, outs),
         scratch_shapes=scratch,
-        compiler_params=SMALL,
+        compiler_params=params,
         cost_estimate=pl.CostEstimate(flops=cost, bytes_accessed=cost, transcendentals=0),
     )
 
@@ -41,10 +45,27 @@
     return jax.ShapeDtypeStruct(shape, jnp.float32)
 
 
-def offer_body(patch_ref, block_ref, weight_ref, state_ref, out_ref):
+def offer_body(
+    patch_hbm, block_hbm, weight_hbm, state_hbm, out_ref, patch_ref, block_ref, weight_ref, wall_ref, arrived
+):
+    copies = [
+        pltpu.make_async_copy(source, target, arrived.at[place])
+        for place, (source, target) in enumerate(
+            (
+                (patch_hbm, patch_ref),
+                (block_hbm, block_ref),
+                (weight_hbm, weight_ref),
+                (state_hbm.at[NV - 1, :, 0:8, :], wall_ref),
+            )
+        )
+    ]
+    for copy in copies:
+        copy.start()
+    for copy in copies:
+        copy.wait()
     rows = []
     for tile in range(2):
-        rows.append(weight_ref[tile] * state_ref[0, tile, 0:1, :])
+        rows.append(weight_ref[tile] * wall_ref[tile, 0:1, :])
     for tile in range(2):
         target = patch_ref[tile] * NB + block_ref[tile]
         rows.append(jnp.full((1, LANES), target.astype(jnp.float32)))
@@ -54,23 +75,22 @@
 
 
 def offer(patch_map, block_map, weight, state, receivers):
-    return pl.pallas_call(
+    return kernel_call(
         offer_body,
-        grid=(1,),
-        out_shape=f32(receivers, 4, LANES),
-        in_specs=[
-            SM,
-            SM,
-            VM,
-            pl.BlockSpec((1, 2, 8, LANES), lambda i: (4, 0, 0, 0)),
+        f32(receivers, 4, LANES),
+        [HBM] * 4,
+        scratch=[
+            pltpu.SMEM((2,), jnp.int32),
+            pltpu.SMEM((2,), jnp.int32),
+            pltpu.VMEM((2, 1, LANES), jnp.float32),
+            pltpu.VMEM((2, 8, LANES), jnp.float32),
+            pltpu.SemaphoreType.DMA((4,)),
         ],
-        out_specs=VM,
-        compiler_params=SMALL,
-        cost_estimate=pl.CostEstimate(flops=4096, bytes_accessed=65536, transcendentals=0),
+        params=None,
     )(patch_map, block_map, weight, state)
 
 
-def collect_body(tiles_ref, _, out_ref):
+def collect_body(tiles_ref, out_ref):
     base = (lax.axis_index("fx") * NB).astype(jnp.float32)
     block = lax.broadcasted_iota(jnp.int32, (NB, LANES), 0).astype(jnp.float32) + base
     sums = [jnp.zeros((NB, LANES), jnp.float32) for _ in range(4)]
@@ -164,27 +184,40 @@
     return state_ref.at[v, xi - 1]
 
 
-def pack_sec_body(low_ref, state_ref, high_ref, out_ref):
-    sec = lax.axis_index("sec")
+def pack_columns(slabs, out_ref):
     lane = lax.broadcasted_iota(jnp.int32, (32, LANES), 1)
 
     def pack(shift):
         packed = jnp.zeros((32, LANES), jnp.float32)
-        for v in range(NV):
-            for xi in range(4):
-                first = 8 * v + 2 * xi
-                cells = slab(low_ref, state_ref, high_ref, v, xi)[...]
-                moved = pltpu.roll(cells, first + shift, axis=1) if first + shift else cells
-                packed = jnp.where((lane == first) | (lane == first + 1), moved, packed)
+        for (v, xi), cells_ref in slabs.items():
+            first = 8 * v + 2 * xi
+            cells = cells_ref[...]
+            moved = pltpu.roll(cells, first + shift, axis=1) if first + shift else cells
+            packed = jnp.where((lane == first) | (lane == first + 1), moved, packed)
         out_ref[...] = packed
 
+    sec = lax.axis_index("sec")
     pl.when(sec == 0)(lambda: pack(2))
     pl.when(sec == 1)(lambda: pack(0))
 
 
-def pack_span_body(low_ref, state_ref, high_ref, beyond_ref, top_ref, bottom_ref):
+def first_round_body(state_ref, _, copy_ref, edge_ref):
+    copy_ref[...] = state_ref[...]
+    pack_columns({(v, xi): state_ref.at[v, xi - 1] for v in range(NV) for xi in (1, 2)}, edge_ref)
+
+
+def corner_body(beyond_ref, out_ref):
+    last = beyond_ref.shape[0] - 1
+    for place, y in enumerate((0, 1, last, last - 1)):
+        out_ref[place : place + 1, :] = beyond_ref[y : y + 1, :]
+    out_ref[4:8, :] = jnp.zeros((4, LANES), jnp.float32)
+
+
+def second_round_body(
+    low_ref, state_ref, high_ref, corner_ref, top_ref, bottom_ref, edge_ref
+):
     last = state_ref.shape[2] - 1
-    for out, rows in ((top_ref, (0, 1)), (bottom_ref, (last, last - 1))):
+    for end, (out, rows) in enumerate(((top_ref, (0, 1)), (bottom_ref, (last, last - 1)))):
         for place, y in enumerate(rows):
             for v in range(NV):
                 for xi in range(4):
@@ -192,8 +225,11 @@
                     out[spot : spot + 1, :] = slab(low_ref, state_ref, high_ref, v, xi)[
                         y : y + 1, :
                     ]
-            out[8 * NV + place : 8 * NV + place + 1, :] = beyond_ref[y : y + 1, :]
+        out[8 * NV : 8 * NV + 2, :] = corner_ref[2 * end : 2 * end + 2, :]
         out[8 * NV + 2 :, :] = jnp.zeros((6, LANES), jnp.float32)
+    outer = {(v, 0): low_ref.at[v, 1] for v in range(NV)}
+    outer |= {(v, 3): high_ref.at[v, 0] for v in range(NV)}
+    pack_columns(outer, edge_ref)
 
 
 def stencil(center, ahead, behind, others, mixed):
@@ -207,7 +243,8 @@
     state_ref,
     high_ref,
     edge_ref,
-    beyond_ref,
+    own_beyond_ref,
+    outer_beyond_ref,
     top_ref,
     bottom_ref,
     before_ref,
@@ -218,6 +255,7 @@
     section,
     packed,
 ):
+    beyond = own_beyond_ref[...] + outer_beyond_ref[...]
     size = state_ref.shape[2]
     end = TOP + size
     sec = lax.axis_index("sec")
@@ -249,10 +287,9 @@
             total = total + mix[v][w] * cells[w]
         return total
 
-    packed[TOP:end, :] = beyond_ref[...]
+    packed[TOP:end, :] = beyond
     packed[TOP - 1 : TOP, :] = before_ref[8 * NV : 8 * NV + 1, :]
     packed[end : end + 1, :] = after_ref[8 * NV : 8 * NV + 1, :]
-    beyond = beyond_ref[...]
     group = lane // 8
     mixed_columns = jnp.zeros((size, LANES), jnp.float32)
     for shift in range(1 - NV, NV):
@@ -378,27 +415,33 @@
     up_y = [(i, i + 1) for i in range(nfy - 1)]
     down_y = [(i + 1, i) for i in range(nfy - 1)]
 
-    low = lax.ppermute(state, "fx", up_x)
-    high = lax.ppermute(state, "fx", down_x)
-
     offered = offer(
         patch_map.reshape(2), block_map.reshape(2), wall_weight, state, nfx * nsec
     )
     tiles = lax.all_to_all(offered, ("fx", "sec"), 0, 0, tiled=True)
 
-    edge = kernel_call(pack_sec_body, f32(32, LANES), [VM] * 3)(low, state, high)
+    columns = f32(32, LANES)
+    sent, edge = kernel_call(first_round_body, (f32(*state.shape), columns), [VM, ANY])(
+        state, offered
+    )
+    low = lax.ppermute(sent, "fx", up_x)
+    high = lax.ppermute(sent, "fx", down_x)
     beyond = lax.ppermute(edge, "sec", [(0, 1), (1, 0)])
+
+    partial = kernel_call(collect_body, f32(nfy, NB, LANES), [VM])(tiles)
+    loads = lax.all_to_all(partial, "fy", 0, 0, tiled=True)
+
     couple = kernel_call(couple_body, f32(NB, NB, LANES), [VM] * 2)(
         connect[0].T, stiffness[0]
     )
-
-    partial = kernel_call(collect_body, f32(nfy, NB, LANES), [VM, ANY])(tiles, edge)
-    loads = lax.all_to_all(partial, "fy", 0, 0, tiled=True)
-
+    corner = kernel_call(corner_body, f32(8, LANES), [VM], cost=LONG_SEC)(beyond)
     span = f32(8 * NV + 8, LANES)
-    top, bottom = kernel_call(pack_span_body, (span, span), [VM] * 4)(low, state, high, beyond)
+    top, bottom, outer_edge = kernel_call(
+        second_round_body, (span, span, columns), [VM] * 4, cost=LONG
+    )(low, sent, high, corner)
     before = lax.ppermute(bottom, "fy", up_y)
     after = lax.ppermute(top, "fy", down_y)
+    outer_beyond = lax.ppermute(outer_edge, "sec", [(0, 1), (1, 0)])
 
     new_disp, new_vel, walls = kernel_call(
         shell_body, (f32(NB, LANES), f32(NB, LANES), f32(nfx, 2, LANES)), [VM] * 5 + [ANY]
@@ -408,13 +451,14 @@
     fluid, part = kernel_call(
         fluid_body,
         (f32(*state.shape), f32(2, 8, LANES)),
-        [SM] + [VM] * 9,
+        [SM] + [VM] * 10,
         scratch=[
             pltpu.VMEM((NV, 4, ROWS, LANES), jnp.float32),
             pltpu.VMEM((NV, 4, ROWS, LANES), jnp.float32),
             pltpu.VMEM((ROWS, LANES), jnp.float32),
         ],
-    )(mixing, low, state, high, edge, beyond, top, bottom, before, after)
+        cost=LONG,
+    )(mixing, low, sent, high, edge, beyond, outer_beyond, top, bottom, before, after)
     new_state = finish(walls, wall_weight, part, fluid)
     return (new_state, new_disp.reshape(1, -1), new_vel.reshape(1, -1))
 

time: 69.2 us -> 67.1 us (0.970)
  waiting for transfers between devices: 20 us -> 8.21 us
  starting transfers between devices: 39.6 us -> 49.7 us
  local copies, waits for them, and re-layouts: 2.27 us -> 1.37 us
    all_to_all x1, waiting for transfers between devices: 8.83 us -> 0.01 us  [shards(): tiles = lax.all_to_all(offered, ('fx', 'sec'), 0, 0, tiled=True)]
    ppermute x1, waiting for transfers between devices: 5.3 us -> 0.01 us  [shards(): beyond = lax.ppermute(edge, 'sec', [(0, 1), (1, 0)])]
    all_to_all x1, waiting for transfers between devices: 0.01 us -> 4.88 us  [shards(): walls = lax.all_to_all(walls, 'fx', 0, 0, tiled=True)]
    ppermute x1, starting transfers between devices: 2.54 us -> 7.04 us  [shards(): beyond = lax.ppermute(edge, 'sec', [(0, 1), (1, 0)])]
    all_to_all x1, starting transfers between devices: 3.48 us -> 6.96 us  [shards(): walls = lax.all_to_all(walls, 'fx', 0, 0, tiled=True)]
    ppermute x1, waiting for transfers between devices: 3.07 us -> 0.01 us  [shards(): after = lax.ppermute(top, 'fy', down_y)]
    ppermute x1, starting transfers between devices: 2.26 us -> 3.54 us  [shards(): before = lax.ppermute(bottom, 'fy', up_y)]
    ppermute x2 -> x3, starting transfers between devices: 5.96 us -> 7.21 us  [the longest x1 4 us: shards(): low = lax.ppermute(sent, 'fx', up_x)]
  transfers between devices with their start and end apart: 8 -> 9, of which waited for: 4 -> 2; matrix products, arithmetic and copies ran while one was open for 0% -> 0% of each run, Pallas kernels for 5% -> 6%
where the time goes in v3:
time: 67.1 us; the launch traced here: 66.5 us
  starting transfers between devices  49.7 us (74%)
  waiting for transfers between devices  8.21 us (12%)
  Pallas kernels  6.32 us (9%)
  local copies, waits for them, and re-layouts  1.37 us (2%)
  between operations  0.85 us (1%)
    all_to_all x1, starting transfers between devices, shards(): loads = lax.all_to_all(partial, 'fy', 0, 0, tiled=True)  12.4 us
    all_to_all x1, starting transfers between devices, shards(): tiles = lax.all_to_all(offered, ('fx', 'sec'), 0, 0, tiled=True)  10.6 us
    ppermute x1, starting transfers between devices, shards(): beyond = lax.ppermute(edge, 'sec', [(0, 1), (1, 0)])  7.04 us
    all_to_all x1, starting transfers between devices, shards(): walls = lax.all_to_all(walls, 'fx', 0, 0, tiled=True)  6.96 us
    all_to_all x1, waiting for transfers between devices, shards(): walls = lax.all_to_all(walls, 'fx', 0, 0, tiled=True)  4.88 us
    ppermute x1, starting transfers between devices, shards(): low = lax.ppermute(sent, 'fx', up_x)  4 us
    ppermute x1, starting transfers between devices, shards(): before = lax.ppermute(bottom, 'fy', up_y)  3.54 us
    all_to_all x1, waiting for transfers between devices, shards(): loads = lax.all_to_all(partial, 'fy', 0, 0, tiled=True)  3.31 us
  transfers between devices with their start and end apart: 9, of which 2 were waited for; matrix products, arithmetic and copies ran while one was open for 0% of the time, Pallas kernels for 6%

profile of v3, /device:TPU:1, one launch (start us, length us, event | category | flops | bytes accessed | tf_op | source)
XLA Modules:
  0.0 66.5 jit_solution(9085689030951740200)
XLA Ops:
  0.6 0.0 copy-start
  0.6 1.5 %shard_map.112._ = f32[32,4,128]{2,1,0:T(4,128)} custom-call(s32[2]{0:T(128)} %bitcast.14, s32[2]{0:T(128)} %bitcast.15, f32[2,1,128]{2,1,0:T(1,128)} %weight_ref.1, f32[5,2,32,128]{3,2,1,0:T(8,128)} %state_ref.1), custom_call_target="tpu_custom_call" | custom-call | flops 20000 | bytes 20000 | tf_op jit(solution)/shard_map/pallas_call | solution.py:78
  2.1 0.0 copy-start.1
  2.1 10.6 %all-to-all-start = ((f32[32,4,128]{2,1,0:T(4,128)}), f32[32,4,128]{2,1,0:T(4,128)S(1)}, u32[]{:S(2)}, u32[]{:S(2)}) async-start(f32[32,4,128]{2,1,0:T(4,128)} %shard_map.112._), calls=%async_computation | async-start | bytes 131072 | tf_op jit(solution)/shard_map/all_to_all | solution.py:421
  12.8 0.0 copy-done
  12.8 0.0 copy-done.1
  12.8 0.1 shard_map.115
  12.9 1.3 %collective-permute-start.1 = (f32[5,2,32,128]{3,2,1,0:T(8,128)S(1)}, f32[5,2,32,128]{3,2,1,0:T(8,128)S(1)}, u32[]{:S(2)}, u32[]{:S(2)}) collective-permute-start(f32[5,2,32,128]{3,2,1,0:T(8,128)S(1)} %get-tuple-element.13.state_ref), channel_id=1, source_target_pairs={{32,0},{64,32},{96,64},{128,96},{160,128},{192,160},{224,192},{256... | collective-permute-start | bytes 491528 | tf_op jit(solution)/shard_map/ppermute | solution.py:428
  14.2 4.0 %collective-permute-start = (f32[5,2,32,128]{3,2,1,0:T(8,128)S(1)}, f32[5,2,32,128]{3,2,1,0:T(8,128)S(1)}, u32[]{:S(2)}, u32[]{:S(2)}) collective-permute-start(f32[5,2,32,128]{3,2,1,0:T(8,128)S(1)} %get-tuple-element.13.state_ref), channel_id=1, source_target_pairs={{0,32},{32,64},{64,96},{96,128},{128,160},{160,192},{192,224},{224... | collective-permute-start | bytes 491528 | tf_op jit(solution)/shard_map/ppermute | solution.py:427
  18.3 7.0 %collective-permute-start.2 = (f32[32,128]{1,0:T(8,128)S(1)}, f32[32,128]{1,0:T(8,128)S(1)}, u32[]{:S(2)}, u32[]{:S(2)}) collective-permute-start(f32[32,128]{1,0:T(8,128)S(1)} %get-tuple-element.14.edge_ref), channel_id=1, source_target_pairs={{0,1},{1,0},{2,3},{3,2},{4,5},{5,4},{6,7},{7,6},{8,9},{9,8},{10,11... | collective-permute-start | bytes 49160 | tf_op jit(solution)/shard_map/ppermute | solution.py:429
  25.3 0.0 all-to-all-done.tiles_ref
  25.3 0.8 %shard_map.113 = f32[16,32,128]{2,1,0:T(8,128)} custom-call(f32[32,4,128]{2,1,0:T(4,128)S(1)} %all-to-all-done.tiles_ref), custom_call_target="tpu_custom_call" | custom-call | flops 20000 | bytes 20000 | tf_op jit(solution)/shard_map/pallas_call | solution.py:431
  26.1 12.4 %all-to-all-start.1 = ((f32[16,32,128]{2,1,0:T(8,128)}), f32[16,32,128]{2,1,0:T(8,128)S(1)}, u32[]{:S(2)}, u32[]{:S(2)}) async-start(f32[16,32,128]{2,1,0:T(8,128)} %shard_map.113), calls=%async_computation.1 | async-start | bytes 524288 | tf_op jit(solution)/shard_map/all_to_all | solution.py:432
  38.5 0.0 collective-permute-done.2.beyond_ref.own_beyond_ref
  38.6 0.0 copy-start.2
  38.6 0.0 collective-permute-done.1.high_ref
  38.6 0.0 collective-permute-done.low_ref
  38.6 0.1 shard_map.117
  38.7 3.5 %collective-permute-start.4 = (f32[48,128]{1,0:T(8,128)S(1)}, f32[48,128]{1,0:T(8,128)S(1)}, u32[]{:S(2)}, u32[]{:S(2)}) collective-permute-start(f32[48,128]{1,0:T(8,128)S(1)} %get-tuple-element.18.bottom_ref), channel_id=1, source_target_pairs={{0,2},{2,4},{4,6},{6,8},{8,10},{10,12},{12,14},{14,16},{16,18},{18... | collective-permute-start | bytes 73736 | tf_op jit(solution)/shard_map/ppermute | solution.py:442
  42.3 1.9 %collective-permute-start.5 = (f32[48,128]{1,0:T(8,128)S(1)}, f32[48,128]{1,0:T(8,128)S(1)}, u32[]{:S(2)}, u32[]{:S(2)}) collective-permute-start(f32[48,128]{1,0:T(8,128)S(1)} %get-tuple-element.15._.top_ref), channel_id=1, source_target_pairs={{2,0},{4,2},{6,4},{8,6},{10,8},{12,10},{14,12},{16,14},{18,16},{20... | collective-permute-start | bytes 73736 | tf_op jit(solution)/shard_map/ppermute | solution.py:443
  44.2 1.9 %collective-permute-start.3 = (f32[32,128]{1,0:T(8,128)S(1)}, f32[32,128]{1,0:T(8,128)S(1)}, u32[]{:S(2)}, u32[]{:S(2)}) collective-permute-start(f32[32,128]{1,0:T(8,128)S(1)} %get-tuple-element.17), channel_id=1, source_target_pairs={{0,1},{1,0},{2,3},{3,2},{4,5},{5,4},{6,7},{7,6},{8,9},{9,8},{10,11... | collective-permute-start | bytes 49160 | tf_op jit(solution)/shard_map/ppermute | solution.py:444
  46.2 0.0 copy-start.6
  46.2 0.0 copy-done.2
  46.2 0.7 copy-done.6
  46.8 0.0 copy-start.3
  46.8 0.0 copy-start.4
  46.8 0.3 shard_map.114.couple_ref
  47.2 3.3 %all-to-all-done.1.loads_ref = f32[16,32,128]{2,1,0:T(8,128)S(1)} async-done(((f32[16,32,128]{2,1,0:T(8,128)}), f32[16,32,128]{2,1,0:T(8,128)S(1)}, u32[]{:S(2)}, u32[]{:S(2)}) %all-to-all-start.1) | async-done | bytes 262176 | tf_op jit(solution)/shard_map/all_to_all | solution.py:432
  50.5 0.0 copy-done.3
  50.5 0.0 copy-done.4
  50.5 0.9 %shard_map.118 = (f32[32,128]{1,0:T(8,128)}, f32[32,128]{1,0:T(8,128)}, f32[16,2,128]{2,1,0:T(2,128)}) custom-call(f32[16,32,128]{2,1,0:T(8,128)S(1)} %all-to-all-done.1.loads_ref, f32[32,4,128]{2,1,0:T(4,128)S(1)} %all-to-all-done.tiles_ref, f32[32,32,128]{2,1,0:T(8,128)S(1)} %shard_map.114.couple_ref, f32[32,128]{1,0:T(8,128)S(1)} %bitcast.11, ...), custom_call_target="tpu_custom_call" | custom-call | flops 20000 | bytes 20000 | tf_op jit(solution)/shard_map/pallas_call | solution.py:446
  51.4 0.0 copy-start.7
  51.4 7.0 %all-to-all-start.2 = ((f32[16,2,128]{2,1,0:T(2,128)}), f32[16,2,128]{2,1,0:T(2,128)S(1)}, u32[]{:S(2)}, u32[]{:S(2)}) async-start(f32[16,2,128]{2,1,0:T(2,128)} %get-tuple-element.16), calls=%async_computation.2 | async-start | bytes 32768 | tf_op jit(solution)/shard_map/all_to_all | solution.py:449
  58.4 0.0 collective-permute-done.3.outer_beyond_ref
  58.4 0.0 collective-permute-done.4.before_ref
  58.4 0.0 collective-permute-done.5.after_ref
  58.4 0.0 copy-done.7
  58.4 1.9 %shard_map.119 = (f32[5,2,32,128]{3,2,1,0:T(8,128)}, f32[2,8,128]{2,1,0:T(8,128)S(1)}) custom-call(f32[5,5]{1,0:T(8,128)S(1)} %copy-done.7, f32[5,2,32,128]{3,2,1,0:T(8,128)S(1)} %collective-permute-done.low_ref, f32[5,2,32,128]{3,2,1,0:T(8,128)S(1)} %get-tuple-element.13.state_ref, f32[5,2,32,128]{3,2,1,0:T(8,128)S(1)} %collective-permute-done.1.high_ref, ...), custom_call_target="tpu_custom_call" | custom-call | flops 3800000000 | bytes 3800000000 | tf_op jit(solution)/shard_map/pallas_call | solution.py:451
  60.3 4.9 %all-to-all-done.2.walls_ref = f32[16,2,128]{2,1,0:T(2,128)S(1)} async-done(((f32[16,2,128]{2,1,0:T(2,128)}), f32[16,2,128]{2,1,0:T(2,128)S(1)}, u32[]{:S(2)}, u32[]{:S(2)}) %all-to-all-start.2) | async-done | bytes 16416 | tf_op jit(solution)/shard_map/all_to_all | solution.py:449
  65.2 0.0 copy-start.5
  65.2 0.7 %copy-done.5 = f32[2,1,128]{2,1,0:T(1,128)S(1)} copy-done((f32[2,1,128]{2,1,0:T(1,128)S(1)}, f32[2,1,128]{2,1,0:T(1,128)}, u32[]{:S(2)}) %copy-start.5) | copy-done | bytes 1048
  65.8 0.6 shard_map.120
  (1 shorter events, 0.0 us)
Async XLA Ops:
  0.6 12.2 %copy-start = (f32[5,2,32,128]{3,2,1,0:T(8,128)S(1)}, f32[5,2,32,128]{3,2,1,0:T(8,128)}, u32[]{:S(2)}) copy-start(f32[5,2,32,128]{3,2,1,0:T(8,128)} %state_ref.1) | copy-start | bytes 491524
  2.1 10.7 %copy-start.1 = (f32[32,4,128]{2,1,0:T(4,128)S(1)}, f32[32,4,128]{2,1,0:T(4,128)}, u32[]{:S(2)}) copy-start(f32[32,4,128]{2,1,0:T(4,128)} %shard_map.112._) | copy-start | bytes 196612
  2.1 23.2 %all-to-all-start = ((f32[32,4,128]{2,1,0:T(4,128)}), f32[32,4,128]{2,1,0:T(4,128)S(1)}, u32[]{:S(2)}, u32[]{:S(2)}) async-start(f32[32,4,128]{2,1,0:T(4,128)} %shard_map.112._), calls=%async_computation | async-start | bytes 131072 | tf_op jit(solution)/shard_map/all_to_all | solution.py:421
  12.9 25.6 %collective-permute-start.1 = (f32[5,2,32,128]{3,2,1,0:T(8,128)S(1)}, f32[5,2,32,128]{3,2,1,0:T(8,128)S(1)}, u32[]{:S(2)}, u32[]{:S(2)}) collective-permute-start(f32[5,2,32,128]{3,2,1,0:T(8,128)S(1)} %get-tuple-element.13.state_ref), channel_id=1, source_target_pairs={{32,0},{64,32},{96,64},{128,96},{160,128},{192,160},{224,192},{256... | collective-permute-start | bytes 491528 | tf_op jit(solution)/shard_map/ppermute | solution.py:428
  14.2 24.3 %collective-permute-start = (f32[5,2,32,128]{3,2,1,0:T(8,128)S(1)}, f32[5,2,32,128]{3,2,1,0:T(8,128)S(1)}, u32[]{:S(2)}, u32[]{:S(2)}) collective-permute-start(f32[5,2,32,128]{3,2,1,0:T(8,128)S(1)} %get-tuple-element.13.state_ref), channel_id=1, source_target_pairs={{0,32},{32,64},{64,96},{96,128},{128,160},{160,192},{192,224},{224... | collective-permute-start | bytes 491528 | tf_op jit(solution)/shard_map/ppermute | solution.py:427
  18.3 20.3 %collective-permute-start.2 = (f32[32,128]{1,0:T(8,128)S(1)}, f32[32,128]{1,0:T(8,128)S(1)}, u32[]{:S(2)}, u32[]{:S(2)}) collective-permute-start(f32[32,128]{1,0:T(8,128)S(1)} %get-tuple-element.14.edge_ref), channel_id=1, source_target_pairs={{0,1},{1,0},{2,3},{3,2},{4,5},{5,4},{6,7},{7,6},{8,9},{9,8},{10,11... | collective-permute-start | bytes 49160 | tf_op jit(solution)/shard_map/ppermute | solution.py:429
  26.1 24.4 %all-to-all-start.1 = ((f32[16,32,128]{2,1,0:T(8,128)}), f32[16,32,128]{2,1,0:T(8,128)S(1)}, u32[]{:S(2)}, u32[]{:S(2)}) async-start(f32[16,32,128]{2,1,0:T(8,128)} %shard_map.113), calls=%async_computation.1 | async-start | bytes 524288 | tf_op jit(solution)/shard_map/all_to_all | solution.py:432
  38.6 7.6 %copy-start.2 = (f32[1,64,128]{2,1,0:T(8,128)S(1)}, f32[1,64,128]{2,1,0:T(8,128)}, u32[]{:S(2)}) copy-start(f32[1,64,128]{2,1,0:T(8,128)} %param.17) | copy-start | bytes 98308
  38.7 19.6 %collective-permute-start.4 = (f32[48,128]{1,0:T(8,128)S(1)}, f32[48,128]{1,0:T(8,128)S(1)}, u32[]{:S(2)}, u32[]{:S(2)}) collective-permute-start(f32[48,128]{1,0:T(8,128)S(1)} %get-tuple-element.18.bottom_ref), channel_id=1, source_target_pairs={{0,2},{2,4},{4,6},{6,8},{8,10},{10,12},{12,14},{14,16},{16,18},{18... | collective-permute-start | bytes 73736 | tf_op jit(solution)/shard_map/ppermute | solution.py:442
  42.3 16.1 %collective-permute-start.5 = (f32[48,128]{1,0:T(8,128)S(1)}, f32[48,128]{1,0:T(8,128)S(1)}, u32[]{:S(2)}, u32[]{:S(2)}) collective-permute-start(f32[48,128]{1,0:T(8,128)S(1)} %get-tuple-element.15._.top_ref), channel_id=1, source_target_pairs={{2,0},{4,2},{6,4},{8,6},{10,8},{12,10},{14,12},{16,14},{18,16},{20... | collective-permute-start | bytes 73736 | tf_op jit(solution)/shard_map/ppermute | solution.py:443
  44.2 14.1 %collective-permute-start.3 = (f32[32,128]{1,0:T(8,128)S(1)}, f32[32,128]{1,0:T(8,128)S(1)}, u32[]{:S(2)}, u32[]{:S(2)}) collective-permute-start(f32[32,128]{1,0:T(8,128)S(1)} %get-tuple-element.17), channel_id=1, source_target_pairs={{0,1},{1,0},{2,3},{3,2},{4,5},{5,4},{6,7},{7,6},{8,9},{9,8},{10,11... | collective-permute-start | bytes 49160 | tf_op jit(solution)/shard_map/ppermute | solution.py:444
  46.2 0.7 %copy-start.6 = (s32[1,64,2]{1,2,0:T(2,128)S(1)}, s32[1,64,2]{1,2,0:T(2,128)}, u32[]{:S(2)}) copy-start(s32[1,64,2]{1,2,0:T(2,128)} %param.16) | copy-start | bytes 1540
  46.8 3.7 %copy-start.3 = (f32[1,4096]{1,0:T(1,128)S(1)}, f32[1,4096]{1,0:T(1,128)}, u32[]{:S(2)}) copy-start(f32[1,4096]{1,0:T(1,128)} %param.14) | copy-start | bytes 49156
  46.8 3.7 %copy-start.4 = (f32[1,4096]{1,0:T(1,128)S(1)}, f32[1,4096]{1,0:T(1,128)}, u32[]{:S(2)}) copy-start(f32[1,4096]{1,0:T(1,128)} %param.15) | copy-start | bytes 49156
  51.4 7.0 %copy-start.7 = (f32[5,5]{1,0:T(8,128)S(1)}, f32[5,5]{1,0:T(8,128)}, u32[]{:S(2)}) copy-start(f32[5,5]{1,0:T(8,128)} %mixing_ref.1) | copy-start | bytes 304
  51.4 13.8 %all-to-all-start.2 = ((f32[16,2,128]{2,1,0:T(2,128)}), f32[16,2,128]{2,1,0:T(2,128)S(1)}, u32[]{:S(2)}, u32[]{:S(2)}) async-start(f32[16,2,128]{2,1,0:T(2,128)} %get-tuple-element.16), calls=%async_computation.2 | async-start | bytes 32768 | tf_op jit(solution)/shard_map/all_to_all | solution.py:449
  65.2 0.7 %copy-start.5 = (f32[2,1,128]{2,1,0:T(1,128)S(1)}, f32[2,1,128]{2,1,0:T(1,128)}, u32[]{:S(2)}) copy-start(f32[2,1,128]{2,1,0:T(1,128)} %weight_ref.1) | copy-start | bytes 3076

commit v4 on v3

--- a/solution.py
+++ b/solution.py
@@ -20,7 +20,6 @@
 ROWS = 48
 
 LONG = 3_800_000_000
-LONG_SEC = 1_300_000_000
 
 VM = pl.BlockSpec(memory_space=pltpu.VMEM)
 SM = pl.BlockSpec(memory_space=pltpu.SMEM)
@@ -45,17 +44,37 @@
     return jax.ShapeDtypeStruct(shape, jnp.float32)
 
 
+def terms(x):
+    found = []
+    for _ in range(3):
+        term = x.astype(jnp.bfloat16)
+        x = x - term.astype(jnp.float32)
+        found.append(term)
+    return found
+
+
+def product(select, x, axis=0):
+    select = select.astype(jnp.bfloat16)
+    total = None
+    for term in terms(x):
+        part = lax.dot_general(
+            select, term, (((1,), (axis,)), ((), ())), preferred_element_type=jnp.float32
+        )
+        total = part if total is None else total + part
+    return total
+
+
 def offer_body(
-    patch_hbm, block_hbm, weight_hbm, state_hbm, out_ref, patch_ref, block_ref, weight_ref, wall_ref, arrived
+    patch_hbm, block_hbm, weight_hbm, state_hbm, out_ref, sent_ref, weight_ref, patch_ref, block_ref, arrived
 ):
     copies = [
         pltpu.make_async_copy(source, target, arrived.at[place])
         for place, (source, target) in enumerate(
             (
+                (state_hbm, sent_ref),
                 (patch_hbm, patch_ref),
                 (block_hbm, block_ref),
                 (weight_hbm, weight_ref),
-                (state_hbm.at[NV - 1, :, 0:8, :], wall_ref),
             )
         )
     ]
@@ -63,12 +82,18 @@
         copy.start()
     for copy in copies:
         copy.wait()
-    rows = []
-    for tile in range(2):
-        rows.append(weight_ref[tile] * wall_ref[tile, 0:1, :])
+    sec = lax.axis_index("sec")
+    column = lax.broadcasted_iota(jnp.int32, (8, LANES), 0)
+    lane = lax.broadcasted_iota(jnp.int32, (8, LANES), 1)
+    wanted = (lane == column + (LANES - 2) * (1 - sec)).astype(jnp.float32)
+    columns = product(wanted, sent_ref[...].reshape(-1, LANES), axis=1)
+    rows = [weight_ref[tile] * sent_ref[NV - 1, tile, 0:1, :] for tile in range(2)]
     for tile in range(2):
         target = patch_ref[tile] * NB + block_ref[tile]
-        rows.append(jnp.full((1, LANES), target.astype(jnp.float32)))
+        target = jnp.full((1, LANES // 2), target.astype(jnp.float32))
+        values = columns[tile : tile + 1, :]
+        rows += [values[:, :LANES], values[:, LANES : 2 * LANES]]
+        rows.append(jnp.concatenate([values[:, 2 * LANES :], target], axis=1))
     rows = jnp.concatenate(rows, axis=0)
     for receiver in range(out_ref.shape[0]):
         out_ref[receiver] = rows
@@ -77,27 +102,32 @@
 def offer(patch_map, block_map, weight, state, receivers):
     return kernel_call(
         offer_body,
-        f32(receivers, 4, LANES),
+        (f32(receivers, 8, LANES), f32(*state.shape), f32(*weight.shape)),
         [HBM] * 4,
         scratch=[
             pltpu.SMEM((2,), jnp.int32),
             pltpu.SMEM((2,), jnp.int32),
-            pltpu.VMEM((2, 1, LANES), jnp.float32),
-            pltpu.VMEM((2, 8, LANES), jnp.float32),
             pltpu.SemaphoreType.DMA((4,)),
         ],
         params=None,
     )(patch_map, block_map, weight, state)
 
 
-def collect_body(tiles_ref, out_ref):
+def targets_of(rows):
+    lane = lax.broadcasted_iota(jnp.int32, (8, LANES), 1)
+    return jnp.where(lane < LANES // 2, pltpu.roll(rows, LANES // 2, axis=1), rows)
+
+
+def collect_body(offered_ref, out_ref):
     base = (lax.axis_index("fx") * NB).astype(jnp.float32)
     block = lax.broadcasted_iota(jnp.int32, (NB, LANES), 0).astype(jnp.float32) + base
     sums = [jnp.zeros((NB, LANES), jnp.float32) for _ in range(4)]
-    for sender in range(tiles_ref.shape[0]):
+    for sender in range(offered_ref.shape[0]):
+        rows = offered_ref[sender]
+        targets = targets_of(rows)
         for tile in range(2):
-            load = tiles_ref[sender, tile : tile + 1, :]
-            target = tiles_ref[sender, 2 + tile : 3 + tile, :]
+            load = rows[tile : tile + 1, :]
+            target = targets[4 + 3 * tile : 5 + 3 * tile, :]
             slot = (2 * sender + tile) % 4
             sums[slot] = sums[slot] + jnp.where(block == target, load, 0.0)
     total = (sums[0] + sums[1]) + (sums[2] + sums[3])
@@ -105,7 +135,7 @@
         out_ref[receiver] = total
 
 
-def couple_body(connect_ref, stiff_ref, out_ref):
+def couple_body(connect_ref, stiff_ref, disp_ref, vel_ref, out_ref, disp_out, vel_out):
     elements = stiff_ref.shape[0]
     block = lax.broadcasted_iota(jnp.int32, (NB, elements), 0)
     first = connect_ref[0:1, :]
@@ -113,18 +143,13 @@
     ends = (block == first).astype(jnp.float32) - (block == second).astype(jnp.float32)
     pairs = [(ends * ends[a : a + 1, :]).astype(jnp.bfloat16) for a in range(NB)]
     pairs = jnp.concatenate(pairs, axis=0)
-    rest = stiff_ref[...]
-    total = None
-    for _ in range(3):
-        term = rest.astype(jnp.bfloat16)
-        rest = rest - term.astype(jnp.float32)
-        product = jnp.dot(pairs, term, preferred_element_type=jnp.float32)
-        total = product if total is None else total + product
-    out_ref[...] = total.reshape(NB, NB, LANES)
+    out_ref[...] = product(pairs, stiff_ref[...]).reshape(NB, NB, LANES)
+    disp_out[...] = disp_ref[...]
+    vel_out[...] = vel_ref[...]
 
 
 def shell_body(
-    loads_ref, tiles_ref, couple_ref, disp_ref, vel_ref, _, disp_out, vel_out, wall_out
+    loads_ref, offered_ref, couple_ref, disp_ref, vel_ref, _, disp_out, vel_out, wall_out
 ):
     base = (lax.axis_index("fx") * NB).astype(jnp.float32)
     sec = lax.axis_index("sec")
@@ -145,8 +170,9 @@
     wall = total * (1.0 / SUBCYCLES)
     block = lax.broadcasted_iota(jnp.int32, (NB, LANES), 0).astype(jnp.float32) + base
     for peer in range(wall_out.shape[0]):
+        targets = targets_of(offered_ref[2 * peer + sec])
         for tile in range(2):
-            target = tiles_ref[2 * peer + sec, 2 + tile : 3 + tile, :]
+            target = targets[4 + 3 * tile : 5 + 3 * tile, :]
             wanted = jnp.where(block == target, wall, 0.0)
             wall_out[peer, tile : tile + 1, :] = jnp.sum(wanted, axis=0, keepdims=True)
     disp_out[...] = disp
@@ -201,23 +227,43 @@
     pl.when(sec == 1)(lambda: pack(0))
 
 
-def first_round_body(state_ref, _, copy_ref, edge_ref):
-    copy_ref[...] = state_ref[...]
-    pack_columns({(v, xi): state_ref.at[v, xi - 1] for v in range(NV) for xi in (1, 2)}, edge_ref)
-
-
-def corner_body(beyond_ref, out_ref):
-    last = beyond_ref.shape[0] - 1
-    for place, y in enumerate((0, 1, last, last - 1)):
-        out_ref[place : place + 1, :] = beyond_ref[y : y + 1, :]
-    out_ref[4:8, :] = jnp.zeros((4, LANES), jnp.float32)
+def unpack_columns(offered_ref):
+    sec = lax.axis_index("sec")
+    fx = lax.axis_index("fx")
+    last = lax.axis_size("fx") - 1
+    rows = [
+        offered_ref[2 * jnp.maximum(fx - 1, 0) + 1 - sec] * (fx > 0).astype(jnp.float32),
+        offered_ref[2 * fx + 1 - sec],
+        offered_ref[2 * jnp.minimum(fx + 1, last) + 1 - sec] * (fx < last).astype(jnp.float32),
+        jnp.zeros((8, LANES), jnp.float32),
+    ]
+    rows = jnp.concatenate(rows, axis=0)
+
+    def place(shape):
+        l = lax.broadcasted_iota(jnp.int32, shape, 0)
+        xi = (l & 7) >> 1
+        neighbour = jnp.where(xi == 0, 0, jnp.where(xi == 3, 2, 1))
+        return neighbour, l & 1, 2 * (l >> 3) + 1 - (xi & 1)
+
+    neighbour, column, source = place((LANES, 32))
+    row = 8 * neighbour + 2 + 3 * column + (source >> 2)
+    here = lax.broadcasted_iota(jnp.int32, (LANES, 32), 1) == row
+    here &= lax.broadcasted_iota(jnp.int32, (LANES, 32), 0) < 8 * NV
+    lines = product(here.astype(jnp.float32), rows)
+    _, _, source = place((LANES, LANES))
+    position = lax.broadcasted_iota(jnp.int32, (LANES, LANES), 1)
+    lines = jnp.where((position >> 5) == (source & 3), lines, 0.0)
+    position = lax.broadcasted_iota(jnp.int32, (32, LANES), 1)
+    y = lax.broadcasted_iota(jnp.int32, (32, LANES), 0)
+    return product(((position & 31) == y).astype(jnp.float32), lines, axis=1)
 
 
 def second_round_body(
-    low_ref, state_ref, high_ref, corner_ref, top_ref, bottom_ref, edge_ref
+    low_ref, state_ref, high_ref, offered_ref, top_ref, bottom_ref, beyond_ref
 ):
+    beyond_ref[...] = unpack_columns(offered_ref)
     last = state_ref.shape[2] - 1
-    for end, (out, rows) in enumerate(((top_ref, (0, 1)), (bottom_ref, (last, last - 1)))):
+    for out, rows in ((top_ref, (0, 1)), (bottom_ref, (last, last - 1))):
         for place, y in enumerate(rows):
             for v in range(NV):
                 for xi in range(4):
@@ -225,11 +271,8 @@
                     out[spot : spot + 1, :] = slab(low_ref, state_ref, high_ref, v, xi)[
                         y : y + 1, :
                     ]
-        out[8 * NV : 8 * NV + 2, :] = corner_ref[2 * end : 2 * end + 2, :]
+            out[8 * NV + place : 8 * NV + place + 1, :] = beyond_ref[y : y + 1, :]
         out[8 * NV + 2 :, :] = jnp.zeros((6, LANES), jnp.float32)
-    outer = {(v, 0): low_ref.at[v, 1] for v in range(NV)}
-    outer |= {(v, 3): high_ref.at[v, 0] for v in range(NV)}
-    pack_columns(outer, edge_ref)
 
 
 def stencil(center, ahead, behind, others, mixed):
@@ -242,9 +285,7 @@
     low_ref,
     state_ref,
     high_ref,
-    edge_ref,
-    own_beyond_ref,
-    outer_beyond_ref,
+    beyond_ref,
     top_ref,
     bottom_ref,
     before_ref,
@@ -254,8 +295,10 @@
     field,
     section,
     packed,
+    edge_ref,
 ):
-    beyond = own_beyond_ref[...] + outer_beyond_ref[...]
+    beyond = beyond_ref[...]
+    pack_columns({(v, xi): state_ref.at[v, xi - 1] for v in range(NV) for xi in (1, 2)}, edge_ref)
     size = state_ref.shape[2]
     end = TOP + size
     sec = lax.axis_index("sec")
@@ -415,51 +458,50 @@
     up_y = [(i, i + 1) for i in range(nfy - 1)]
     down_y = [(i + 1, i) for i in range(nfy - 1)]
 
-    offered = offer(
+    offered, sent, weight = offer(
         patch_map.reshape(2), block_map.reshape(2), wall_weight, state, nfx * nsec
     )
-    tiles = lax.all_to_all(offered, ("fx", "sec"), 0, 0, tiled=True)
-
-    columns = f32(32, LANES)
-    sent, edge = kernel_call(first_round_body, (f32(*state.shape), columns), [VM, ANY])(
-        state, offered
-    )
+    offered = lax.all_to_all(offered, ("fx", "sec"), 0, 0, tiled=True)
     low = lax.ppermute(sent, "fx", up_x)
     high = lax.ppermute(sent, "fx", down_x)
-    beyond = lax.ppermute(edge, "sec", [(0, 1), (1, 0)])
-
-    partial = kernel_call(collect_body, f32(nfy, NB, LANES), [VM])(tiles)
+
+    partial = kernel_call(collect_body, f32(nfy, NB, LANES), [VM])(offered)
     loads = lax.all_to_all(partial, "fy", 0, 0, tiled=True)
 
-    couple = kernel_call(couple_body, f32(NB, NB, LANES), [VM] * 2)(
-        connect[0].T, stiffness[0]
+    block = f32(NB, LANES)
+    couple, disp, vel = kernel_call(
+        couple_body, (f32(NB, NB, LANES), block, block), [VM] * 4
+    )(
+        connect[0].T,
+        stiffness[0],
+        shell_disp.reshape(NB, LANES),
+        shell_vel.reshape(NB, LANES),
     )
-    corner = kernel_call(corner_body, f32(8, LANES), [VM], cost=LONG_SEC)(beyond)
     span = f32(8 * NV + 8, LANES)
-    top, bottom, outer_edge = kernel_call(
-        second_round_body, (span, span, columns), [VM] * 4, cost=LONG
-    )(low, sent, high, corner)
+    top, bottom, beyond = kernel_call(
+        second_round_body, (span, span, f32(32, LANES)), [VM] * 4, cost=LONG
+    )(low, sent, high, offered)
     before = lax.ppermute(bottom, "fy", up_y)
     after = lax.ppermute(top, "fy", down_y)
-    outer_beyond = lax.ppermute(outer_edge, "sec", [(0, 1), (1, 0)])
 
     new_disp, new_vel, walls = kernel_call(
-        shell_body, (f32(NB, LANES), f32(NB, LANES), f32(nfx, 2, LANES)), [VM] * 5 + [ANY]
-    )(loads, tiles, couple, shell_disp.reshape(NB, LANES), shell_vel.reshape(NB, LANES), top)
+        shell_body, (block, block, f32(nfx, 2, LANES)), [VM] * 5 + [ANY]
+    )(loads, offered, couple, disp, vel, top)
     walls = lax.all_to_all(walls, "fx", 0, 0, tiled=True)
 
     fluid, part = kernel_call(
         fluid_body,
         (f32(*state.shape), f32(2, 8, LANES)),
-        [SM] + [VM] * 10,
+        [SM] + [VM] * 8,
         scratch=[
             pltpu.VMEM((NV, 4, ROWS, LANES), jnp.float32),
             pltpu.VMEM((NV, 4, ROWS, LANES), jnp.float32),
             pltpu.VMEM((ROWS, LANES), jnp.float32),
+            pltpu.VMEM((32, LANES), jnp.float32),
         ],
         cost=LONG,
-    )(mixing, low, sent, high, edge, beyond, outer_beyond, top, bottom, before, after)
-    new_state = finish(walls, wall_weight, part, fluid)
+    )(mixing, low, sent, high, beyond, top, bottom, before, after)
+    new_state = finish(walls, weight, part, fluid)
     return (new_state, new_disp.reshape(1, -1), new_vel.reshape(1, -1))
 
 

time: 67.1 us -> 62.6 us (0.933)
  starting transfers between devices: 49.7 us -> 39.2 us
  waiting for transfers between devices: 8.21 us -> 13.9 us
    ppermute x2 -> x0, starting transfers between devices: 8.96 us -> none  [the longest x1 7.04 us: shards(): beyond = lax.ppermute(edge, 'sec', [(0, 1), (1, 0)])]
    all_to_all x1, waiting for transfers between devices: 0.01 us -> 4.06 us  [shards(): offered = lax.all_to_all(offered, ('fx', 'sec'), 0, 0, tiled=True)]
    all_to_all x1, starting transfers between devices: 6.96 us -> 5.07 us  [shards(): walls = lax.all_to_all(walls, 'fx', 0, 0, tiled=True)]
    all_to_all x1, waiting for transfers between devices: 3.31 us -> 5.01 us  [shards(): loads = lax.all_to_all(partial, 'fy', 0, 0, tiled=True)]
    pallas_call x7 -> x5, Pallas kernels: 3.82 us -> 4.29 us  [the longest x1 1.83 us: offer(): kernel_call(offer_body, (f32(receivers, 8, LANES), f32(*state.shape), f32...]
    unnamed x16 -> x14, local copies, waits for them, and re-layouts: 1.37 us -> 1.34 us
  transfers between devices with their start and end apart: 9 -> 7, of which waited for: 2 -> 3; matrix products, arithmetic and copies ran while one was open for 0% -> 0% of each run, Pallas kernels for 6% -> 7%
where the time goes in v4:
time: 62.6 us; the launch traced here: 62.1 us
  starting transfers between devices  39.2 us (63%)
  waiting for transfers between devices  13.9 us (22%)
  Pallas kernels  6.88 us (11%)
  local copies, waits for them, and re-layouts  1.34 us (2%)
  between operations  0.81 us (1%)
    all_to_all x1, starting transfers between devices, shards(): loads = lax.all_to_all(partial, 'fy', 0, 0, tiled=True)  12.7 us
    all_to_all x1, starting transfers between devices, shards(): offered = lax.all_to_all(offered, ('fx', 'sec'), 0, 0, tiled=True)  10.6 us
    all_to_all x1, starting transfers between devices, shards(): walls = lax.all_to_all(walls, 'fx', 0, 0, tiled=True)  5.07 us
    all_to_all x1, waiting for transfers between devices, shards(): loads = lax.all_to_all(partial, 'fy', 0, 0, tiled=True)  5.01 us
    all_to_all x1, waiting for transfers between devices, shards(): walls = lax.all_to_all(walls, 'fx', 0, 0, tiled=True)  4.78 us
    all_to_all x1, waiting for transfers between devices, shards(): offered = lax.all_to_all(offered, ('fx', 'sec'), 0, 0, tiled=True)  4.06 us
    ppermute x1, starting transfers between devices, shards(): low = lax.ppermute(sent, 'fx', up_x)  4 us
    ppermute x1, starting transfers between devices, shards(): before = lax.ppermute(bottom, 'fy', up_y)  3.59 us
  transfers between devices with their start and end apart: 7, of which 3 were waited for; matrix products, arithmetic and copies ran while one was open for 0% of the time, Pallas kernels for 7%

profile of v4, /device:TPU:1, one launch (start us, length us, event | category | flops | bytes accessed | tf_op | source)
XLA Modules:
  0.0 62.1 jit_solution(15250796748123036910)
XLA Ops:
  0.6 1.8 %shard_map.112 = (f32[32,8,128]{2,1,0:T(8,128)}, f32[5,2,32,128]{3,2,1,0:T(8,128)}, f32[2,1,128]{2,1,0:T(1,128)}) custom-call(s32[2]{0:T(128)} %bitcast.14, s32[2]{0:T(128)} %bitcast.15, f32[2,1,128]{2,1,0:T(1,128)} %weight_hbm.1, f32[5,2,32,128]{3,2,1,0:T(8,128)} %state_hbm.1), custom_call_target="tpu_custom_call" | custom-call | flops 20000 | bytes 20000 | tf_op jit(solution)/shard_map/pallas_call | solution.py:103
  2.5 0.0 copy-start.5
  2.5 10.6 %all-to-all-start = ((f32[32,8,128]{2,1,0:T(8,128)}), f32[32,8,128]{2,1,0:T(8,128)S(1)}, u32[]{:S(2)}, u32[]{:S(2)}) async-start(f32[32,8,128]{2,1,0:T(8,128)} %get-tuple-element.17), calls=%async_computation | async-start | bytes 262144 | tf_op jit(solution)/shard_map/all_to_all | solution.py:464
  13.1 0.0 copy-done.5
  13.1 1.3 %collective-permute-start.1 = (f32[5,2,32,128]{3,2,1,0:T(8,128)S(1)}, f32[5,2,32,128]{3,2,1,0:T(8,128)S(1)}, u32[]{:S(2)}, u32[]{:S(2)}) collective-permute-start(f32[5,2,32,128]{3,2,1,0:T(8,128)S(1)} %copy-done.5), channel_id=1, source_target_pairs={{32,0},{64,32},{96,64},{128,96},{160,128},{192,160},{224,192},{256... | collective-permute-start | bytes 491528 | tf_op jit(solution)/shard_map/ppermute | solution.py:466
  14.4 4.0 %collective-permute-start = (f32[5,2,32,128]{3,2,1,0:T(8,128)S(1)}, f32[5,2,32,128]{3,2,1,0:T(8,128)S(1)}, u32[]{:S(2)}, u32[]{:S(2)}) collective-permute-start(f32[5,2,32,128]{3,2,1,0:T(8,128)S(1)} %copy-done.5), channel_id=1, source_target_pairs={{0,32},{32,64},{64,96},{96,128},{128,160},{160,192},{192,224},{224... | collective-permute-start | bytes 491528 | tf_op jit(solution)/shard_map/ppermute | solution.py:465
  18.4 4.1 %all-to-all-done.offered_ref = f32[32,8,128]{2,1,0:T(8,128)S(1)} async-done(((f32[32,8,128]{2,1,0:T(8,128)}), f32[32,8,128]{2,1,0:T(8,128)S(1)}, u32[]{:S(2)}, u32[]{:S(2)}) %all-to-all-start) | async-done | bytes 131104 | tf_op jit(solution)/shard_map/all_to_all | solution.py:464
  22.5 0.9 %shard_map.113 = f32[16,32,128]{2,1,0:T(8,128)} custom-call(f32[32,8,128]{2,1,0:T(8,128)S(1)} %all-to-all-done.offered_ref), custom_call_target="tpu_custom_call" | custom-call | flops 20000 | bytes 20000 | tf_op jit(solution)/shard_map/pallas_call | solution.py:468
  23.4 12.7 %all-to-all-start.1 = ((f32[16,32,128]{2,1,0:T(8,128)}), f32[16,32,128]{2,1,0:T(8,128)S(1)}, u32[]{:S(2)}, u32[]{:S(2)}) async-start(f32[16,32,128]{2,1,0:T(8,128)} %shard_map.113), calls=%async_computation.1 | async-start | bytes 524288 | tf_op jit(solution)/shard_map/all_to_all | solution.py:469
  36.1 0.0 collective-permute-done.1.high_ref
  36.1 0.0 collective-permute-done.low_ref
  36.1 0.0 copy-start
  36.1 0.0 copy-start.1
  36.1 0.0 copy-start.2
  36.1 0.3 shard_map.115
  36.5 3.6 %collective-permute-start.2 = (f32[48,128]{1,0:T(8,128)S(1)}, f32[48,128]{1,0:T(8,128)S(1)}, u32[]{:S(2)}, u32[]{:S(2)}) collective-permute-start(f32[48,128]{1,0:T(8,128)S(1)} %get-tuple-element.26.bottom_ref), channel_id=1, source_target_pairs={{0,2},{2,4},{4,6},{6,8},{8,10},{10,12},{12,14},{14,16},{16,18},{18... | collective-permute-start | bytes 73736 | tf_op jit(solution)/shard_map/ppermute | solution.py:484
  40.0 1.9 %collective-permute-start.3 = (f32[48,128]{1,0:T(8,128)S(1)}, f32[48,128]{1,0:T(8,128)S(1)}, u32[]{:S(2)}, u32[]{:S(2)}) collective-permute-start(f32[48,128]{1,0:T(8,128)S(1)} %get-tuple-element.22._.top_ref), channel_id=1, source_target_pairs={{2,0},{4,2},{6,4},{8,6},{10,8},{12,10},{14,12},{16,14},{18,16},{20... | collective-permute-start | bytes 73736 | tf_op jit(solution)/shard_map/ppermute | solution.py:485
  42.0 0.0 copy-start.3
  42.0 0.0 copy-done
  42.0 0.0 copy-done.1
  42.0 0.0 copy-done.2
  42.0 0.6 %copy-done.3 = s32[1,64,2]{1,2,0:T(2,128)S(1)} copy-done((s32[1,64,2]{1,2,0:T(2,128)S(1)}, s32[1,64,2]{1,2,0:T(2,128)}, u32[]{:S(2)}) %copy-start.3) | copy-done | bytes 536
  42.7 0.3 shard_map.114
  43.0 5.0 %all-to-all-done.1.loads_ref = f32[16,32,128]{2,1,0:T(8,128)S(1)} async-done(((f32[16,32,128]{2,1,0:T(8,128)}), f32[16,32,128]{2,1,0:T(8,128)S(1)}, u32[]{:S(2)}, u32[]{:S(2)}) %all-to-all-start.1) | async-done | bytes 262176 | tf_op jit(solution)/shard_map/all_to_all | solution.py:469
  48.0 0.9 %shard_map.116 = (f32[32,128]{1,0:T(8,128)}, f32[32,128]{1,0:T(8,128)}, f32[16,2,128]{2,1,0:T(2,128)}) custom-call(f32[16,32,128]{2,1,0:T(8,128)S(1)} %all-to-all-done.1.loads_ref, f32[32,8,128]{2,1,0:T(8,128)S(1)} %all-to-all-done.offered_ref, f32[32,32,128]{2,1,0:T(8,128)S(1)} %get-tuple-element.18.couple_ref, f32[32,128]{1,0:T(8,128)S(1)} %get-tuple-element.19.disp_ref, ...), custom_call_target="tpu_custom_call" | custom-call | flops 20000 | bytes 20000 | tf_op jit(solution)/shard_map/pallas_call | solution.py:487
  48.9 0.0 copy-start.6
  48.9 5.1 %all-to-all-start.2 = ((f32[16,2,128]{2,1,0:T(2,128)}), f32[16,2,128]{2,1,0:T(2,128)S(1)}, u32[]{:S(2)}, u32[]{:S(2)}) async-start(f32[16,2,128]{2,1,0:T(2,128)} %get-tuple-element.23), calls=%async_computation.2 | async-start | bytes 32768 | tf_op jit(solution)/shard_map/all_to_all | solution.py:490
  54.0 0.0 collective-permute-done.2.before_ref
  54.0 0.0 collective-permute-done.3.after_ref
  54.0 0.0 copy-done.6
  54.0 2.0 %shard_map.117 = (f32[5,2,32,128]{3,2,1,0:T(8,128)}, f32[2,8,128]{2,1,0:T(8,128)S(1)}) custom-call(f32[5,5]{1,0:T(8,128)S(1)} %copy-done.6, f32[5,2,32,128]{3,2,1,0:T(8,128)S(1)} %collective-permute-done.low_ref, f32[5,2,32,128]{3,2,1,0:T(8,128)S(1)} %copy-done.5, f32[5,2,32,128]{3,2,1,0:T(8,128)S(1)} %collective-permute-done.1.high_ref, ...), custom_call_target="tpu_custom_call" | custom-call | flops 3800000000 | bytes 3800000000 | tf_op jit(solution)/shard_map/pallas_call | solution.py:492
  56.0 4.8 %all-to-all-done.2.walls_ref = f32[16,2,128]{2,1,0:T(2,128)S(1)} async-done(((f32[16,2,128]{2,1,0:T(2,128)}), f32[16,2,128]{2,1,0:T(2,128)S(1)}, u32[]{:S(2)}, u32[]{:S(2)}) %all-to-all-start.2) | async-done | bytes 16416 | tf_op jit(solution)/shard_map/all_to_all | solution.py:490
  60.8 0.0 copy-start.4
  60.8 0.7 %copy-done.4 = f32[2,1,128]{2,1,0:T(1,128)S(1)} copy-done((f32[2,1,128]{2,1,0:T(1,128)S(1)}, f32[2,1,128]{2,1,0:T(1,128)}, u32[]{:S(2)}) %copy-start.4) | copy-done | bytes 1048
  61.4 0.6 %shard_map.118 = f32[5,2,32,128]{3,2,1,0:T(8,128)} custom-call(f32[16,2,128]{2,1,0:T(2,128)S(1)} %all-to-all-done.2.walls_ref, f32[2,1,128]{2,1,0:T(1,128)S(1)} %copy-done.4, f32[2,8,128]{2,1,0:T(8,128)S(1)} %get-tuple-element.27.part_ref, f32[5,2,32,128]{3,2,1,0:T(8,128)} %get-tuple-element.28._), custom_call_target="tpu_custom_call", output_to_operand_aliasing={{}: (3, {})} | custom-call | flops 4096 | bytes 65536 | tf_op jit(solution)/shard_map/pallas_call | solution.py:193
Async XLA Ops:
  2.5 10.7 %copy-start.5 = (f32[5,2,32,128]{3,2,1,0:T(8,128)S(1)}, f32[5,2,32,128]{3,2,1,0:T(8,128)}, u32[]{:S(2)}) copy-start(f32[5,2,32,128]{3,2,1,0:T(8,128)} %get-tuple-element.21.state_ref) | copy-start | bytes 491524
  2.5 20.0 %all-to-all-start = ((f32[32,8,128]{2,1,0:T(8,128)}), f32[32,8,128]{2,1,0:T(8,128)S(1)}, u32[]{:S(2)}, u32[]{:S(2)}) async-start(f32[32,8,128]{2,1,0:T(8,128)} %get-tuple-element.17), calls=%async_computation | async-start | bytes 262144 | tf_op jit(solution)/shard_map/all_to_all | solution.py:464
  13.1 22.9 %collective-permute-start.1 = (f32[5,2,32,128]{3,2,1,0:T(8,128)S(1)}, f32[5,2,32,128]{3,2,1,0:T(8,128)S(1)}, u32[]{:S(2)}, u32[]{:S(2)}) collective-permute-start(f32[5,2,32,128]{3,2,1,0:T(8,128)S(1)} %copy-done.5), channel_id=1, source_target_pairs={{32,0},{64,32},{96,64},{128,96},{160,128},{192,160},{224,192},{256... | collective-permute-start | bytes 491528 | tf_op jit(solution)/shard_map/ppermute | solution.py:466
  14.4 21.6 %collective-permute-start = (f32[5,2,32,128]{3,2,1,0:T(8,128)S(1)}, f32[5,2,32,128]{3,2,1,0:T(8,128)S(1)}, u32[]{:S(2)}, u32[]{:S(2)}) collective-permute-start(f32[5,2,32,128]{3,2,1,0:T(8,128)S(1)} %copy-done.5), channel_id=1, source_target_pairs={{0,32},{32,64},{64,96},{96,128},{128,160},{160,192},{192,224},{224... | collective-permute-start | bytes 491528 | tf_op jit(solution)/shard_map/ppermute | solution.py:465
  23.4 24.6 %all-to-all-start.1 = ((f32[16,32,128]{2,1,0:T(8,128)}), f32[16,32,128]{2,1,0:T(8,128)S(1)}, u32[]{:S(2)}, u32[]{:S(2)}) async-start(f32[16,32,128]{2,1,0:T(8,128)} %shard_map.113), calls=%async_computation.1 | async-start | bytes 524288 | tf_op jit(solution)/shard_map/all_to_all | solution.py:469
  36.1 5.9 %copy-start = (f32[1,64,128]{2,1,0:T(8,128)S(1)}, f32[1,64,128]{2,1,0:T(8,128)}, u32[]{:S(2)}) copy-start(f32[1,64,128]{2,1,0:T(8,128)} %param.17) | copy-start | bytes 98308
  36.1 5.9 %copy-start.1 = (f32[1,4096]{1,0:T(1,128)S(1)}, f32[1,4096]{1,0:T(1,128)}, u32[]{:S(2)}) copy-start(f32[1,4096]{1,0:T(1,128)} %param.14) | copy-start | bytes 49156
  36.1 5.9 %copy-start.2 = (f32[1,4096]{1,0:T(1,128)S(1)}, f32[1,4096]{1,0:T(1,128)}, u32[]{:S(2)}) copy-start(f32[1,4096]{1,0:T(1,128)} %param.15) | copy-start | bytes 49156
  36.5 17.5 %collective-permute-start.2 = (f32[48,128]{1,0:T(8,128)S(1)}, f32[48,128]{1,0:T(8,128)S(1)}, u32[]{:S(2)}, u32[]{:S(2)}) collective-permute-start(f32[48,128]{1,0:T(8,128)S(1)} %get-tuple-element.26.bottom_ref), channel_id=1, source_target_pairs={{0,2},{2,4},{4,6},{6,8},{8,10},{10,12},{12,14},{14,16},{16,18},{18... | collective-permute-start | bytes 73736 | tf_op jit(solution)/shard_map/ppermute | solution.py:484
  40.0 14.0 %collective-permute-start.3 = (f32[48,128]{1,0:T(8,128)S(1)}, f32[48,128]{1,0:T(8,128)S(1)}, u32[]{:S(2)}, u32[]{:S(2)}) collective-permute-start(f32[48,128]{1,0:T(8,128)S(1)} %get-tuple-element.22._.top_ref), channel_id=1, source_target_pairs={{2,0},{4,2},{6,4},{8,6},{10,8},{12,10},{14,12},{16,14},{18,16},{20... | collective-permute-start | bytes 73736 | tf_op jit(solution)/shard_map/ppermute | solution.py:485
  42.0 0.7 %copy-start.3 = (s32[1,64,2]{1,2,0:T(2,128)S(1)}, s32[1,64,2]{1,2,0:T(2,128)}, u32[]{:S(2)}) copy-start(s32[1,64,2]{1,2,0:T(2,128)} %param.16) | copy-start | bytes 1540
  48.9 5.1 %copy-start.6 = (f32[5,5]{1,0:T(8,128)S(1)}, f32[5,5]{1,0:T(8,128)}, u32[]{:S(2)}) copy-start(f32[5,5]{1,0:T(8,128)} %mixing_ref.1) | copy-start | bytes 304
  48.9 11.9 %all-to-all-start.2 = ((f32[16,2,128]{2,1,0:T(2,128)}), f32[16,2,128]{2,1,0:T(2,128)S(1)}, u32[]{:S(2)}, u32[]{:S(2)}) async-start(f32[16,2,128]{2,1,0:T(2,128)} %get-tuple-element.23), calls=%async_computation.2 | async-start | bytes 32768 | tf_op jit(solution)/shard_map/all_to_all | solution.py:490
  60.8 0.7 %copy-start.4 = (f32[2,1,128]{2,1,0:T(1,128)S(1)}, f32[2,1,128]{2,1,0:T(1,128)}, u32[]{:S(2)}) copy-start(f32[2,1,128]{2,1,0:T(1,128)} %get-tuple-element.24.weight_ref) | copy-start | bytes 3076

commit v5 on v4

--- a/solution.py
+++ b/solution.py
@@ -65,13 +65,22 @@
 
 
 def offer_body(
-    patch_hbm, block_hbm, weight_hbm, state_hbm, out_ref, sent_ref, weight_ref, patch_ref, block_ref, arrived
+    patch_hbm,
+    block_hbm,
+    weight_hbm,
+    state_hbm,
+    out_ref,
+    patch_ref,
+    block_ref,
+    weight_ref,
+    state_ref,
+    arrived,
 ):
     copies = [
         pltpu.make_async_copy(source, target, arrived.at[place])
         for place, (source, target) in enumerate(
             (
-                (state_hbm, sent_ref),
+                (state_hbm, state_ref),
                 (patch_hbm, patch_ref),
                 (block_hbm, block_ref),
                 (weight_hbm, weight_ref),
@@ -86,8 +95,8 @@
     column = lax.broadcasted_iota(jnp.int32, (8, LANES), 0)
     lane = lax.broadcasted_iota(jnp.int32, (8, LANES), 1)
     wanted = (lane == column + (LANES - 2) * (1 - sec)).astype(jnp.float32)
-    columns = product(wanted, sent_ref[...].reshape(-1, LANES), axis=1)
-    rows = [weight_ref[tile] * sent_ref[NV - 1, tile, 0:1, :] for tile in range(2)]
+    columns = product(wanted, state_ref[...].reshape(-1, LANES), axis=1)
+    rows = [weight_ref[tile] * state_ref[NV - 1, tile, 0:1, :] for tile in range(2)]
     for tile in range(2):
         target = patch_ref[tile] * NB + block_ref[tile]
         target = jnp.full((1, LANES // 2), target.astype(jnp.float32))
@@ -102,11 +111,13 @@
 def offer(patch_map, block_map, weight, state, receivers):
     return kernel_call(
         offer_body,
-        (f32(receivers, 8, LANES), f32(*state.shape), f32(*weight.shape)),
+        f32(receivers, 8, LANES),
         [HBM] * 4,
         scratch=[
             pltpu.SMEM((2,), jnp.int32),
             pltpu.SMEM((2,), jnp.int32),
+            pltpu.VMEM(weight.shape, jnp.float32),
+            pltpu.VMEM(state.shape, jnp.float32),
             pltpu.SemaphoreType.DMA((4,)),
         ],
         params=None,
@@ -135,7 +146,9 @@
         out_ref[receiver] = total
 
 
-def couple_body(connect_ref, stiff_ref, disp_ref, vel_ref, out_ref, disp_out, vel_out):
+def couple_body(
+    connect_ref, stiff_ref, disp_ref, vel_ref, weight_ref, out_ref, disp_out, vel_out, weight_out
+):
     elements = stiff_ref.shape[0]
     block = lax.broadcasted_iota(jnp.int32, (NB, elements), 0)
     first = connect_ref[0:1, :]
@@ -146,6 +159,7 @@
     out_ref[...] = product(pairs, stiff_ref[...]).reshape(NB, NB, LANES)
     disp_out[...] = disp_ref[...]
     vel_out[...] = vel_ref[...]
+    weight_out[...] = weight_ref[...]
 
 
 def shell_body(
@@ -202,12 +216,17 @@
     )(walls, weight, part, state)
 
 
-def slab(low_ref, state_ref, high_ref, v, xi):
-    if xi == 0:
-        return low_ref.at[v, 1]
-    if xi == 3:
-        return high_ref.at[v, 0]
-    return state_ref.at[v, xi - 1]
+def sides(axis, near, far):
+    even = lax.rem(lax.axis_index(axis), 2) == 0
+    return jnp.where(even, far, near), jnp.where(even, near, far)
+
+
+def slab(near_ref, state_ref, far_ref, v, xi, rows=slice(None)):
+    if xi < 1:
+        return sides("fx", near_ref[v, 1 + xi, rows, :], far_ref[v, 1 + xi, rows, :])[0]
+    if xi > 2:
+        return sides("fx", near_ref[v, xi - 3, rows, :], far_ref[v, xi - 3, rows, :])[1]
+    return state_ref[v, xi - 1, rows, :]
 
 
 def pack_columns(slabs, out_ref):
@@ -259,19 +278,28 @@
 
 
 def second_round_body(
-    low_ref, state_ref, high_ref, offered_ref, top_ref, bottom_ref, beyond_ref
+    near_ref, state_ref, far_ref, offered_ref, to_near_ref, to_far_ref, beyond_ref
 ):
     beyond_ref[...] = unpack_columns(offered_ref)
     last = state_ref.shape[2] - 1
-    for out, rows in ((top_ref, (0, 1)), (bottom_ref, (last, last - 1))):
-        for place, y in enumerate(rows):
-            for v in range(NV):
-                for xi in range(4):
-                    spot = 8 * v + 4 * place + xi
-                    out[spot : spot + 1, :] = slab(low_ref, state_ref, high_ref, v, xi)[
-                        y : y + 1, :
-                    ]
-            out[8 * NV + place : 8 * NV + place + 1, :] = beyond_ref[y : y + 1, :]
+
+    def put(spot, low, high):
+        to_far, to_near = sides("fy", high, low)
+        to_near_ref[spot : spot + 1, :] = to_near
+        to_far_ref[spot : spot + 1, :] = to_far
+
+    for place in range(2):
+        low = slice(place, place + 1)
+        high = slice(last - place, last - place + 1)
+        for v in range(NV):
+            for xi in range(4):
+                put(
+                    8 * v + 4 * place + xi,
+                    slab(near_ref, state_ref, far_ref, v, xi, low),
+                    slab(near_ref, state_ref, far_ref, v, xi, high),
+                )
+        put(8 * NV + place, beyond_ref[low, :], beyond_ref[high, :])
+    for out in (to_near_ref, to_far_ref):
         out[8 * NV + 2 :, :] = jnp.zeros((6, LANES), jnp.float32)
 
 
@@ -282,14 +310,14 @@
 
 def fluid_body(
     mixing_ref,
-    low_ref,
+    near_ref,
     state_ref,
-    high_ref,
+    far_ref,
     beyond_ref,
-    top_ref,
-    bottom_ref,
-    before_ref,
-    after_ref,
+    to_near_ref,
+    to_far_ref,
+    from_near_ref,
+    from_far_ref,
     out_ref,
     part_ref,
     field,
@@ -297,6 +325,8 @@
     packed,
     edge_ref,
 ):
+    top, bottom = sides("fy", to_near_ref[...], to_far_ref[...])
+    before, after = sides("fy", from_near_ref[...], from_far_ref[...])
     beyond = beyond_ref[...]
     pack_columns({(v, xi): state_ref.at[v, xi - 1] for v in range(NV) for xi in (1, 2)}, edge_ref)
     size = state_ref.shape[2]
@@ -331,8 +361,8 @@
         return total
 
     packed[TOP:end, :] = beyond
-    packed[TOP - 1 : TOP, :] = before_ref[8 * NV : 8 * NV + 1, :]
-    packed[end : end + 1, :] = after_ref[8 * NV : 8 * NV + 1, :]
+    packed[TOP - 1 : TOP, :] = before[8 * NV : 8 * NV + 1, :]
+    packed[end : end + 1, :] = after[8 * NV : 8 * NV + 1, :]
     group = lane // 8
     mixed_columns = jnp.zeros((size, LANES), jnp.float32)
     for shift in range(1 - NV, NV):
@@ -358,17 +388,17 @@
     row_cells = []
     row_others = []
     row_columns = jnp.where(
-        row < 4, before_ref[8 * NV : 8 * NV + 1, :], after_ref[8 * NV : 8 * NV + 1, :]
+        row < 4, before[8 * NV : 8 * NV + 1, :], after[8 * NV : 8 * NV + 1, :]
     )
     for v in range(NV):
         cells = jnp.concatenate(
-            [before_ref[8 * v : 8 * v + 4, :], after_ref[8 * v : 8 * v + 4, :]], axis=0
+            [before[8 * v : 8 * v + 4, :], after[8 * v : 8 * v + 4, :]], axis=0
         )
         outer = jnp.concatenate(
-            [before_ref[8 * v + 4 : 8 * v + 8, :], after_ref[8 * v + 4 : 8 * v + 8, :]], axis=0
+            [before[8 * v + 4 : 8 * v + 8, :], after[8 * v + 4 : 8 * v + 8, :]], axis=0
         )
         inner = jnp.concatenate(
-            [top_ref[8 * v : 8 * v + 4, :], bottom_ref[8 * v : 8 * v + 4, :]], axis=0
+            [top[8 * v : 8 * v + 4, :], bottom[8 * v : 8 * v + 4, :]], axis=0
         )
         columns = jnp.zeros((8, LANES), jnp.float32)
         for xi in (1, 2):
@@ -390,22 +420,20 @@
             row_others[v],
             mixed(row_cells, v),
         )
-        after = inside_rows * (cells + TIME_STEP * rate)
+        later = inside_rows * (cells + TIME_STEP * rate)
         for xi in (1, 2):
-            section[v, xi, TOP - 1 : TOP, :] = after[xi : xi + 1, :]
-            section[v, xi, end : end + 1, :] = after[4 + xi : 5 + xi, :]
+            section[v, xi, TOP - 1 : TOP, :] = later[xi : xi + 1, :]
+            section[v, xi, end : end + 1, :] = later[4 + xi : 5 + xi, :]
 
     for v in range(NV):
         for xi in range(4):
-            field[v, xi, TOP:end, :] = slab(low_ref, state_ref, high_ref, v, xi)[...]
-            field[v, xi, TOP - 1 : TOP, :] = before_ref[8 * v + xi : 8 * v + xi + 1, :]
-            field[v, xi, end : end + 1, :] = after_ref[8 * v + xi : 8 * v + xi + 1, :]
+            field[v, xi, TOP:end, :] = slab(near_ref, state_ref, far_ref, v, xi)
+            field[v, xi, TOP - 1 : TOP, :] = before[8 * v + xi : 8 * v + xi + 1, :]
+            field[v, xi, end : end + 1, :] = after[8 * v + xi : 8 * v + xi + 1, :]
 
     def center(v, x):
-        if x < 0:
-            return low_ref[v, 0]
-        if x > 3:
-            return high_ref[v, 1]
+        if x < 0 or x > 3:
+            return slab(near_ref, state_ref, far_ref, v, x)
         return field[v, x, TOP:end, :]
 
     for xi in range(4):
@@ -419,12 +447,12 @@
             rate = stencil(
                 cells[v], center(v, xi + 1), center(v, xi - 1), others, mixed(cells, v)
             )
-            after = cells[v] + TIME_STEP * rate
+            later = cells[v] + TIME_STEP * rate
             if xi == 0:
-                after = inside_low * after
+                later = inside_low * later
             if xi == 3:
-                after = inside_high * after
-            section[v, xi, TOP:end, :] = after
+                later = inside_high * later
+            section[v, xi, TOP:end, :] = later
             if xi in (1, 2):
                 out_ref[v, xi - 1] = cells[v] + 0.5 * TIME_STEP * rate
 
@@ -453,40 +481,42 @@
     state, mixing, wall_weight, patch_map, block_map, shell_disp, shell_vel, connect, stiffness
 ):
     nfx, nfy, nsec = (lax.axis_size(axis) for axis in ("fx", "fy", "sec"))
-    up_x = [(i, i + 1) for i in range(nfx - 1)]
-    down_x = [(i + 1, i) for i in range(nfx - 1)]
-    up_y = [(i, i + 1) for i in range(nfy - 1)]
-    down_y = [(i + 1, i) for i in range(nfy - 1)]
-
-    offered, sent, weight = offer(
+    near_x, far_x, near_y, far_y = (
+        [pair for i in range(first, n - 1, 2) for pair in ((i, i + 1), (i + 1, i))]
+        for n in (nfx, nfy)
+        for first in (0, 1)
+    )
+
+    offered = offer(
         patch_map.reshape(2), block_map.reshape(2), wall_weight, state, nfx * nsec
     )
     offered = lax.all_to_all(offered, ("fx", "sec"), 0, 0, tiled=True)
-    low = lax.ppermute(sent, "fx", up_x)
-    high = lax.ppermute(sent, "fx", down_x)
+    near = lax.ppermute(state, "fx", near_x)
+    far = lax.ppermute(state, "fx", far_x)
 
     partial = kernel_call(collect_body, f32(nfy, NB, LANES), [VM])(offered)
     loads = lax.all_to_all(partial, "fy", 0, 0, tiled=True)
 
     block = f32(NB, LANES)
-    couple, disp, vel = kernel_call(
-        couple_body, (f32(NB, NB, LANES), block, block), [VM] * 4
+    couple, disp, vel, weight = kernel_call(
+        couple_body, (f32(NB, NB, LANES), block, block, f32(*wall_weight.shape)), [VM] * 5
     )(
         connect[0].T,
         stiffness[0],
         shell_disp.reshape(NB, LANES),
         shell_vel.reshape(NB, LANES),
+        wall_weight,
     )
     span = f32(8 * NV + 8, LANES)
-    top, bottom, beyond = kernel_call(
+    to_near, to_far, beyond = kernel_call(
         second_round_body, (span, span, f32(32, LANES)), [VM] * 4, cost=LONG
-    )(low, sent, high, offered)
-    before = lax.ppermute(bottom, "fy", up_y)
-    after = lax.ppermute(top, "fy", down_y)
+    )(near, state, far, offered)
+    from_near = lax.ppermute(to_near, "fy", near_y)
+    from_far = lax.ppermute(to_far, "fy", far_y)
 
     new_disp, new_vel, walls = kernel_call(
         shell_body, (block, block, f32(nfx, 2, LANES)), [VM] * 5 + [ANY]
-    )(loads, offered, couple, disp, vel, top)
+    )(loads, offered, couple, disp, vel, to_near)
     walls = lax.all_to_all(walls, "fx", 0, 0, tiled=True)
 
     fluid, part = kernel_call(
@@ -500,7 +530,7 @@
             pltpu.VMEM((32, LANES), jnp.float32),
         ],
         cost=LONG,
-    )(mixing, low, sent, high, beyond, top, bottom, before, after)
+    )(mixing, near, state, far, beyond, to_near, to_far, from_near, from_far)
     new_state = finish(walls, weight, part, fluid)
     return (new_state, new_disp.reshape(1, -1), new_vel.reshape(1, -1))
 

time: 62.6 us -> 60.5 us (0.966)
  waiting for transfers between devices: 13.9 us -> 12.9 us
  local copies, waits for them, and re-layouts: 1.34 us -> 0.67 us
    all_to_all x1, starting transfers between devices: 5.07 us -> 3.62 us  [shards(): walls = lax.all_to_all(walls, 'fx', 0, 0, tiled=True)]
    ppermute x4, starting transfers between devices: 10.8 us -> 11.7 us  [the longest x1 5.56 us: shards(): near = lax.ppermute(state, 'fx', near_x)]
    all_to_all x1, waiting for transfers between devices: 4.06 us -> 3.14 us  [shards(): offered = lax.all_to_all(offered, ('fx', 'sec'), 0, 0, tiled=True)]
    unnamed x14, local copies, waits for them, and re-layouts: 1.34 us -> 0.67 us
where the time goes in v5:
time: 60.5 us; the launch traced here: 60 us
  starting transfers between devices  38.7 us (64%)
  waiting for transfers between devices  12.9 us (21%)
  Pallas kernels  6.91 us (11%)
  between operations  0.82 us (1%)
  local copies, waits for them, and re-layouts  0.67 us (1%)
    all_to_all x1, starting transfers between devices, shards(): loads = lax.all_to_all(partial, 'fy', 0, 0, tiled=True)  12.7 us
    all_to_all x1, starting transfers between devices, shards(): offered = lax.all_to_all(offered, ('fx', 'sec'), 0, 0, tiled=True)  10.6 us
    ppermute x1, starting transfers between devices, shards(): near = lax.ppermute(state, 'fx', near_x)  5.56 us
    all_to_all x1, waiting for transfers between devices, shards(): loads = lax.all_to_all(partial, 'fy', 0, 0, tiled=True)  4.98 us
    all_to_all x1, waiting for transfers between devices, shards(): walls = lax.all_to_all(walls, 'fx', 0, 0, tiled=True)  4.82 us
    all_to_all x1, starting transfers between devices, shards(): walls = lax.all_to_all(walls, 'fx', 0, 0, tiled=True)  3.62 us
    ppermute x1, starting transfers between devices, shards(): from_far = lax.ppermute(to_far, 'fy', far_y)  3.59 us
    all_to_all x1, waiting for transfers between devices, shards(): offered = lax.all_to_all(offered, ('fx', 'sec'), 0, 0, tiled=True)  3.14 us
  transfers between devices with their start and end apart: 7, of which 3 were waited for; matrix products, arithmetic and copies ran while one was open for 0% of the time, Pallas kernels for 7%

profile of v5, /device:TPU:1, one launch (start us, length us, event | category | flops | bytes accessed | tf_op | source)
XLA Modules:
  0.0 60.0 jit_solution(14416686740076731011)
XLA Ops:
  0.6 1.8 %shard_map.112 = f32[32,8,128]{2,1,0:T(8,128)} custom-call(s32[2]{0:T(128)} %bitcast.14, s32[2]{0:T(128)} %bitcast.15, f32[2,1,128]{2,1,0:T(1,128)} %weight_ref.1, f32[5,2,32,128]{3,2,1,0:T(8,128)} %state_ref.3), custom_call_target="tpu_custom_call" | custom-call | flops 20000 | bytes 20000 | tf_op jit(solution)/shard_map/pallas_call | solution.py:112
  2.5 0.0 copy-start
  2.5 10.6 %all-to-all-start = ((f32[32,8,128]{2,1,0:T(8,128)}), f32[32,8,128]{2,1,0:T(8,128)S(1)}, u32[]{:S(2)}, u32[]{:S(2)}) async-start(f32[32,8,128]{2,1,0:T(8,128)} %shard_map.112), calls=%async_computation | async-start | bytes 262144 | tf_op jit(solution)/shard_map/all_to_all | solution.py:493
  13.1 0.0 copy-done
  13.2 0.7 %collective-permute-start.1 = (f32[5,2,32,128]{3,2,1,0:T(8,128)S(1)}, f32[5,2,32,128]{3,2,1,0:T(8,128)S(1)}, u32[]{:S(2)}, u32[]{:S(2)}) collective-permute-start(f32[5,2,32,128]{3,2,1,0:T(8,128)S(1)} %copy-done), channel_id=1, source_target_pairs={{32,64},{64,32},{96,128},{128,96},{160,192},{192,160},{224,256},{2... | collective-permute-start | bytes 491528 | tf_op jit(solution)/shard_map/ppermute | solution.py:495
  13.8 5.6 %collective-permute-start = (f32[5,2,32,128]{3,2,1,0:T(8,128)S(1)}, f32[5,2,32,128]{3,2,1,0:T(8,128)S(1)}, u32[]{:S(2)}, u32[]{:S(2)}) collective-permute-start(f32[5,2,32,128]{3,2,1,0:T(8,128)S(1)} %copy-done), channel_id=1, source_target_pairs={{0,32},{32,0},{64,96},{96,64},{128,160},{160,128},{192,224},{224,1... | collective-permute-start | bytes 491528 | tf_op jit(solution)/shard_map/ppermute | solution.py:494
  19.4 3.1 %all-to-all-done.offered_ref = f32[32,8,128]{2,1,0:T(8,128)S(1)} async-done(((f32[32,8,128]{2,1,0:T(8,128)}), f32[32,8,128]{2,1,0:T(8,128)S(1)}, u32[]{:S(2)}, u32[]{:S(2)}) %all-to-all-start) | async-done | bytes 131104 | tf_op jit(solution)/shard_map/all_to_all | solution.py:493
  22.5 0.9 %shard_map.113 = f32[16,32,128]{2,1,0:T(8,128)} custom-call(f32[32,8,128]{2,1,0:T(8,128)S(1)} %all-to-all-done.offered_ref), custom_call_target="tpu_custom_call" | custom-call | flops 20000 | bytes 20000 | tf_op jit(solution)/shard_map/pallas_call | solution.py:497
  23.4 12.7 %all-to-all-start.1 = ((f32[16,32,128]{2,1,0:T(8,128)}), f32[16,32,128]{2,1,0:T(8,128)S(1)}, u32[]{:S(2)}, u32[]{:S(2)}) async-start(f32[16,32,128]{2,1,0:T(8,128)} %shard_map.113), calls=%async_computation.1 | async-start | bytes 524288 | tf_op jit(solution)/shard_map/all_to_all | solution.py:498
  36.1 0.0 collective-permute-done.1.far_ref
  36.1 0.0 collective-permute-done.near_ref
  36.1 0.0 copy-start.1
  36.1 0.0 copy-start.2
  36.1 0.0 copy-start.3
  36.1 0.0 copy-start.5
  36.2 0.3 shard_map.115
  36.5 3.6 %collective-permute-start.3 = (f32[48,128]{1,0:T(8,128)S(1)}, f32[48,128]{1,0:T(8,128)S(1)}, u32[]{:S(2)}, u32[]{:S(2)}) collective-permute-start(f32[48,128]{1,0:T(8,128)S(1)} %get-tuple-element.22.to_far_ref), channel_id=1, source_target_pairs={{2,4},{4,2},{6,8},{8,6},{10,12},{12,10},{14,16},{16,14},{18,20},{2... | collective-permute-start | bytes 73736 | tf_op jit(solution)/shard_map/ppermute | solution.py:515
  40.1 1.9 %collective-permute-start.2 = (f32[48,128]{1,0:T(8,128)S(1)}, f32[48,128]{1,0:T(8,128)S(1)}, u32[]{:S(2)}, u32[]{:S(2)}) collective-permute-start(f32[48,128]{1,0:T(8,128)S(1)} %get-tuple-element.18._.to_near_ref), channel_id=1, source_target_pairs={{0,2},{2,0},{4,6},{6,4},{8,10},{10,8},{12,14},{14,12},{16,18},{18,... | collective-permute-start | bytes 73736 | tf_op jit(solution)/shard_map/ppermute | solution.py:514
  42.0 0.0 copy-start.4
  42.0 0.0 copy-done.1
  42.1 0.0 copy-done.2
  42.1 0.0 copy-done.3
  42.1 0.0 copy-done.5
  42.1 0.6 %copy-done.4 = f32[2,1,128]{2,1,0:T(1,128)S(1)} copy-done((f32[2,1,128]{2,1,0:T(1,128)S(1)}, f32[2,1,128]{2,1,0:T(1,128)}, u32[]{:S(2)}) %copy-start.4) | copy-done | bytes 1048
  42.7 0.3 shard_map.114
  43.1 5.0 %all-to-all-done.1.loads_ref = f32[16,32,128]{2,1,0:T(8,128)S(1)} async-done(((f32[16,32,128]{2,1,0:T(8,128)}), f32[16,32,128]{2,1,0:T(8,128)S(1)}, u32[]{:S(2)}, u32[]{:S(2)}) %all-to-all-start.1) | async-done | bytes 262176 | tf_op jit(solution)/shard_map/all_to_all | solution.py:498
  48.0 0.9 %shard_map.116 = (f32[32,128]{1,0:T(8,128)}, f32[32,128]{1,0:T(8,128)}, f32[16,2,128]{2,1,0:T(2,128)}) custom-call(f32[16,32,128]{2,1,0:T(8,128)S(1)} %all-to-all-done.1.loads_ref, f32[32,8,128]{2,1,0:T(8,128)S(1)} %all-to-all-done.offered_ref, f32[32,32,128]{2,1,0:T(8,128)S(1)} %get-tuple-element.15.couple_ref, f32[32,128]{1,0:T(8,128)S(1)} %get-tuple-element.16.disp_ref, ...), custom_call_target="tpu_custom_call" | custom-call | flops 20000 | bytes 20000 | tf_op jit(solution)/shard_map/pallas_call | solution.py:517
  48.9 0.0 copy-start.6
  48.9 3.6 %all-to-all-start.2 = ((f32[16,2,128]{2,1,0:T(2,128)}), f32[16,2,128]{2,1,0:T(2,128)S(1)}, u32[]{:S(2)}, u32[]{:S(2)}) async-start(f32[16,2,128]{2,1,0:T(2,128)} %get-tuple-element.19), calls=%async_computation.2 | async-start | bytes 32768 | tf_op jit(solution)/shard_map/all_to_all | solution.py:520
  52.6 0.0 collective-permute-done.3.from_far_ref
  52.6 0.0 collective-permute-done.2.from_near_ref
  52.6 0.0 copy-done.6
  52.6 2.0 %shard_map.117 = (f32[5,2,32,128]{3,2,1,0:T(8,128)}, f32[2,8,128]{2,1,0:T(8,128)S(1)}) custom-call(f32[5,5]{1,0:T(8,128)S(1)} %copy-done.6, f32[5,2,32,128]{3,2,1,0:T(8,128)S(1)} %collective-permute-done.near_ref, f32[5,2,32,128]{3,2,1,0:T(8,128)S(1)} %copy-done, f32[5,2,32,128]{3,2,1,0:T(8,128)S(1)} %collective-permute-done.1.far_ref, ...), custom_call_target="tpu_custom_call" | custom-call | flops 3800000000 | bytes 3800000000 | tf_op jit(solution)/shard_map/pallas_call | solution.py:522
  54.6 4.8 %all-to-all-done.2.walls_ref = f32[16,2,128]{2,1,0:T(2,128)S(1)} async-done(((f32[16,2,128]{2,1,0:T(2,128)}), f32[16,2,128]{2,1,0:T(2,128)S(1)}, u32[]{:S(2)}, u32[]{:S(2)}) %all-to-all-start.2) | async-done | bytes 16416 | tf_op jit(solution)/shard_map/all_to_all | solution.py:520
  59.4 0.6 %shard_map.118 = f32[5,2,32,128]{3,2,1,0:T(8,128)} custom-call(f32[16,2,128]{2,1,0:T(2,128)S(1)} %all-to-all-done.2.walls_ref, f32[2,1,128]{2,1,0:T(1,128)S(1)} %get-tuple-element.20.weight_ref, f32[2,8,128]{2,1,0:T(8,128)S(1)} %get-tuple-element.23.part_ref, f32[5,2,32,128]{3,2,1,0:T(8,128)} %get-tuple-element.24._), custom_call_target="tpu_custom_call", output_to_operand_aliasing={{}: (3, {})} | custom-call | flops 4096 | bytes 65536 | tf_op jit(solution)/shard_map/pallas_call | solution.py:207
Async XLA Ops:
  2.5 10.7 %copy-start = (f32[5,2,32,128]{3,2,1,0:T(8,128)S(1)}, f32[5,2,32,128]{3,2,1,0:T(8,128)}, u32[]{:S(2)}) copy-start(f32[5,2,32,128]{3,2,1,0:T(8,128)} %state_ref.3) | copy-start | bytes 491524
  2.5 20.0 %all-to-all-start = ((f32[32,8,128]{2,1,0:T(8,128)}), f32[32,8,128]{2,1,0:T(8,128)S(1)}, u32[]{:S(2)}, u32[]{:S(2)}) async-start(f32[32,8,128]{2,1,0:T(8,128)} %shard_map.112), calls=%async_computation | async-start | bytes 262144 | tf_op jit(solution)/shard_map/all_to_all | solution.py:493
  13.2 22.9 %collective-permute-start.1 = (f32[5,2,32,128]{3,2,1,0:T(8,128)S(1)}, f32[5,2,32,128]{3,2,1,0:T(8,128)S(1)}, u32[]{:S(2)}, u32[]{:S(2)}) collective-permute-start(f32[5,2,32,128]{3,2,1,0:T(8,128)S(1)} %copy-done), channel_id=1, source_target_pairs={{32,64},{64,32},{96,128},{128,96},{160,192},{192,160},{224,256},{2... | collective-permute-start | bytes 491528 | tf_op jit(solution)/shard_map/ppermute | solution.py:495
  13.8 22.3 %collective-permute-start = (f32[5,2,32,128]{3,2,1,0:T(8,128)S(1)}, f32[5,2,32,128]{3,2,1,0:T(8,128)S(1)}, u32[]{:S(2)}, u32[]{:S(2)}) collective-permute-start(f32[5,2,32,128]{3,2,1,0:T(8,128)S(1)} %copy-done), channel_id=1, source_target_pairs={{0,32},{32,0},{64,96},{96,64},{128,160},{160,128},{192,224},{224,1... | collective-permute-start | bytes 491528 | tf_op jit(solution)/shard_map/ppermute | solution.py:494
  23.4 24.6 %all-to-all-start.1 = ((f32[16,32,128]{2,1,0:T(8,128)}), f32[16,32,128]{2,1,0:T(8,128)S(1)}, u32[]{:S(2)}, u32[]{:S(2)}) async-start(f32[16,32,128]{2,1,0:T(8,128)} %shard_map.113), calls=%async_computation.1 | async-start | bytes 524288 | tf_op jit(solution)/shard_map/all_to_all | solution.py:498
  36.1 5.9 %copy-start.1 = (f32[1,64,128]{2,1,0:T(8,128)S(1)}, f32[1,64,128]{2,1,0:T(8,128)}, u32[]{:S(2)}) copy-start(f32[1,64,128]{2,1,0:T(8,128)} %param.17) | copy-start | bytes 98308
  36.1 5.9 %copy-start.2 = (f32[1,4096]{1,0:T(1,128)S(1)}, f32[1,4096]{1,0:T(1,128)}, u32[]{:S(2)}) copy-start(f32[1,4096]{1,0:T(1,128)} %param.14) | copy-start | bytes 49156
  36.1 5.9 %copy-start.3 = (f32[1,4096]{1,0:T(1,128)S(1)}, f32[1,4096]{1,0:T(1,128)}, u32[]{:S(2)}) copy-start(f32[1,4096]{1,0:T(1,128)} %param.15) | copy-start | bytes 49156
  36.1 5.9 %copy-start.5 = (s32[1,64,2]{1,2,0:T(2,128)S(1)}, s32[1,64,2]{1,2,0:T(2,128)}, u32[]{:S(2)}) copy-start(s32[1,64,2]{1,2,0:T(2,128)} %param.16) | copy-start | bytes 1540
  36.5 16.1 %collective-permute-start.3 = (f32[48,128]{1,0:T(8,128)S(1)}, f32[48,128]{1,0:T(8,128)S(1)}, u32[]{:S(2)}, u32[]{:S(2)}) collective-permute-start(f32[48,128]{1,0:T(8,128)S(1)} %get-tuple-element.22.to_far_ref), channel_id=1, source_target_pairs={{2,4},{4,2},{6,8},{8,6},{10,12},{12,10},{14,16},{16,14},{18,20},{2... | collective-permute-start | bytes 73736 | tf_op jit(solution)/shard_map/ppermute | solution.py:515
  40.1 12.5 %collective-permute-start.2 = (f32[48,128]{1,0:T(8,128)S(1)}, f32[48,128]{1,0:T(8,128)S(1)}, u32[]{:S(2)}, u32[]{:S(2)}) collective-permute-start(f32[48,128]{1,0:T(8,128)S(1)} %get-tuple-element.18._.to_near_ref), channel_id=1, source_target_pairs={{0,2},{2,0},{4,6},{6,4},{8,10},{10,8},{12,14},{14,12},{16,18},{18,... | collective-permute-start | bytes 73736 | tf_op jit(solution)/shard_map/ppermute | solution.py:514
  42.0 0.7 %copy-start.4 = (f32[2,1,128]{2,1,0:T(1,128)S(1)}, f32[2,1,128]{2,1,0:T(1,128)}, u32[]{:S(2)}) copy-start(f32[2,1,128]{2,1,0:T(1,128)} %weight_ref.1) | copy-start | bytes 3076
  48.9 3.7 %copy-start.6 = (f32[5,5]{1,0:T(8,128)S(1)}, f32[5,5]{1,0:T(8,128)}, u32[]{:S(2)}) copy-start(f32[5,5]{1,0:T(8,128)} %mixing_ref.1) | copy-start | bytes 304
  48.9 10.5 %all-to-all-start.2 = ((f32[16,2,128]{2,1,0:T(2,128)}), f32[16,2,128]{2,1,0:T(2,128)S(1)}, u32[]{:S(2)}, u32[]{:S(2)}) async-start(f32[16,2,128]{2,1,0:T(2,128)} %get-tuple-element.19), calls=%async_computation.2 | async-start | bytes 32768 | tf_op jit(solution)/shard_map/all_to_all | solution.py:520

commit v6 on v5

--- a/solution.py
+++ b/solution.py
@@ -9,6 +9,8 @@
 NB = 32
 SUBCYCLES = 4
 LANES = 128
+HALF = 64
+FY = ("z", "core")
 
 DIFFUSION = 0.25
 TRANSPORT = 0.5
@@ -129,6 +131,26 @@
     return jnp.where(lane < LANES // 2, pltpu.roll(rows, LANES // 2, axis=1), rows)
 
 
+def halved(x, core):
+    keep = jnp.where(core == 0, x[: NB // 2], x[NB // 2 :])
+    move = jnp.where(core == 0, x[NB // 2 :], x[: NB // 2])
+    lane = lax.broadcasted_iota(jnp.int32, keep.shape, 1)
+    return jnp.where((lane < HALF) == (core == 0), keep, pltpu.roll(move, HALF, axis=1))
+
+
+def doubled(rows):
+    lane = lax.broadcasted_iota(jnp.int32, rows.shape, 1)
+    moved = pltpu.roll(rows, HALF, axis=1)
+    return jnp.where(lane < HALF, rows, moved), jnp.where(lane < HALF, moved, rows)
+
+
+def joined(first, second):
+    lane = lax.broadcasted_iota(jnp.int32, first.shape, 1)
+    low = jnp.where(lane < HALF, first, pltpu.roll(second, HALF, axis=1))
+    high = jnp.where(lane < HALF, pltpu.roll(first, HALF, axis=1), second)
+    return low, high
+
+
 def collect_body(offered_ref, out_ref):
     base = (lax.axis_index("fx") * NB).astype(jnp.float32)
     block = lax.broadcasted_iota(jnp.int32, (NB, LANES), 0).astype(jnp.float32) + base
@@ -142,13 +164,15 @@
             slot = (2 * sender + tile) % 4
             sums[slot] = sums[slot] + jnp.where(block == target, load, 0.0)
     total = (sums[0] + sums[1]) + (sums[2] + sums[3])
+    halves = [halved(total, core) for core in range(2)]
     for receiver in range(out_ref.shape[0]):
-        out_ref[receiver] = total
+        out_ref[receiver] = halves[receiver % 2]
 
 
 def couple_body(
     connect_ref, stiff_ref, disp_ref, vel_ref, weight_ref, out_ref, disp_out, vel_out, weight_out
 ):
+    core = lax.axis_index("core")
     elements = stiff_ref.shape[0]
     block = lax.broadcasted_iota(jnp.int32, (NB, elements), 0)
     first = connect_ref[0:1, :]
@@ -156,17 +180,18 @@
     ends = (block == first).astype(jnp.float32) - (block == second).astype(jnp.float32)
     pairs = [(ends * ends[a : a + 1, :]).astype(jnp.bfloat16) for a in range(NB)]
     pairs = jnp.concatenate(pairs, axis=0)
-    out_ref[...] = product(pairs, stiff_ref[...]).reshape(NB, NB, LANES)
-    disp_out[...] = disp_ref[...]
-    vel_out[...] = vel_ref[...]
+    low, high = doubled(stiff_ref[...])
+    force = product(pairs, jnp.where(core == 0, low, high)).reshape(NB, NB, LANES)
+    lane = lax.broadcasted_iota(jnp.int32, (NB, NB // 2, LANES), 2)
+    out_ref[...] = jnp.where(lane < HALF, force[:, : NB // 2, :], force[:, NB // 2 :, :])
+    disp_out[...] = halved(disp_ref[...], core)
+    vel_out[...] = halved(vel_ref[...], core)
     weight_out[...] = weight_ref[...]
 
 
 def shell_body(
-    loads_ref, offered_ref, couple_ref, disp_ref, vel_ref, _, disp_out, vel_out, wall_out
+    loads_ref, wanted_ref, from_near_ref, couple_ref, disp_ref, vel_ref, last_out, wall_out
 ):
-    base = (lax.axis_index("fx") * NB).astype(jnp.float32)
-    sec = lax.axis_index("sec")
     disp = disp_ref[...]
     vel = vel_ref[...]
     load = loads_ref[0]
@@ -174,50 +199,71 @@
         load = load + loads_ref[sender]
     total = jnp.zeros_like(disp)
     for _ in range(SUBCYCLES):
+        low, high = doubled(disp)
         inner = [jnp.zeros_like(disp) for _ in range(4)]
-        for a in range(NB):
-            inner[a % 4] = inner[a % 4] + couple_ref[a] * disp[a : a + 1, :]
+        for a in range(NB // 2):
+            inner[a % 2] = inner[a % 2] + couple_ref[a] * low[a : a + 1, :]
+            inner[2 + a % 2] = inner[2 + a % 2] + couple_ref[NB // 2 + a] * high[a : a + 1, :]
         inner = (inner[0] + inner[1]) + (inner[2] + inner[3])
         vel = vel + SHELL_STEP * (load - inner - DAMPING * vel)
         disp = disp + SHELL_STEP * vel
         total = total + disp
-    wall = total * (1.0 / SUBCYCLES)
-    block = lax.broadcasted_iota(jnp.int32, (NB, LANES), 0).astype(jnp.float32) + base
-    for peer in range(wall_out.shape[0]):
-        targets = targets_of(offered_ref[2 * peer + sec])
-        for tile in range(2):
-            target = targets[4 + 3 * tile : 5 + 3 * tile, :]
-            wanted = jnp.where(block == target, wall, 0.0)
-            wall_out[peer, tile : tile + 1, :] = jnp.sum(wanted, axis=0, keepdims=True)
-    disp_out[...] = disp
-    vel_out[...] = vel
-
-
-def finish_body(walls_ref, weight_ref, part_ref, _, out_ref):
-    wall = walls_ref[0]
-    for owner in range(1, walls_ref.shape[0]):
-        wall = wall + walls_ref[owner]
+    peers = wall_out.shape[0] // 2
+    wall = jnp.concatenate(doubled(total * (1.0 / SUBCYCLES)), axis=0)
+    wanted = jnp.concatenate([wanted_ref[...], from_near_ref[8 * NV + 8 :, :]], axis=0)
+    found = product(wanted[:, :NB], wall)
+    lane = lax.broadcasted_iota(jnp.int32, (peers, LANES), 1)
+    own = jnp.where(lane < HALF, found[:peers], found[peers : 2 * peers])
+    other = jnp.where(lane < HALF, found[2 * peers : 3 * peers], found[3 * peers :])
+    core = lax.axis_index("core")
+    even = jnp.where(core == 0, own, other)
+    odd = jnp.where(core == 0, other, own)
+    for peer in range(peers):
+        wall_out[2 * peer] = even[peer : peer + 1, :]
+        wall_out[2 * peer + 1] = odd[peer : peer + 1, :]
+    last_out[: NB // 2, :] = disp
+    last_out[NB // 2 :, :] = vel
+
+
+def finish_body(
+    walls_ref, weight_ref, part_ref, own_ref, other_ref, _, out_ref, disp_out, vel_out
+):
+    halves = []
+    for core in range(2):
+        wall = walls_ref[core]
+        for owner in range(1, walls_ref.shape[0] // 2):
+            wall = wall + walls_ref[2 * owner + core]
+        halves.append(wall)
+    walls = joined(*halves)
     row = lax.broadcasted_iota(jnp.int32, (8, LANES), 0)
     for tile in range(2):
-        gain = weight_ref[tile] * wall[tile : tile + 1, :]
+        gain = weight_ref[tile] * walls[tile]
         out_ref[0, tile] = part_ref[tile] + jnp.where(row == 0, gain, 0.0)
-
-
-def finish(walls, weight, part, state):
+    core = lax.axis_index("core")
+    first = jnp.where(core == 0, own_ref[...], other_ref[...])
+    second = jnp.where(core == 0, other_ref[...], own_ref[...])
+    for rows, out in ((slice(0, NB // 2), disp_out), (slice(NB // 2, NB), vel_out)):
+        low, high = joined(first[rows], second[rows])
+        out[: NB // 2, :] = low
+        out[NB // 2 :, :] = high
+
+
+def finish(walls, weight, part, own, other, state):
+    block = pl.BlockSpec((NB, LANES), lambda i: (0, 0))
     return pl.pallas_call(
         finish_body,
         grid=(1,),
-        out_shape=f32(*state.shape),
-        in_specs=[VM, VM, VM, ANY],
-        out_specs=pl.BlockSpec((1, 2, 8, LANES), lambda i: (2, 0, 0, 0)),
-        input_output_aliases={3: 0},
+        out_shape=(f32(*state.shape), f32(NB, LANES), f32(NB, LANES)),
+        in_specs=[VM] * 5 + [ANY],
+        out_specs=(pl.BlockSpec((1, 2, 8, LANES), lambda i: (2, 0, 0, 0)), block, block),
+        input_output_aliases={5: 0},
         compiler_params=SMALL,
         cost_estimate=pl.CostEstimate(flops=4096, bytes_accessed=65536, transcendentals=0),
-    )(walls, weight, part, state)
+    )(walls, weight, part, own, other, state)
 
 
 def sides(axis, near, far):
-    even = lax.rem(lax.axis_index(axis), 2) == 0
+    even = lax.rem(lax.axis_index("core" if axis == "fy" else axis), 2) == 0
     return jnp.where(even, far, near), jnp.where(even, near, far)
 
 
@@ -277,10 +323,23 @@
     return product(((position & 31) == y).astype(jnp.float32), lines, axis=1)
 
 
+def wanted_blocks(offered_ref, peers):
+    base = (lax.axis_index("fx") * NB).astype(jnp.float32)
+    sec = lax.axis_index("sec")
+    targets = [targets_of(offered_ref[2 * peer + sec]) for peer in range(peers)]
+    rows = [found[4:5, :] for found in targets] + [found[7:8, :] for found in targets]
+    rows = jnp.concatenate(rows, axis=0)
+    lane = lax.broadcasted_iota(jnp.int32, rows.shape, 1)
+    return ((lane.astype(jnp.float32) + base == rows) & (lane < NB)).astype(jnp.float32)
+
+
 def second_round_body(
-    near_ref, state_ref, far_ref, offered_ref, to_near_ref, to_far_ref, beyond_ref
+    near_ref, state_ref, far_ref, offered_ref, to_near_ref, to_far_ref, beyond_ref, wanted_ref
 ):
     beyond_ref[...] = unpack_columns(offered_ref)
+    wanted = wanted_blocks(offered_ref, wanted_ref.shape[0] // 2)
+    wanted_ref[...] = wanted
+    to_near_ref[8 * NV + 8 :, :] = wanted
     last = state_ref.shape[2] - 1
 
     def put(spot, low, high):
@@ -300,7 +359,7 @@
                 )
         put(8 * NV + place, beyond_ref[low, :], beyond_ref[high, :])
     for out in (to_near_ref, to_far_ref):
-        out[8 * NV + 2 :, :] = jnp.zeros((6, LANES), jnp.float32)
+        out[8 * NV + 2 : 8 * NV + 8, :] = jnp.zeros((6, LANES), jnp.float32)
 
 
 def stencil(center, ahead, behind, others, mixed):
@@ -325,19 +384,20 @@
     packed,
     edge_ref,
 ):
-    top, bottom = sides("fy", to_near_ref[...], to_far_ref[...])
-    before, after = sides("fy", from_near_ref[...], from_far_ref[...])
+    rows = 8 * NV + 8
+    top, bottom = sides("fy", to_near_ref[:rows, :], to_far_ref[...])
+    before, after = sides("fy", from_near_ref[:rows, :], from_far_ref[...])
     beyond = beyond_ref[...]
     pack_columns({(v, xi): state_ref.at[v, xi - 1] for v in range(NV) for xi in (1, 2)}, edge_ref)
     size = state_ref.shape[2]
     end = TOP + size
     sec = lax.axis_index("sec")
     fx = lax.axis_index("fx")
-    fy = lax.axis_index("fy")
+    fy = 2 * lax.axis_index("z") + lax.axis_index("core")
     inside_low = (fx > 0).astype(jnp.float32)
     inside_high = (fx < lax.axis_size("fx") - 1).astype(jnp.float32)
     inside_before = (fy > 0).astype(jnp.float32)
-    inside_after = (fy < lax.axis_size("fy") - 1).astype(jnp.float32)
+    inside_after = (fy < 2 * lax.axis_size("z") - 1).astype(jnp.float32)
     mix = [[mixing_ref[v, w] for w in range(NV)] for v in range(NV)]
 
     lane = lax.broadcasted_iota(jnp.int32, (1, LANES), 1)
@@ -480,7 +540,7 @@
 def shards(
     state, mixing, wall_weight, patch_map, block_map, shell_disp, shell_vel, connect, stiffness
 ):
-    nfx, nfy, nsec = (lax.axis_size(axis) for axis in ("fx", "fy", "sec"))
+    nfx, nfy, nsec = (lax.axis_size(axis) for axis in ("fx", FY, "sec"))
     near_x, far_x, near_y, far_y = (
         [pair for i in range(first, n - 1, 2) for pair in ((i, i + 1), (i + 1, i))]
         for n in (nfx, nfy)
@@ -494,12 +554,14 @@
     near = lax.ppermute(state, "fx", near_x)
     far = lax.ppermute(state, "fx", far_x)
 
-    partial = kernel_call(collect_body, f32(nfy, NB, LANES), [VM])(offered)
-    loads = lax.all_to_all(partial, "fy", 0, 0, tiled=True)
-
-    block = f32(NB, LANES)
+    partial = kernel_call(collect_body, f32(nfy, NB // 2, LANES), [VM])(offered)
+    loads = lax.all_to_all(partial, FY, 0, 0, tiled=True)
+
+    half = f32(NB // 2, LANES)
     couple, disp, vel, weight = kernel_call(
-        couple_body, (f32(NB, NB, LANES), block, block, f32(*wall_weight.shape)), [VM] * 5
+        couple_body,
+        (f32(NB, NB // 2, LANES), half, half, f32(*wall_weight.shape)),
+        [VM] * 5,
     )(
         connect[0].T,
         stiffness[0],
@@ -508,16 +570,20 @@
         wall_weight,
     )
     span = f32(8 * NV + 8, LANES)
-    to_near, to_far, beyond = kernel_call(
-        second_round_body, (span, span, f32(32, LANES)), [VM] * 4, cost=LONG
+    to_near, to_far, beyond, wanted = kernel_call(
+        second_round_body,
+        (f32(8 * NV + 8 + 2 * nfx, LANES), span, f32(32, LANES), f32(2 * nfx, LANES)),
+        [VM] * 4,
+        cost=LONG,
     )(near, state, far, offered)
-    from_near = lax.ppermute(to_near, "fy", near_y)
-    from_far = lax.ppermute(to_far, "fy", far_y)
-
-    new_disp, new_vel, walls = kernel_call(
-        shell_body, (block, block, f32(nfx, 2, LANES)), [VM] * 5 + [ANY]
-    )(loads, offered, couple, disp, vel, to_near)
-    walls = lax.all_to_all(walls, "fx", 0, 0, tiled=True)
+    from_near = lax.ppermute(to_near, FY, near_y)
+    from_far = lax.ppermute(to_far, FY, far_y)
+
+    own, walls = kernel_call(
+        shell_body, (f32(NB, LANES), f32(2 * nfx, 1, LANES)), [VM] * 6
+    )(loads, wanted, from_near, couple, disp, vel)
+    walls = lax.all_to_all(walls, ("fx", "core"), 0, 0, tiled=True)
+    other = lax.ppermute(own, FY, near_y)
 
     fluid, part = kernel_call(
         fluid_body,
@@ -531,25 +597,29 @@
         ],
         cost=LONG,
     )(mixing, near, state, far, beyond, to_near, to_far, from_near, from_far)
-    new_state = finish(walls, weight, part, fluid)
+    new_state, new_disp, new_vel = finish(walls, weight, part, own, other, fluid)
     return (new_state, new_disp.reshape(1, -1), new_vel.reshape(1, -1))
 
 
 def solution(mesh):
+    nfx, nfy, nsec = mesh.devices.shape
+    mesh = jax.sharding.Mesh(
+        mesh.devices.reshape(nfx, nfy // 2, 2, nsec), ("fx", "z", "core", "sec")
+    )
     return jax.shard_map(
         shards,
         mesh=mesh,
         in_specs=(
-            P(None, "fx", "fy", "sec"),
+            P(None, "fx", FY, "sec"),
             P(),
-            P("fx", "fy", "sec"),
-            P("fx", "fy", "sec", None),
-            P("fx", "fy", "sec", None),
+            P("fx", FY, "sec"),
+            P("fx", FY, "sec", None),
+            P("fx", FY, "sec", None),
             P("fx", None),
             P("fx", None),
             P("fx", None, None),
             P("fx", None, None),
         ),
-        out_specs=(P(None, "fx", "fy", "sec"), P("fx", None), P("fx", None)),
+        out_specs=(P(None, "fx", FY, "sec"), P("fx", None), P("fx", None)),
         check_vma=False,
     )

time: 60.5 us -> 58.2 us (0.962)
  waiting for transfers between devices: 12.9 us -> 7.96 us
  starting transfers between devices: 38.7 us -> 40.8 us
    all_to_all x2, waiting for transfers between devices: 9.79 us -> 4.81 us  [the longest x1 2.83 us: shards(): walls = lax.all_to_all(walls, ('fx', 'core'), 0, 0, tiled=True)]
    ppermute x2 -> x3, starting transfers between devices: 5.51 us -> 7.54 us  [the longest x1 3.58 us: shards(): from_far = lax.ppermute(to_far, FY, far_y)]
  transfers between devices with their start and end apart: 7 -> 8, of which waited for: 3 -> 3; matrix products, arithmetic and copies ran while one was open for 0% -> 0% of each run, Pallas kernels for 7% -> 8%
where the time goes in v6:
time: 58.2 us; the launch traced here: 57.7 us
  starting transfers between devices  40.8 us (70%)
  waiting for transfers between devices  7.96 us (14%)
  Pallas kernels  7.42 us (13%)
  between operations  0.83 us (1%)
  local copies, waits for them, and re-layouts  0.67 us (1%)
    all_to_all x1, starting transfers between devices, shards(): loads = lax.all_to_all(partial, FY, 0, 0, tiled=True)  12.7 us
    all_to_all x1, starting transfers between devices, shards(): offered = lax.all_to_all(offered, ('fx', 'sec'), 0, 0, tiled=True)  10.6 us
    ppermute x1, starting transfers between devices, shards(): near = lax.ppermute(state, 'fx', near_x)  5.56 us
    all_to_all x1, starting transfers between devices, shards(): walls = lax.all_to_all(walls, ('fx', 'core'), 0, 0, tiled=True)  3.75 us
    ppermute x1, starting transfers between devices, shards(): from_far = lax.ppermute(to_far, FY, far_y)  3.58 us
    all_to_all x1, waiting for transfers between devices, shards(): offered = lax.all_to_all(offered, ('fx', 'sec'), 0, 0, tiled=True)  3.14 us
    all_to_all x1, waiting for transfers between devices, shards(): walls = lax.all_to_all(walls, ('fx', 'core'), 0, 0, tiled=True)  2.83 us
    ppermute x1, starting transfers between devices, shards(): from_near = lax.ppermute(to_near, FY, near_y)  2.04 us
  transfers between devices with their start and end apart: 8, of which 3 were waited for; matrix products, arithmetic and copies ran while one was open for 0% of the time, Pallas kernels for 8%

profile of v6, /device:TPU:1, one launch (start us, length us, event | category | flops | bytes accessed | tf_op | source)
XLA Modules:
  0.0 57.7 jit_solution(2804323751232753849)
XLA Ops:
  0.6 1.8 %shard_map.112 = f32[32,8,128]{2,1,0:T(8,128)} custom-call(s32[2]{0:T(128)} %bitcast.14, s32[2]{0:T(128)} %bitcast.15, f32[2,1,128]{2,1,0:T(1,128)} %weight_ref.1, f32[5,2,32,128]{3,2,1,0:T(8,128)} %state_ref.3), custom_call_target="tpu_custom_call" | custom-call | flops 20000 | bytes 20000 | tf_op jit(solution)/shard_map/pallas_call | solution.py:114
  2.5 0.0 copy-start
  2.5 10.6 %all-to-all-start = ((f32[32,8,128]{2,1,0:T(8,128)}), f32[32,8,128]{2,1,0:T(8,128)S(1)}, u32[]{:S(2)}, u32[]{:S(2)}) async-start(f32[32,8,128]{2,1,0:T(8,128)} %shard_map.112), calls=%async_computation | async-start | bytes 262144 | tf_op jit(solution)/shard_map/all_to_all | solution.py:553
  13.1 0.0 copy-done
  13.2 0.7 %collective-permute-start.1 = (f32[5,2,32,128]{3,2,1,0:T(8,128)S(1)}, f32[5,2,32,128]{3,2,1,0:T(8,128)S(1)}, u32[]{:S(2)}, u32[]{:S(2)}) collective-permute-start(f32[5,2,32,128]{3,2,1,0:T(8,128)S(1)} %copy-done), channel_id=1, source_target_pairs={{32,64},{64,32},{96,128},{128,96},{160,192},{192,160},{224,256},{2... | collective-permute-start | bytes 491528 | tf_op jit(solution)/shard_map/ppermute | solution.py:555
  13.8 5.6 %collective-permute-start = (f32[5,2,32,128]{3,2,1,0:T(8,128)S(1)}, f32[5,2,32,128]{3,2,1,0:T(8,128)S(1)}, u32[]{:S(2)}, u32[]{:S(2)}) collective-permute-start(f32[5,2,32,128]{3,2,1,0:T(8,128)S(1)} %copy-done), channel_id=1, source_target_pairs={{0,32},{32,0},{64,96},{96,64},{128,160},{160,128},{192,224},{224,1... | collective-permute-start | bytes 491528 | tf_op jit(solution)/shard_map/ppermute | solution.py:554
  19.4 3.1 %all-to-all-done.offered_ref = f32[32,8,128]{2,1,0:T(8,128)S(1)} async-done(((f32[32,8,128]{2,1,0:T(8,128)}), f32[32,8,128]{2,1,0:T(8,128)S(1)}, u32[]{:S(2)}, u32[]{:S(2)}) %all-to-all-start) | async-done | bytes 131104 | tf_op jit(solution)/shard_map/all_to_all | solution.py:553
  22.5 0.9 %shard_map.113 = f32[16,16,128]{2,1,0:T(8,128)} custom-call(f32[32,8,128]{2,1,0:T(8,128)S(1)} %all-to-all-done.offered_ref), custom_call_target="tpu_custom_call" | custom-call | flops 20000 | bytes 20000 | tf_op jit(solution)/shard_map/pallas_call | solution.py:557
  23.4 12.7 %all-to-all-start.1 = ((f32[16,16,128]{2,1,0:T(8,128)}), f32[16,16,128]{2,1,0:T(8,128)S(1)}, u32[]{:S(2)}, u32[]{:S(2)}) async-start(f32[16,16,128]{2,1,0:T(8,128)} %shard_map.113), calls=%async_computation.1 | async-start | bytes 262144 | tf_op jit(solution)/shard_map/all_to_all | solution.py:558
  36.1 0.0 collective-permute-done.1.far_ref
  36.1 0.0 collective-permute-done.near_ref
  36.1 0.0 copy-start.1
  36.1 0.0 copy-start.2
  36.1 0.0 copy-start.3
  36.2 0.0 copy-start.5
  36.2 0.4 shard_map.114
  36.5 2.0 %collective-permute-start.2 = (f32[80,128]{1,0:T(8,128)S(1)}, f32[80,128]{1,0:T(8,128)S(1)}, u32[]{:S(2)}, u32[]{:S(2)}) collective-permute-start(f32[80,128]{1,0:T(8,128)S(1)} %get-tuple-element.19.to_near_ref), channel_id=1, source_target_pairs={{0,2},{2,0},{4,6},{6,4},{8,10},{10,8},{12,14},{14,12},{16,18},{18,... | collective-permute-start | bytes 122888 | tf_op jit(solution)/shard_map/ppermute | solution.py:579
  38.6 3.6 %collective-permute-start.3 = (f32[48,128]{1,0:T(8,128)S(1)}, f32[48,128]{1,0:T(8,128)S(1)}, u32[]{:S(2)}, u32[]{:S(2)}) collective-permute-start(f32[48,128]{1,0:T(8,128)S(1)} %get-tuple-element.26.to_far_ref), channel_id=1, source_target_pairs={{2,4},{4,2},{6,8},{8,6},{10,12},{12,10},{14,16},{16,14},{18,20},{2... | collective-permute-start | bytes 73736 | tf_op jit(solution)/shard_map/ppermute | solution.py:580
  42.2 0.0 copy-start.4
  42.2 0.0 copy-done.1
  42.2 0.0 copy-done.2
  42.2 0.0 copy-done.3
  42.2 0.0 copy-done.5
  42.2 0.6 %copy-done.4 = f32[2,1,128]{2,1,0:T(1,128)S(1)} copy-done((f32[2,1,128]{2,1,0:T(1,128)S(1)}, f32[2,1,128]{2,1,0:T(1,128)}, u32[]{:S(2)}) %copy-start.4) | copy-done | bytes 1048
  42.9 0.4 shard_map.115
  43.3 0.0 collective-permute-done.2.from_near_ref
  43.3 2.0 %all-to-all-done.1.loads_ref = f32[16,16,128]{2,1,0:T(8,128)S(1)} async-done(((f32[16,16,128]{2,1,0:T(8,128)}), f32[16,16,128]{2,1,0:T(8,128)S(1)}, u32[]{:S(2)}, u32[]{:S(2)}) %all-to-all-start.1) | async-done | bytes 131104 | tf_op jit(solution)/shard_map/all_to_all | solution.py:558
  45.3 1.2 %shard_map.116 = (f32[32,128]{1,0:T(8,128)S(1)}, f32[32,1,128]{2,1,0:T(1,128)}) custom-call(f32[16,16,128]{2,1,0:T(8,128)S(1)} %all-to-all-done.1.loads_ref, f32[32,128]{1,0:T(8,128)S(1)} %get-tuple-element.18.wanted_ref, f32[80,128]{1,0:T(8,128)S(1)} %collective-permute-done.2.from_near_ref, f32[32,16,128]{2,1,0:T(8,128)S(1)} %get-tuple-element.20.couple_ref, ...), custom_call_target="tpu_custom_call" | custom-call | flops 20000 | bytes 20000 | tf_op jit(solution)/shard_map/pallas_call | solution.py:582
  46.5 0.0 copy-start.6
  46.5 3.7 %all-to-all-start.2 = ((f32[32,1,128]{2,1,0:T(1,128)}), f32[32,1,128]{2,1,0:T(1,128)S(1)}, u32[]{:S(2)}, u32[]{:S(2)}) async-start(f32[32,1,128]{2,1,0:T(1,128)} %get-tuple-element.23), calls=%async_computation.2 | async-start | bytes 32768 | tf_op jit(solution)/shard_map/all_to_all | solution.py:585
  50.2 1.9 %collective-permute-start.4 = (f32[32,128]{1,0:T(8,128)S(1)}, f32[32,128]{1,0:T(8,128)S(1)}, u32[]{:S(2)}, u32[]{:S(2)}) collective-permute-start(f32[32,128]{1,0:T(8,128)S(1)} %get-tuple-element.28.own_ref), channel_id=1, source_target_pairs={{0,2},{2,0},{4,6},{6,4},{8,10},{10,8},{12,14},{14,12},{16,18},{18,... | collective-permute-start | bytes 49160 | tf_op jit(solution)/shard_map/ppermute | solution.py:586
  52.2 0.0 collective-permute-done.3.from_far_ref
  52.2 0.0 copy-done.6
  52.2 2.0 %shard_map.117 = (f32[5,2,32,128]{3,2,1,0:T(8,128)}, f32[2,8,128]{2,1,0:T(8,128)S(1)}) custom-call(f32[5,5]{1,0:T(8,128)S(1)} %copy-done.6, f32[5,2,32,128]{3,2,1,0:T(8,128)S(1)} %collective-permute-done.near_ref, f32[5,2,32,128]{3,2,1,0:T(8,128)S(1)} %copy-done, f32[5,2,32,128]{3,2,1,0:T(8,128)S(1)} %collective-permute-done.1.far_ref, ...), custom_call_target="tpu_custom_call" | custom-call | flops 3800000000 | bytes 3800000000 | tf_op jit(solution)/shard_map/pallas_call | solution.py:588
  54.2 0.0 collective-permute-done.4.other_ref
  54.2 2.8 %all-to-all-done.2.walls_ref = f32[32,1,128]{2,1,0:T(1,128)S(1)} async-done(((f32[32,1,128]{2,1,0:T(1,128)}), f32[32,1,128]{2,1,0:T(1,128)S(1)}, u32[]{:S(2)}, u32[]{:S(2)}) %all-to-all-start.2) | async-done | bytes 16416 | tf_op jit(solution)/shard_map/all_to_all | solution.py:585
  57.0 0.7 %shard_map.118 = (f32[5,2,32,128]{3,2,1,0:T(8,128)}, f32[32,128]{1,0:T(8,128)}, f32[32,128]{1,0:T(8,128)}) custom-call(f32[32,1,128]{2,1,0:T(1,128)S(1)} %all-to-all-done.2.walls_ref, f32[2,1,128]{2,1,0:T(1,128)S(1)} %get-tuple-element.24.weight_ref, f32[2,8,128]{2,1,0:T(8,128)S(1)} %get-tuple-element.27.part_ref, ...), custom_call_target="tpu_custom_call", output_to_operand_aliasing={{0}: (5, {})} | custom-call | flops 4096 | bytes 65536 | tf_op jit(solution)/shard_map/pallas_call | solution.py:253
Async XLA Ops:
  2.5 10.7 %copy-start = (f32[5,2,32,128]{3,2,1,0:T(8,128)S(1)}, f32[5,2,32,128]{3,2,1,0:T(8,128)}, u32[]{:S(2)}) copy-start(f32[5,2,32,128]{3,2,1,0:T(8,128)} %state_ref.3) | copy-start | bytes 491524
  2.5 20.0 %all-to-all-start = ((f32[32,8,128]{2,1,0:T(8,128)}), f32[32,8,128]{2,1,0:T(8,128)S(1)}, u32[]{:S(2)}, u32[]{:S(2)}) async-start(f32[32,8,128]{2,1,0:T(8,128)} %shard_map.112), calls=%async_computation | async-start | bytes 262144 | tf_op jit(solution)/shard_map/all_to_all | solution.py:553
  13.2 23.0 %collective-permute-start.1 = (f32[5,2,32,128]{3,2,1,0:T(8,128)S(1)}, f32[5,2,32,128]{3,2,1,0:T(8,128)S(1)}, u32[]{:S(2)}, u32[]{:S(2)}) collective-permute-start(f32[5,2,32,128]{3,2,1,0:T(8,128)S(1)} %copy-done), channel_id=1, source_target_pairs={{32,64},{64,32},{96,128},{128,96},{160,192},{192,160},{224,256},{2... | collective-permute-start | bytes 491528 | tf_op jit(solution)/shard_map/ppermute | solution.py:555
  13.8 22.3 %collective-permute-start = (f32[5,2,32,128]{3,2,1,0:T(8,128)S(1)}, f32[5,2,32,128]{3,2,1,0:T(8,128)S(1)}, u32[]{:S(2)}, u32[]{:S(2)}) collective-permute-start(f32[5,2,32,128]{3,2,1,0:T(8,128)S(1)} %copy-done), channel_id=1, source_target_pairs={{0,32},{32,0},{64,96},{96,64},{128,160},{160,128},{192,224},{224,1... | collective-permute-start | bytes 491528 | tf_op jit(solution)/shard_map/ppermute | solution.py:554
  23.4 21.8 %all-to-all-start.1 = ((f32[16,16,128]{2,1,0:T(8,128)}), f32[16,16,128]{2,1,0:T(8,128)S(1)}, u32[]{:S(2)}, u32[]{:S(2)}) async-start(f32[16,16,128]{2,1,0:T(8,128)} %shard_map.113), calls=%async_computation.1 | async-start | bytes 262144 | tf_op jit(solution)/shard_map/all_to_all | solution.py:558
  36.1 6.1 %copy-start.1 = (f32[1,64,128]{2,1,0:T(8,128)S(1)}, f32[1,64,128]{2,1,0:T(8,128)}, u32[]{:S(2)}) copy-start(f32[1,64,128]{2,1,0:T(8,128)} %param.17) | copy-start | bytes 98308
  36.1 6.1 %copy-start.2 = (f32[1,4096]{1,0:T(1,128)S(1)}, f32[1,4096]{1,0:T(1,128)}, u32[]{:S(2)}) copy-start(f32[1,4096]{1,0:T(1,128)} %param.14) | copy-start | bytes 49156
  36.1 6.1 %copy-start.3 = (f32[1,4096]{1,0:T(1,128)S(1)}, f32[1,4096]{1,0:T(1,128)}, u32[]{:S(2)}) copy-start(f32[1,4096]{1,0:T(1,128)} %param.15) | copy-start | bytes 49156
  36.2 6.1 %copy-start.5 = (s32[1,64,2]{1,2,0:T(2,128)S(1)}, s32[1,64,2]{1,2,0:T(2,128)}, u32[]{:S(2)}) copy-start(s32[1,64,2]{1,2,0:T(2,128)} %param.16) | copy-start | bytes 1540
  36.5 6.7 %collective-permute-start.2 = (f32[80,128]{1,0:T(8,128)S(1)}, f32[80,128]{1,0:T(8,128)S(1)}, u32[]{:S(2)}, u32[]{:S(2)}) collective-permute-start(f32[80,128]{1,0:T(8,128)S(1)} %get-tuple-element.19.to_near_ref), channel_id=1, source_target_pairs={{0,2},{2,0},{4,6},{6,4},{8,10},{10,8},{12,14},{14,12},{16,18},{18,... | collective-permute-start | bytes 122888 | tf_op jit(solution)/shard_map/ppermute | solution.py:579
  38.6 13.6 %collective-permute-start.3 = (f32[48,128]{1,0:T(8,128)S(1)}, f32[48,128]{1,0:T(8,128)S(1)}, u32[]{:S(2)}, u32[]{:S(2)}) collective-permute-start(f32[48,128]{1,0:T(8,128)S(1)} %get-tuple-element.26.to_far_ref), channel_id=1, source_target_pairs={{2,4},{4,2},{6,8},{8,6},{10,12},{12,10},{14,16},{16,14},{18,20},{2... | collective-permute-start | bytes 73736 | tf_op jit(solution)/shard_map/ppermute | solution.py:580
  42.2 0.7 %copy-start.4 = (f32[2,1,128]{2,1,0:T(1,128)S(1)}, f32[2,1,128]{2,1,0:T(1,128)}, u32[]{:S(2)}) copy-start(f32[2,1,128]{2,1,0:T(1,128)} %weight_ref.1) | copy-start | bytes 3076
  46.5 5.7 %copy-start.6 = (f32[5,5]{1,0:T(8,128)S(1)}, f32[5,5]{1,0:T(8,128)}, u32[]{:S(2)}) copy-start(f32[5,5]{1,0:T(8,128)} %mixing_ref.1) | copy-start | bytes 304
  46.5 10.5 %all-to-all-start.2 = ((f32[32,1,128]{2,1,0:T(1,128)}), f32[32,1,128]{2,1,0:T(1,128)S(1)}, u32[]{:S(2)}, u32[]{:S(2)}) async-start(f32[32,1,128]{2,1,0:T(1,128)} %get-tuple-element.23), calls=%async_computation.2 | async-start | bytes 32768 | tf_op jit(solution)/shard_map/all_to_all | solution.py:585
  50.2 3.9 %collective-permute-start.4 = (f32[32,128]{1,0:T(8,128)S(1)}, f32[32,128]{1,0:T(8,128)S(1)}, u32[]{:S(2)}, u32[]{:S(2)}) collective-permute-start(f32[32,128]{1,0:T(8,128)S(1)} %get-tuple-element.28.own_ref), channel_id=1, source_target_pairs={{0,2},{2,0},{4,6},{6,4},{8,10},{10,8},{12,14},{14,12},{16,18},{18,... | collective-permute-start | bytes 49160 | tf_op jit(solution)/shard_map/ppermute | solution.py:586

commit v7 on v6

--- a/solution.py
+++ b/solution.py
@@ -181,11 +181,10 @@
     pairs = [(ends * ends[a : a + 1, :]).astype(jnp.bfloat16) for a in range(NB)]
     pairs = jnp.concatenate(pairs, axis=0)
     low, high = doubled(stiff_ref[...])
-    force = product(pairs, jnp.where(core == 0, low, high)).reshape(NB, NB, LANES)
-    lane = lax.broadcasted_iota(jnp.int32, (NB, NB // 2, LANES), 2)
-    out_ref[...] = jnp.where(lane < HALF, force[:, : NB // 2, :], force[:, NB // 2 :, :])
-    disp_out[...] = halved(disp_ref[...], core)
-    vel_out[...] = halved(vel_ref[...], core)
+    out_ref[...] = product(pairs, jnp.where(core == 0, low, high)).reshape(NB, NB, LANES)
+    for source, out in ((disp_ref, disp_out), (vel_ref, vel_out)):
+        low, high = doubled(source[...])
+        out[...] = jnp.where(core == 0, low, high)
     weight_out[...] = weight_ref[...]
 
 
@@ -197,44 +196,39 @@
     load = loads_ref[0]
     for sender in range(1, loads_ref.shape[0]):
         load = load + loads_ref[sender]
+    load = jnp.concatenate(doubled(load), axis=0)
     total = jnp.zeros_like(disp)
     for _ in range(SUBCYCLES):
-        low, high = doubled(disp)
         inner = [jnp.zeros_like(disp) for _ in range(4)]
-        for a in range(NB // 2):
-            inner[a % 2] = inner[a % 2] + couple_ref[a] * low[a : a + 1, :]
-            inner[2 + a % 2] = inner[2 + a % 2] + couple_ref[NB // 2 + a] * high[a : a + 1, :]
+        for a in range(NB):
+            inner[a % 4] = inner[a % 4] + couple_ref[a] * disp[a : a + 1, :]
         inner = (inner[0] + inner[1]) + (inner[2] + inner[3])
         vel = vel + SHELL_STEP * (load - inner - DAMPING * vel)
         disp = disp + SHELL_STEP * vel
         total = total + disp
-    peers = wall_out.shape[0] // 2
-    wall = jnp.concatenate(doubled(total * (1.0 / SUBCYCLES)), axis=0)
-    wanted = jnp.concatenate([wanted_ref[...], from_near_ref[8 * NV + 8 :, :]], axis=0)
-    found = product(wanted[:, :NB], wall)
-    lane = lax.broadcasted_iota(jnp.int32, (peers, LANES), 1)
-    own = jnp.where(lane < HALF, found[:peers], found[peers : 2 * peers])
-    other = jnp.where(lane < HALF, found[2 * peers : 3 * peers], found[3 * peers :])
-    core = lax.axis_index("core")
-    even = jnp.where(core == 0, own, other)
-    odd = jnp.where(core == 0, other, own)
-    for peer in range(peers):
-        wall_out[2 * peer] = even[peer : peer + 1, :]
-        wall_out[2 * peer + 1] = odd[peer : peer + 1, :]
-    last_out[: NB // 2, :] = disp
-    last_out[NB // 2 :, :] = vel
+    slots = wall_out.shape[0]
+    wanted = wanted_ref[...] + from_near_ref[8 * NV + 8 :, :]
+    found = jnp.dot(
+        wanted[:, : 3 * NB].astype(jnp.bfloat16),
+        jnp.concatenate(terms(total * (1.0 / SUBCYCLES)), axis=0),
+        preferred_element_type=jnp.float32,
+    )
+    lane = lax.broadcasted_iota(jnp.int32, (slots, LANES), 1)
+    wall_out[...] = jnp.where(lane < HALF, found[:slots], found[slots:])
+    lane = lax.broadcasted_iota(jnp.int32, (NB // 2, LANES), 1)
+    last_out[: NB // 2, :] = jnp.where(lane < HALF, disp[: NB // 2], disp[NB // 2 :])
+    last_out[NB // 2 :, :] = jnp.where(lane < HALF, vel[: NB // 2], vel[NB // 2 :])
 
 
 def finish_body(
     walls_ref, weight_ref, part_ref, own_ref, other_ref, _, out_ref, disp_out, vel_out
 ):
-    halves = []
-    for core in range(2):
-        wall = walls_ref[core]
-        for owner in range(1, walls_ref.shape[0] // 2):
-            wall = wall + walls_ref[2 * owner + core]
-        halves.append(wall)
-    walls = joined(*halves)
+    wall = walls_ref[0:8, :]
+    for first in range(8, walls_ref.shape[0], 8):
+        wall = wall + walls_ref[first : first + 8, :]
+    wall = wall + pltpu.roll(wall, 4, axis=0)
+    wall = wall + pltpu.roll(wall, 2, axis=0)
+    walls = joined(wall[0:1, :], wall[1:2, :])
     row = lax.broadcasted_iota(jnp.int32, (8, LANES), 0)
     for tile in range(2):
         gain = weight_ref[tile] * walls[tile]
@@ -327,17 +321,19 @@
     base = (lax.axis_index("fx") * NB).astype(jnp.float32)
     sec = lax.axis_index("sec")
     targets = [targets_of(offered_ref[2 * peer + sec]) for peer in range(peers)]
-    rows = [found[4:5, :] for found in targets] + [found[7:8, :] for found in targets]
+    rows = [found[row : row + 1, :] for row in (4, 7) for found in targets for _ in range(2)]
     rows = jnp.concatenate(rows, axis=0)
     lane = lax.broadcasted_iota(jnp.int32, rows.shape, 1)
-    return ((lane.astype(jnp.float32) + base == rows) & (lane < NB)).astype(jnp.float32)
+    here = (lax.broadcasted_iota(jnp.int32, rows.shape, 0) & 1) == lax.axis_index("core")
+    asked = (lane & (NB - 1)).astype(jnp.float32) + base == rows
+    return (asked & here & (lane < 3 * NB)).astype(jnp.float32)
 
 
 def second_round_body(
     near_ref, state_ref, far_ref, offered_ref, to_near_ref, to_far_ref, beyond_ref, wanted_ref
 ):
     beyond_ref[...] = unpack_columns(offered_ref)
-    wanted = wanted_blocks(offered_ref, wanted_ref.shape[0] // 2)
+    wanted = wanted_blocks(offered_ref, wanted_ref.shape[0] // 4)
     wanted_ref[...] = wanted
     to_near_ref[8 * NV + 8 :, :] = wanted
     last = state_ref.shape[2] - 1
@@ -557,10 +553,10 @@
     partial = kernel_call(collect_body, f32(nfy, NB // 2, LANES), [VM])(offered)
     loads = lax.all_to_all(partial, FY, 0, 0, tiled=True)
 
-    half = f32(NB // 2, LANES)
+    block = f32(NB, LANES)
     couple, disp, vel, weight = kernel_call(
         couple_body,
-        (f32(NB, NB // 2, LANES), half, half, f32(*wall_weight.shape)),
+        (f32(NB, NB, LANES), block, block, f32(*wall_weight.shape)),
         [VM] * 5,
     )(
         connect[0].T,
@@ -572,7 +568,7 @@
     span = f32(8 * NV + 8, LANES)
     to_near, to_far, beyond, wanted = kernel_call(
         second_round_body,
-        (f32(8 * NV + 8 + 2 * nfx, LANES), span, f32(32, LANES), f32(2 * nfx, LANES)),
+        (f32(8 * NV + 8 + 4 * nfx, LANES), span, f32(32, LANES), f32(4 * nfx, LANES)),
         [VM] * 4,
         cost=LONG,
     )(near, state, far, offered)
@@ -580,7 +576,7 @@
     from_far = lax.ppermute(to_far, FY, far_y)
 
     own, walls = kernel_call(
-        shell_body, (f32(NB, LANES), f32(2 * nfx, 1, LANES)), [VM] * 6
+        shell_body, (f32(NB, LANES), f32(2 * nfx, LANES)), [VM] * 6
     )(loads, wanted, from_near, couple, disp, vel)
     walls = lax.all_to_all(walls, ("fx", "core"), 0, 0, tiled=True)
     other = lax.ppermute(own, FY, near_y)

time: 58.2 us -> 58 us (level)
  no operation moved by 1% of the time
where the time goes in v7:
time: 58 us; the launch traced here: 57.5 us
  starting transfers between devices  40.8 us (70%)
  waiting for transfers between devices  7.98 us (14%)
  Pallas kernels  7.16 us (12%)
  between operations  0.83 us (1%)
  local copies, waits for them, and re-layouts  0.67 us (1%)
    all_to_all x1, starting transfers between devices, shards(): loads = lax.all_to_all(partial, FY, 0, 0, tiled=True)  12.7 us
    all_to_all x1, starting transfers between devices, shards(): offered = lax.all_to_all(offered, ('fx', 'sec'), 0, 0, tiled=True)  10.6 us
    ppermute x1, starting transfers between devices, shards(): near = lax.ppermute(state, 'fx', near_x)  5.56 us
    all_to_all x1, starting transfers between devices, shards(): walls = lax.all_to_all(walls, ('fx', 'core'), 0, 0, tiled=True)  3.75 us
    ppermute x1, starting transfers between devices, shards(): from_far = lax.ppermute(to_far, FY, far_y)  3.58 us
    all_to_all x1, waiting for transfers between devices, shards(): offered = lax.all_to_all(offered, ('fx', 'sec'), 0, 0, tiled=True)  3.14 us
    all_to_all x1, waiting for transfers between devices, shards(): walls = lax.all_to_all(walls, ('fx', 'core'), 0, 0, tiled=True)  2.83 us
    ppermute x1, starting transfers between devices, shards(): from_near = lax.ppermute(to_near, FY, near_y)  2.04 us
  transfers between devices with their start and end apart: 8, of which 3 were waited for; matrix products, arithmetic and copies ran while one was open for 0% of the time, Pallas kernels for 8%

profile of v7, /device:TPU:1, one launch (start us, length us, event | category | flops | bytes accessed | tf_op | source)
XLA Modules:
  0.0 57.5 jit_solution(11883138816759276517)
XLA Ops:
  0.6 1.8 %shard_map.112 = f32[32,8,128]{2,1,0:T(8,128)} custom-call(s32[2]{0:T(128)} %bitcast.19, s32[2]{0:T(128)} %bitcast.20, f32[2,1,128]{2,1,0:T(1,128)} %weight_ref.1, f32[5,2,32,128]{3,2,1,0:T(8,128)} %state_ref.3), custom_call_target="tpu_custom_call" | custom-call | flops 20000 | bytes 20000 | tf_op jit(solution)/shard_map/pallas_call | solution.py:114
  2.5 0.0 copy-start
  2.5 10.6 %all-to-all-start = ((f32[32,8,128]{2,1,0:T(8,128)}), f32[32,8,128]{2,1,0:T(8,128)S(1)}, u32[]{:S(2)}, u32[]{:S(2)}) async-start(f32[32,8,128]{2,1,0:T(8,128)} %shard_map.112), calls=%async_computation | async-start | bytes 262144 | tf_op jit(solution)/shard_map/all_to_all | solution.py:549
  13.1 0.0 copy-done
  13.2 0.7 %collective-permute-start.1 = (f32[5,2,32,128]{3,2,1,0:T(8,128)S(1)}, f32[5,2,32,128]{3,2,1,0:T(8,128)S(1)}, u32[]{:S(2)}, u32[]{:S(2)}) collective-permute-start(f32[5,2,32,128]{3,2,1,0:T(8,128)S(1)} %copy-done), channel_id=1, source_target_pairs={{32,64},{64,32},{96,128},{128,96},{160,192},{192,160},{224,256},{2... | collective-permute-start | bytes 491528 | tf_op jit(solution)/shard_map/ppermute | solution.py:551
  13.8 5.6 %collective-permute-start = (f32[5,2,32,128]{3,2,1,0:T(8,128)S(1)}, f32[5,2,32,128]{3,2,1,0:T(8,128)S(1)}, u32[]{:S(2)}, u32[]{:S(2)}) collective-permute-start(f32[5,2,32,128]{3,2,1,0:T(8,128)S(1)} %copy-done), channel_id=1, source_target_pairs={{0,32},{32,0},{64,96},{96,64},{128,160},{160,128},{192,224},{224,1... | collective-permute-start | bytes 491528 | tf_op jit(solution)/shard_map/ppermute | solution.py:550
  19.4 3.1 %all-to-all-done.offered_ref = f32[32,8,128]{2,1,0:T(8,128)S(1)} async-done(((f32[32,8,128]{2,1,0:T(8,128)}), f32[32,8,128]{2,1,0:T(8,128)S(1)}, u32[]{:S(2)}, u32[]{:S(2)}) %all-to-all-start) | async-done | bytes 131104 | tf_op jit(solution)/shard_map/all_to_all | solution.py:549
  22.5 0.9 %shard_map.113 = f32[16,16,128]{2,1,0:T(8,128)} custom-call(f32[32,8,128]{2,1,0:T(8,128)S(1)} %all-to-all-done.offered_ref), custom_call_target="tpu_custom_call" | custom-call | flops 20000 | bytes 20000 | tf_op jit(solution)/shard_map/pallas_call | solution.py:553
  23.4 12.7 %all-to-all-start.1 = ((f32[16,16,128]{2,1,0:T(8,128)}), f32[16,16,128]{2,1,0:T(8,128)S(1)}, u32[]{:S(2)}, u32[]{:S(2)}) async-start(f32[16,16,128]{2,1,0:T(8,128)} %shard_map.113), calls=%async_computation.1 | async-start | bytes 262144 | tf_op jit(solution)/shard_map/all_to_all | solution.py:554
  36.1 0.0 collective-permute-done.1.far_ref
  36.1 0.0 collective-permute-done.near_ref
  36.1 0.0 copy-start.1
  36.1 0.0 copy-start.2
  36.1 0.0 copy-start.3
  36.2 0.0 copy-start.5
  36.2 0.4 shard_map.114
  36.5 2.0 %collective-permute-start.2 = (f32[112,128]{1,0:T(8,128)S(1)}, f32[112,128]{1,0:T(8,128)S(1)}, u32[]{:S(2)}, u32[]{:S(2)}) collective-permute-start(f32[112,128]{1,0:T(8,128)S(1)} %get-tuple-element.19.to_near_ref), channel_id=1, source_target_pairs={{0,2},{2,0},{4,6},{6,4},{8,10},{10,8},{12,14},{14,12},{16,18},{18,... | collective-permute-start | bytes 172040 | tf_op jit(solution)/shard_map/ppermute | solution.py:575
  38.6 3.6 %collective-permute-start.3 = (f32[48,128]{1,0:T(8,128)S(1)}, f32[48,128]{1,0:T(8,128)S(1)}, u32[]{:S(2)}, u32[]{:S(2)}) collective-permute-start(f32[48,128]{1,0:T(8,128)S(1)} %get-tuple-element.26.to_far_ref), channel_id=1, source_target_pairs={{2,4},{4,2},{6,8},{8,6},{10,12},{12,10},{14,16},{16,14},{18,20},{2... | collective-permute-start | bytes 73736 | tf_op jit(solution)/shard_map/ppermute | solution.py:576
  42.2 0.0 copy-start.4
  42.2 0.0 copy-done.1
  42.2 0.0 copy-done.2
  42.2 0.0 copy-done.3
  42.2 0.0 copy-done.5
  42.2 0.6 %copy-done.4 = f32[2,1,128]{2,1,0:T(1,128)S(1)} copy-done((f32[2,1,128]{2,1,0:T(1,128)S(1)}, f32[2,1,128]{2,1,0:T(1,128)}, u32[]{:S(2)}) %copy-start.4) | copy-done | bytes 1048
  42.8 0.4 shard_map.115
  43.3 0.0 collective-permute-done.2.from_near_ref
  43.3 2.0 %all-to-all-done.1.loads_ref = f32[16,16,128]{2,1,0:T(8,128)S(1)} async-done(((f32[16,16,128]{2,1,0:T(8,128)}), f32[16,16,128]{2,1,0:T(8,128)S(1)}, u32[]{:S(2)}, u32[]{:S(2)}) %all-to-all-start.1) | async-done | bytes 131104 | tf_op jit(solution)/shard_map/all_to_all | solution.py:554
  45.3 1.0 %shard_map.116 = (f32[32,128]{1,0:T(8,128)S(1)}, f32[32,128]{1,0:T(8,128)}) custom-call(f32[16,16,128]{2,1,0:T(8,128)S(1)} %all-to-all-done.1.loads_ref, f32[64,128]{1,0:T(8,128)S(1)} %get-tuple-element.18.wanted_ref, f32[112,128]{1,0:T(8,128)S(1)} %collective-permute-done.2.from_near_ref, f32[32,32,128]{2,1,0:T(8,128)S(1)} %get-tuple-element.20.couple_ref, ...), custom_call_target="tpu_custom_call" | custom-call | flops 20000 | bytes 20000 | tf_op jit(solution)/shard_map/pallas_call | solution.py:578
  46.2 0.0 copy-start.6
  46.2 3.7 %all-to-all-start.2 = ((f32[32,1,128]{2,1,0:T(1,128)}), f32[32,1,128]{2,1,0:T(1,128)S(1)}, u32[]{:S(2)}, u32[]{:S(2)}) async-start(f32[32,1,128]{2,1,0:T(1,128)} %bitcast.8), calls=%async_computation.2 | async-start | bytes 32768 | tf_op jit(solution)/shard_map/all_to_all | solution.py:581
  50.0 1.9 %collective-permute-start.4 = (f32[32,128]{1,0:T(8,128)S(1)}, f32[32,128]{1,0:T(8,128)S(1)}, u32[]{:S(2)}, u32[]{:S(2)}) collective-permute-start(f32[32,128]{1,0:T(8,128)S(1)} %get-tuple-element.28.own_ref), channel_id=1, source_target_pairs={{0,2},{2,0},{4,6},{6,4},{8,10},{10,8},{12,14},{14,12},{16,18},{18,... | collective-permute-start | bytes 49160 | tf_op jit(solution)/shard_map/ppermute | solution.py:582
  51.9 0.0 collective-permute-done.3.from_far_ref
  51.9 0.0 copy-done.6
  52.0 2.0 %shard_map.117 = (f32[5,2,32,128]{3,2,1,0:T(8,128)}, f32[2,8,128]{2,1,0:T(8,128)S(1)}) custom-call(f32[5,5]{1,0:T(8,128)S(1)} %copy-done.6, f32[5,2,32,128]{3,2,1,0:T(8,128)S(1)} %collective-permute-done.near_ref, f32[5,2,32,128]{3,2,1,0:T(8,128)S(1)} %copy-done, f32[5,2,32,128]{3,2,1,0:T(8,128)S(1)} %collective-permute-done.1.far_ref, ...), custom_call_target="tpu_custom_call" | custom-call | flops 3800000000 | bytes 3800000000 | tf_op jit(solution)/shard_map/pallas_call | solution.py:584
  53.9 0.0 collective-permute-done.4.other_ref
  53.9 2.8 %all-to-all-done.2 = f32[32,1,128]{2,1,0:T(1,128)S(1)} async-done(((f32[32,1,128]{2,1,0:T(1,128)}), f32[32,1,128]{2,1,0:T(1,128)S(1)}, u32[]{:S(2)}, u32[]{:S(2)}) %all-to-all-start.2) | async-done | bytes 16416 | tf_op jit(solution)/shard_map/all_to_all | solution.py:581
  56.8 0.7 %shard_map.118 = (f32[5,2,32,128]{3,2,1,0:T(8,128)}, f32[32,128]{1,0:T(8,128)}, f32[32,128]{1,0:T(8,128)}) custom-call(f32[32,128]{1,0:T(8,128)S(1)} %bitcast.14, f32[2,1,128]{2,1,0:T(1,128)S(1)} %get-tuple-element.24.weight_ref, f32[2,8,128]{2,1,0:T(8,128)S(1)} %get-tuple-element.27.part_ref, ...), custom_call_target="tpu_custom_call", output_to_operand_aliasing={{0}: (5, {})} | custom-call | flops 4096 | bytes 65536 | tf_op jit(solution)/shard_map/pallas_call | solution.py:247
Async XLA Ops:
  2.5 10.7 %copy-start = (f32[5,2,32,128]{3,2,1,0:T(8,128)S(1)}, f32[5,2,32,128]{3,2,1,0:T(8,128)}, u32[]{:S(2)}) copy-start(f32[5,2,32,128]{3,2,1,0:T(8,128)} %state_ref.3) | copy-start | bytes 491524
  2.5 20.0 %all-to-all-start = ((f32[32,8,128]{2,1,0:T(8,128)}), f32[32,8,128]{2,1,0:T(8,128)S(1)}, u32[]{:S(2)}, u32[]{:S(2)}) async-start(f32[32,8,128]{2,1,0:T(8,128)} %shard_map.112), calls=%async_computation | async-start | bytes 262144 | tf_op jit(solution)/shard_map/all_to_all | solution.py:549
  13.2 23.0 %collective-permute-start.1 = (f32[5,2,32,128]{3,2,1,0:T(8,128)S(1)}, f32[5,2,32,128]{3,2,1,0:T(8,128)S(1)}, u32[]{:S(2)}, u32[]{:S(2)}) collective-permute-start(f32[5,2,32,128]{3,2,1,0:T(8,128)S(1)} %copy-done), channel_id=1, source_target_pairs={{32,64},{64,32},{96,128},{128,96},{160,192},{192,160},{224,256},{2... | collective-permute-start | bytes 491528 | tf_op jit(solution)/shard_map/ppermute | solution.py:551
  13.8 22.3 %collective-permute-start = (f32[5,2,32,128]{3,2,1,0:T(8,128)S(1)}, f32[5,2,32,128]{3,2,1,0:T(8,128)S(1)}, u32[]{:S(2)}, u32[]{:S(2)}) collective-permute-start(f32[5,2,32,128]{3,2,1,0:T(8,128)S(1)} %copy-done), channel_id=1, source_target_pairs={{0,32},{32,0},{64,96},{96,64},{128,160},{160,128},{192,224},{224,1... | collective-permute-start | bytes 491528 | tf_op jit(solution)/shard_map/ppermute | solution.py:550
  23.4 21.8 %all-to-all-start.1 = ((f32[16,16,128]{2,1,0:T(8,128)}), f32[16,16,128]{2,1,0:T(8,128)S(1)}, u32[]{:S(2)}, u32[]{:S(2)}) async-start(f32[16,16,128]{2,1,0:T(8,128)} %shard_map.113), calls=%async_computation.1 | async-start | bytes 262144 | tf_op jit(solution)/shard_map/all_to_all | solution.py:554
  36.1 6.1 %copy-start.1 = (f32[1,64,128]{2,1,0:T(8,128)S(1)}, f32[1,64,128]{2,1,0:T(8,128)}, u32[]{:S(2)}) copy-start(f32[1,64,128]{2,1,0:T(8,128)} %param.17) | copy-start | bytes 98308
  36.1 6.1 %copy-start.2 = (f32[1,4096]{1,0:T(1,128)S(1)}, f32[1,4096]{1,0:T(1,128)}, u32[]{:S(2)}) copy-start(f32[1,4096]{1,0:T(1,128)} %param.14) | copy-start | bytes 49156
  36.1 6.0 %copy-start.3 = (f32[1,4096]{1,0:T(1,128)S(1)}, f32[1,4096]{1,0:T(1,128)}, u32[]{:S(2)}) copy-start(f32[1,4096]{1,0:T(1,128)} %param.15) | copy-start | bytes 49156
  36.2 6.0 %copy-start.5 = (s32[1,64,2]{1,2,0:T(2,128)S(1)}, s32[1,64,2]{1,2,0:T(2,128)}, u32[]{:S(2)}) copy-start(s32[1,64,2]{1,2,0:T(2,128)} %param.16) | copy-start | bytes 1540
  36.5 6.7 %collective-permute-start.2 = (f32[112,128]{1,0:T(8,128)S(1)}, f32[112,128]{1,0:T(8,128)S(1)}, u32[]{:S(2)}, u32[]{:S(2)}) collective-permute-start(f32[112,128]{1,0:T(8,128)S(1)} %get-tuple-element.19.to_near_ref), channel_id=1, source_target_pairs={{0,2},{2,0},{4,6},{6,4},{8,10},{10,8},{12,14},{14,12},{16,18},{18,... | collective-permute-start | bytes 172040 | tf_op jit(solution)/shard_map/ppermute | solution.py:575
  38.6 13.4 %collective-permute-start.3 = (f32[48,128]{1,0:T(8,128)S(1)}, f32[48,128]{1,0:T(8,128)S(1)}, u32[]{:S(2)}, u32[]{:S(2)}) collective-permute-start(f32[48,128]{1,0:T(8,128)S(1)} %get-tuple-element.26.to_far_ref), channel_id=1, source_target_pairs={{2,4},{4,2},{6,8},{8,6},{10,12},{12,10},{14,16},{16,14},{18,20},{2... | collective-permute-start | bytes 73736 | tf_op jit(solution)/shard_map/ppermute | solution.py:576
  42.2 0.7 %copy-start.4 = (f32[2,1,128]{2,1,0:T(1,128)S(1)}, f32[2,1,128]{2,1,0:T(1,128)}, u32[]{:S(2)}) copy-start(f32[2,1,128]{2,1,0:T(1,128)} %weight_ref.1) | copy-start | bytes 3076
  46.2 5.7 %copy-start.6 = (f32[5,5]{1,0:T(8,128)S(1)}, f32[5,5]{1,0:T(8,128)}, u32[]{:S(2)}) copy-start(f32[5,5]{1,0:T(8,128)} %mixing_ref.1) | copy-start | bytes 304
  46.2 10.5 %all-to-all-start.2 = ((f32[32,1,128]{2,1,0:T(1,128)}), f32[32,1,128]{2,1,0:T(1,128)S(1)}, u32[]{:S(2)}, u32[]{:S(2)}) async-start(f32[32,1,128]{2,1,0:T(1,128)} %bitcast.8), calls=%async_computation.2 | async-start | bytes 32768 | tf_op jit(solution)/shard_map/all_to_all | solution.py:581
  50.0 3.9 %collective-permute-start.4 = (f32[32,128]{1,0:T(8,128)S(1)}, f32[32,128]{1,0:T(8,128)S(1)}, u32[]{:S(2)}, u32[]{:S(2)}) collective-permute-start(f32[32,128]{1,0:T(8,128)S(1)} %get-tuple-element.28.own_ref), channel_id=1, source_target_pairs={{0,2},{2,0},{4,6},{6,4},{8,10},{10,8},{12,14},{14,12},{16,18},{18,... | collective-permute-start | bytes 49160 | tf_op jit(solution)/shard_map/ppermute | solution.py:582

commit v8 on v7

--- a/solution.py
+++ b/solution.py
@@ -166,7 +166,7 @@
     total = (sums[0] + sums[1]) + (sums[2] + sums[3])
     halves = [halved(total, core) for core in range(2)]
     for receiver in range(out_ref.shape[0]):
-        out_ref[receiver] = halves[receiver % 2]
+        out_ref[receiver] = halves[receiver // (out_ref.shape[0] // 2)]
 
 
 def couple_body(
@@ -193,10 +193,10 @@
 ):
     disp = disp_ref[...]
     vel = vel_ref[...]
-    load = loads_ref[0]
-    for sender in range(1, loads_ref.shape[0]):
-        load = load + loads_ref[sender]
-    load = jnp.concatenate(doubled(load), axis=0)
+    parts = [loads_ref[sender] for sender in range(loads_ref.shape[0])]
+    while len(parts) > 1:
+        parts = [sum(parts[i + 1 : i + 2], parts[i]) for i in range(0, len(parts), 2)]
+    load = jnp.concatenate(doubled(parts[0]), axis=0)
     total = jnp.zeros_like(disp)
     for _ in range(SUBCYCLES):
         inner = [jnp.zeros_like(disp) for _ in range(4)]
@@ -551,7 +551,7 @@
     far = lax.ppermute(state, "fx", far_x)
 
     partial = kernel_call(collect_body, f32(nfy, NB // 2, LANES), [VM])(offered)
-    loads = lax.all_to_all(partial, FY, 0, 0, tiled=True)
+    loads = lax.all_to_all(partial, ("core", "z"), 0, 0, tiled=True)
 
     block = f32(NB, LANES)
     couple, disp, vel, weight = kernel_call(

time: 58 us -> 57.7 us (level)
  waiting for transfers between devices: 7.98 us -> 6.23 us
  starting transfers between devices: 40.8 us -> 42.3 us
    all_to_all x1, waiting for transfers between devices: 1.99 us -> 0.13 us  [shards(): loads = lax.all_to_all(partial, ('core', 'z'), 0, 0, tiled=True)]
    all_to_all x1, starting transfers between devices: 3.75 us -> 4.89 us  [shards(): walls = lax.all_to_all(walls, ('fx', 'core'), 0, 0, tiled=True)]
where the time goes in v8:
time: 57.7 us; the launch traced here: 57.2 us
  starting transfers between devices  42.3 us (73%)
  Pallas kernels  7.15 us (12%)
  waiting for transfers between devices  6.23 us (11%)
  between operations  0.83 us (1%)
  local copies, waits for them, and re-layouts  0.67 us (1%)
    all_to_all x1, starting transfers between devices, shards(): loads = lax.all_to_all(partial, ('core', 'z'), 0, 0, tiled=True)  12.7 us
    all_to_all x1, starting transfers between devices, shards(): offered = lax.all_to_all(offered, ('fx', 'sec'), 0, 0, tiled=True)  10.6 us
    ppermute x1, starting transfers between devices, shards(): near = lax.ppermute(state, 'fx', near_x)  5.56 us
    all_to_all x1, starting transfers between devices, shards(): walls = lax.all_to_all(walls, ('fx', 'core'), 0, 0, tiled=True)  4.89 us
    ppermute x1, starting transfers between devices, shards(): from_far = lax.ppermute(to_far, FY, far_y)  3.58 us
    all_to_all x1, waiting for transfers between devices, shards(): offered = lax.all_to_all(offered, ('fx', 'sec'), 0, 0, tiled=True)  3.14 us
    all_to_all x1, waiting for transfers between devices, shards(): walls = lax.all_to_all(walls, ('fx', 'core'), 0, 0, tiled=True)  2.96 us
    ppermute x1, starting transfers between devices, shards(): other = lax.ppermute(own, FY, near_y)  2.26 us
  transfers between devices with their start and end apart: 8, of which 3 were waited for; matrix products, arithmetic and copies ran while one was open for 0% of the time, Pallas kernels for 8%

profile of v8, /device:TPU:1, one launch (start us, length us, event | category | flops | bytes accessed | tf_op | source)
XLA Modules:
  0.0 57.2 jit_solution(8990170298634632414)
XLA Ops:
  0.6 1.8 %shard_map.112 = f32[32,8,128]{2,1,0:T(8,128)} custom-call(s32[2]{0:T(128)} %bitcast.19, s32[2]{0:T(128)} %bitcast.20, f32[2,1,128]{2,1,0:T(1,128)} %weight_ref.1, f32[5,2,32,128]{3,2,1,0:T(8,128)} %state_ref.3), custom_call_target="tpu_custom_call" | custom-call | flops 20000 | bytes 20000 | tf_op jit(solution)/shard_map/pallas_call | solution.py:114
  2.5 0.0 copy-start
  2.5 10.6 %all-to-all-start = ((f32[32,8,128]{2,1,0:T(8,128)}), f32[32,8,128]{2,1,0:T(8,128)S(1)}, u32[]{:S(2)}, u32[]{:S(2)}) async-start(f32[32,8,128]{2,1,0:T(8,128)} %shard_map.112), calls=%async_computation | async-start | bytes 262144 | tf_op jit(solution)/shard_map/all_to_all | solution.py:549
  13.1 0.0 copy-done
  13.2 0.7 %collective-permute-start.1 = (f32[5,2,32,128]{3,2,1,0:T(8,128)S(1)}, f32[5,2,32,128]{3,2,1,0:T(8,128)S(1)}, u32[]{:S(2)}, u32[]{:S(2)}) collective-permute-start(f32[5,2,32,128]{3,2,1,0:T(8,128)S(1)} %copy-done), channel_id=1, source_target_pairs={{32,64},{64,32},{96,128},{128,96},{160,192},{192,160},{224,256},{2... | collective-permute-start | bytes 491528 | tf_op jit(solution)/shard_map/ppermute | solution.py:551
  13.8 5.6 %collective-permute-start = (f32[5,2,32,128]{3,2,1,0:T(8,128)S(1)}, f32[5,2,32,128]{3,2,1,0:T(8,128)S(1)}, u32[]{:S(2)}, u32[]{:S(2)}) collective-permute-start(f32[5,2,32,128]{3,2,1,0:T(8,128)S(1)} %copy-done), channel_id=1, source_target_pairs={{0,32},{32,0},{64,96},{96,64},{128,160},{160,128},{192,224},{224,1... | collective-permute-start | bytes 491528 | tf_op jit(solution)/shard_map/ppermute | solution.py:550
  19.4 3.1 %all-to-all-done.offered_ref = f32[32,8,128]{2,1,0:T(8,128)S(1)} async-done(((f32[32,8,128]{2,1,0:T(8,128)}), f32[32,8,128]{2,1,0:T(8,128)S(1)}, u32[]{:S(2)}, u32[]{:S(2)}) %all-to-all-start) | async-done | bytes 131104 | tf_op jit(solution)/shard_map/all_to_all | solution.py:549
  22.5 0.9 %shard_map.113 = f32[16,16,128]{2,1,0:T(8,128)} custom-call(f32[32,8,128]{2,1,0:T(8,128)S(1)} %all-to-all-done.offered_ref), custom_call_target="tpu_custom_call" | custom-call | flops 20000 | bytes 20000 | tf_op jit(solution)/shard_map/pallas_call | solution.py:553
  23.4 12.7 %all-to-all-start.1 = ((f32[16,16,128]{2,1,0:T(8,128)}), f32[16,16,128]{2,1,0:T(8,128)S(1)}, u32[]{:S(2)}, u32[]{:S(2)}) async-start(f32[16,16,128]{2,1,0:T(8,128)} %shard_map.113), calls=%async_computation.1 | async-start | bytes 262144 | tf_op jit(solution)/shard_map/all_to_all | solution.py:554
  36.1 0.0 collective-permute-done.1.far_ref
  36.1 0.0 collective-permute-done.near_ref
  36.1 0.0 copy-start.1
  36.1 0.0 copy-start.2
  36.1 0.0 copy-start.3
  36.2 0.0 copy-start.5
  36.2 0.4 shard_map.114
  36.5 2.0 %collective-permute-start.2 = (f32[112,128]{1,0:T(8,128)S(1)}, f32[112,128]{1,0:T(8,128)S(1)}, u32[]{:S(2)}, u32[]{:S(2)}) collective-permute-start(f32[112,128]{1,0:T(8,128)S(1)} %get-tuple-element.19.to_near_ref), channel_id=1, source_target_pairs={{0,2},{2,0},{4,6},{6,4},{8,10},{10,8},{12,14},{14,12},{16,18},{18,... | collective-permute-start | bytes 172040 | tf_op jit(solution)/shard_map/ppermute | solution.py:575
  38.6 3.6 %collective-permute-start.3 = (f32[48,128]{1,0:T(8,128)S(1)}, f32[48,128]{1,0:T(8,128)S(1)}, u32[]{:S(2)}, u32[]{:S(2)}) collective-permute-start(f32[48,128]{1,0:T(8,128)S(1)} %get-tuple-element.26.to_far_ref), channel_id=1, source_target_pairs={{2,4},{4,2},{6,8},{8,6},{10,12},{12,10},{14,16},{16,14},{18,20},{2... | collective-permute-start | bytes 73736 | tf_op jit(solution)/shard_map/ppermute | solution.py:576
  42.2 0.0 copy-start.4
  42.2 0.0 copy-done.1
  42.2 0.0 copy-done.2
  42.2 0.0 copy-done.3
  42.2 0.0 copy-done.5
  42.2 0.6 %copy-done.4 = f32[2,1,128]{2,1,0:T(1,128)S(1)} copy-done((f32[2,1,128]{2,1,0:T(1,128)S(1)}, f32[2,1,128]{2,1,0:T(1,128)}, u32[]{:S(2)}) %copy-start.4) | copy-done | bytes 1048
  42.8 0.4 shard_map.115
  43.3 0.0 collective-permute-done.2.from_near_ref
  43.3 0.1 all-to-all-done.1.loads_ref
  43.4 1.0 %shard_map.116 = (f32[32,128]{1,0:T(8,128)S(1)}, f32[32,128]{1,0:T(8,128)}) custom-call(f32[16,16,128]{2,1,0:T(8,128)S(1)} %all-to-all-done.1.loads_ref, f32[64,128]{1,0:T(8,128)S(1)} %get-tuple-element.18.wanted_ref, f32[112,128]{1,0:T(8,128)S(1)} %collective-permute-done.2.from_near_ref, f32[32,32,128]{2,1,0:T(8,128)S(1)} %get-tuple-element.20.couple_ref, ...), custom_call_target="tpu_custom_call" | custom-call | flops 20000 | bytes 20000 | tf_op jit(solution)/shard_map/pallas_call | solution.py:578
  44.4 0.0 copy-start.6
  44.4 4.9 %all-to-all-start.2 = ((f32[32,1,128]{2,1,0:T(1,128)}), f32[32,1,128]{2,1,0:T(1,128)S(1)}, u32[]{:S(2)}, u32[]{:S(2)}) async-start(f32[32,1,128]{2,1,0:T(1,128)} %bitcast.8), calls=%async_computation.2 | async-start | bytes 32768 | tf_op jit(solution)/shard_map/all_to_all | solution.py:581
  49.3 2.3 %collective-permute-start.4 = (f32[32,128]{1,0:T(8,128)S(1)}, f32[32,128]{1,0:T(8,128)S(1)}, u32[]{:S(2)}, u32[]{:S(2)}) collective-permute-start(f32[32,128]{1,0:T(8,128)S(1)} %get-tuple-element.28.own_ref), channel_id=1, source_target_pairs={{0,2},{2,0},{4,6},{6,4},{8,10},{10,8},{12,14},{14,12},{16,18},{18,... | collective-permute-start | bytes 49160 | tf_op jit(solution)/shard_map/ppermute | solution.py:582
  51.5 0.0 collective-permute-done.3.from_far_ref
  51.5 0.0 copy-done.6
  51.5 2.0 %shard_map.117 = (f32[5,2,32,128]{3,2,1,0:T(8,128)}, f32[2,8,128]{2,1,0:T(8,128)S(1)}) custom-call(f32[5,5]{1,0:T(8,128)S(1)} %copy-done.6, f32[5,2,32,128]{3,2,1,0:T(8,128)S(1)} %collective-permute-done.near_ref, f32[5,2,32,128]{3,2,1,0:T(8,128)S(1)} %copy-done, f32[5,2,32,128]{3,2,1,0:T(8,128)S(1)} %collective-permute-done.1.far_ref, ...), custom_call_target="tpu_custom_call" | custom-call | flops 3800000000 | bytes 3800000000 | tf_op jit(solution)/shard_map/pallas_call | solution.py:584
  53.5 0.0 collective-permute-done.4.other_ref
  53.5 3.0 %all-to-all-done.2 = f32[32,1,128]{2,1,0:T(1,128)S(1)} async-done(((f32[32,1,128]{2,1,0:T(1,128)}), f32[32,1,128]{2,1,0:T(1,128)S(1)}, u32[]{:S(2)}, u32[]{:S(2)}) %all-to-all-start.2) | async-done | bytes 16416 | tf_op jit(solution)/shard_map/all_to_all | solution.py:581
  56.5 0.7 %shard_map.118 = (f32[5,2,32,128]{3,2,1,0:T(8,128)}, f32[32,128]{1,0:T(8,128)}, f32[32,128]{1,0:T(8,128)}) custom-call(f32[32,128]{1,0:T(8,128)S(1)} %bitcast.14, f32[2,1,128]{2,1,0:T(1,128)S(1)} %get-tuple-element.24.weight_ref, f32[2,8,128]{2,1,0:T(8,128)S(1)} %get-tuple-element.27.part_ref, ...), custom_call_target="tpu_custom_call", output_to_operand_aliasing={{0}: (5, {})} | custom-call | flops 4096 | bytes 65536 | tf_op jit(solution)/shard_map/pallas_call | solution.py:247
Async XLA Ops:
  2.5 10.7 %copy-start = (f32[5,2,32,128]{3,2,1,0:T(8,128)S(1)}, f32[5,2,32,128]{3,2,1,0:T(8,128)}, u32[]{:S(2)}) copy-start(f32[5,2,32,128]{3,2,1,0:T(8,128)} %state_ref.3) | copy-start | bytes 491524
  2.5 20.0 %all-to-all-start = ((f32[32,8,128]{2,1,0:T(8,128)}), f32[32,8,128]{2,1,0:T(8,128)S(1)}, u32[]{:S(2)}, u32[]{:S(2)}) async-start(f32[32,8,128]{2,1,0:T(8,128)} %shard_map.112), calls=%async_computation | async-start | bytes 262144 | tf_op jit(solution)/shard_map/all_to_all | solution.py:549
  13.2 23.0 %collective-permute-start.1 = (f32[5,2,32,128]{3,2,1,0:T(8,128)S(1)}, f32[5,2,32,128]{3,2,1,0:T(8,128)S(1)}, u32[]{:S(2)}, u32[]{:S(2)}) collective-permute-start(f32[5,2,32,128]{3,2,1,0:T(8,128)S(1)} %copy-done), channel_id=1, source_target_pairs={{32,64},{64,32},{96,128},{128,96},{160,192},{192,160},{224,256},{2... | collective-permute-start | bytes 491528 | tf_op jit(solution)/shard_map/ppermute | solution.py:551
  13.8 22.3 %collective-permute-start = (f32[5,2,32,128]{3,2,1,0:T(8,128)S(1)}, f32[5,2,32,128]{3,2,1,0:T(8,128)S(1)}, u32[]{:S(2)}, u32[]{:S(2)}) collective-permute-start(f32[5,2,32,128]{3,2,1,0:T(8,128)S(1)} %copy-done), channel_id=1, source_target_pairs={{0,32},{32,0},{64,96},{96,64},{128,160},{160,128},{192,224},{224,1... | collective-permute-start | bytes 491528 | tf_op jit(solution)/shard_map/ppermute | solution.py:550
  23.4 20.0 %all-to-all-start.1 = ((f32[16,16,128]{2,1,0:T(8,128)}), f32[16,16,128]{2,1,0:T(8,128)S(1)}, u32[]{:S(2)}, u32[]{:S(2)}) async-start(f32[16,16,128]{2,1,0:T(8,128)} %shard_map.113), calls=%async_computation.1 | async-start | bytes 262144 | tf_op jit(solution)/shard_map/all_to_all | solution.py:554
  36.1 6.0 %copy-start.1 = (f32[1,64,128]{2,1,0:T(8,128)S(1)}, f32[1,64,128]{2,1,0:T(8,128)}, u32[]{:S(2)}) copy-start(f32[1,64,128]{2,1,0:T(8,128)} %param.17) | copy-start | bytes 98308
  36.1 6.0 %copy-start.2 = (f32[1,4096]{1,0:T(1,128)S(1)}, f32[1,4096]{1,0:T(1,128)}, u32[]{:S(2)}) copy-start(f32[1,4096]{1,0:T(1,128)} %param.14) | copy-start | bytes 49156
  36.1 6.0 %copy-start.3 = (f32[1,4096]{1,0:T(1,128)S(1)}, f32[1,4096]{1,0:T(1,128)}, u32[]{:S(2)}) copy-start(f32[1,4096]{1,0:T(1,128)} %param.15) | copy-start | bytes 49156
  36.2 6.0 %copy-start.5 = (s32[1,64,2]{1,2,0:T(2,128)S(1)}, s32[1,64,2]{1,2,0:T(2,128)}, u32[]{:S(2)}) copy-start(s32[1,64,2]{1,2,0:T(2,128)} %param.16) | copy-start | bytes 1540
  36.5 6.7 %collective-permute-start.2 = (f32[112,128]{1,0:T(8,128)S(1)}, f32[112,128]{1,0:T(8,128)S(1)}, u32[]{:S(2)}, u32[]{:S(2)}) collective-permute-start(f32[112,128]{1,0:T(8,128)S(1)} %get-tuple-element.19.to_near_ref), channel_id=1, source_target_pairs={{0,2},{2,0},{4,6},{6,4},{8,10},{10,8},{12,14},{14,12},{16,18},{18,... | collective-permute-start | bytes 172040 | tf_op jit(solution)/shard_map/ppermute | solution.py:575
  38.6 13.0 %collective-permute-start.3 = (f32[48,128]{1,0:T(8,128)S(1)}, f32[48,128]{1,0:T(8,128)S(1)}, u32[]{:S(2)}, u32[]{:S(2)}) collective-permute-start(f32[48,128]{1,0:T(8,128)S(1)} %get-tuple-element.26.to_far_ref), channel_id=1, source_target_pairs={{2,4},{4,2},{6,8},{8,6},{10,12},{12,10},{14,16},{16,14},{18,20},{2... | collective-permute-start | bytes 73736 | tf_op jit(solution)/shard_map/ppermute | solution.py:576
  42.2 0.7 %copy-start.4 = (f32[2,1,128]{2,1,0:T(1,128)S(1)}, f32[2,1,128]{2,1,0:T(1,128)}, u32[]{:S(2)}) copy-start(f32[2,1,128]{2,1,0:T(1,128)} %weight_ref.1) | copy-start | bytes 3076
  44.4 7.2 %copy-start.6 = (f32[5,5]{1,0:T(8,128)S(1)}, f32[5,5]{1,0:T(8,128)}, u32[]{:S(2)}) copy-start(f32[5,5]{1,0:T(8,128)} %mixing_ref.1) | copy-start | bytes 304
  44.4 12.1 %all-to-all-start.2 = ((f32[32,1,128]{2,1,0:T(1,128)}), f32[32,1,128]{2,1,0:T(1,128)S(1)}, u32[]{:S(2)}, u32[]{:S(2)}) async-start(f32[32,1,128]{2,1,0:T(1,128)} %bitcast.8), calls=%async_computation.2 | async-start | bytes 32768 | tf_op jit(solution)/shard_map/all_to_all | solution.py:581
  49.3 4.3 %collective-permute-start.4 = (f32[32,128]{1,0:T(8,128)S(1)}, f32[32,128]{1,0:T(8,128)S(1)}, u32[]{:S(2)}, u32[]{:S(2)}) collective-permute-start(f32[32,128]{1,0:T(8,128)S(1)} %get-tuple-element.28.own_ref), channel_id=1, source_target_pairs={{0,2},{2,0},{4,6},{6,4},{8,10},{10,8},{12,14},{14,12},{16,18},{18,... | collective-permute-start | bytes 49160 | tf_op jit(solution)/shard_map/ppermute | solution.py:582

commit v9 on v8

--- a/solution.py
+++ b/solution.py
@@ -221,7 +221,7 @@
 
 
 def finish_body(
-    walls_ref, weight_ref, part_ref, own_ref, other_ref, _, out_ref, disp_out, vel_out
+    walls_ref, weight_ref, part_ref, _, out_ref
 ):
     wall = walls_ref[0:8, :]
     for first in range(8, walls_ref.shape[0], 8):
@@ -233,27 +233,19 @@
     for tile in range(2):
         gain = weight_ref[tile] * walls[tile]
         out_ref[0, tile] = part_ref[tile] + jnp.where(row == 0, gain, 0.0)
-    core = lax.axis_index("core")
-    first = jnp.where(core == 0, own_ref[...], other_ref[...])
-    second = jnp.where(core == 0, other_ref[...], own_ref[...])
-    for rows, out in ((slice(0, NB // 2), disp_out), (slice(NB // 2, NB), vel_out)):
-        low, high = joined(first[rows], second[rows])
-        out[: NB // 2, :] = low
-        out[NB // 2 :, :] = high
-
-
-def finish(walls, weight, part, own, other, state):
-    block = pl.BlockSpec((NB, LANES), lambda i: (0, 0))
+
+
+def finish(walls, weight, part, state):
     return pl.pallas_call(
         finish_body,
         grid=(1,),
-        out_shape=(f32(*state.shape), f32(NB, LANES), f32(NB, LANES)),
-        in_specs=[VM] * 5 + [ANY],
-        out_specs=(pl.BlockSpec((1, 2, 8, LANES), lambda i: (2, 0, 0, 0)), block, block),
-        input_output_aliases={5: 0},
+        out_shape=f32(*state.shape),
+        in_specs=[VM] * 3 + [ANY],
+        out_specs=pl.BlockSpec((1, 2, 8, LANES), lambda i: (2, 0, 0, 0)),
+        input_output_aliases={3: 0},
         compiler_params=SMALL,
         cost_estimate=pl.CostEstimate(flops=4096, bytes_accessed=65536, transcendentals=0),
-    )(walls, weight, part, own, other, state)
+    )(walls, weight, part, state)
 
 
 def sides(axis, near, far):
@@ -363,6 +355,16 @@
     return DIFFUSION * (beside - 6.0 * center) - TRANSPORT * 0.5 * (ahead - behind) + mixed
 
 
+def join_halves(own_ref, other_ref, disp_out, vel_out):
+    core = lax.axis_index("core")
+    first = jnp.where(core == 0, own_ref[...], other_ref[...])
+    second = jnp.where(core == 0, other_ref[...], own_ref[...])
+    for rows, out in ((slice(0, NB // 2), disp_out), (slice(NB // 2, NB), vel_out)):
+        low, high = joined(first[rows], second[rows])
+        out[: NB // 2, :] = low
+        out[NB // 2 :, :] = high
+
+
 def fluid_body(
     mixing_ref,
     near_ref,
@@ -373,13 +375,18 @@
     to_far_ref,
     from_near_ref,
     from_far_ref,
+    own_ref,
+    other_ref,
     out_ref,
     part_ref,
+    disp_out,
+    vel_out,
     field,
     section,
     packed,
     edge_ref,
 ):
+    join_halves(own_ref, other_ref, disp_out, vel_out)
     rows = 8 * NV + 8
     top, bottom = sides("fy", to_near_ref[:rows, :], to_far_ref[...])
     before, after = sides("fy", from_near_ref[:rows, :], from_far_ref[...])
@@ -581,10 +588,10 @@
     walls = lax.all_to_all(walls, ("fx", "core"), 0, 0, tiled=True)
     other = lax.ppermute(own, FY, near_y)
 
-    fluid, part = kernel_call(
+    fluid, part, new_disp, new_vel = kernel_call(
         fluid_body,
-        (f32(*state.shape), f32(2, 8, LANES)),
-        [SM] + [VM] * 8,
+        (f32(*state.shape), f32(2, 8, LANES), block, block),
+        [SM] + [VM] * 10,
         scratch=[
             pltpu.VMEM((NV, 4, ROWS, LANES), jnp.float32),
             pltpu.VMEM((NV, 4, ROWS, LANES), jnp.float32),
@@ -592,8 +599,8 @@
             pltpu.VMEM((32, LANES), jnp.float32),
         ],
         cost=LONG,
-    )(mixing, near, state, far, beyond, to_near, to_far, from_near, from_far)
-    new_state, new_disp, new_vel = finish(walls, weight, part, own, other, fluid)
+    )(mixing, near, state, far, beyond, to_near, to_far, from_near, from_far, own, other)
+    new_state = finish(walls, weight, part, fluid)
     return (new_state, new_disp.reshape(1, -1), new_vel.reshape(1, -1))
 
 

time: 57.7 us -> 59.4 us (1.029)
  waiting for transfers between devices: 6.23 us -> 10.6 us
  starting transfers between devices: 42.3 us -> 39.5 us
    ppermute x1, starting transfers between devices: 5.56 us -> 3.14 us  [shards(): near = lax.ppermute(state, 'fx', near_x)]
    all_to_all x1, waiting for transfers between devices: 3.14 us -> 5.54 us  [shards(): offered = lax.all_to_all(offered, ('fx', 'sec'), 0, 0, tiled=True)]
    all_to_all x1, waiting for transfers between devices: 2.96 us -> 4.95 us  [shards(): walls = lax.all_to_all(walls, ('fx', 'core'), 0, 0, tiled=True)]
    all_to_all x1, starting transfers between devices: 4.89 us -> 3.6 us  [shards(): walls = lax.all_to_all(walls, ('fx', 'core'), 0, 0, tiled=True)]
    ppermute x1, starting transfers between devices: 2.26 us -> 3.17 us  [shards(): other = lax.ppermute(own, FY, near_y)]
where the time goes in v9:
time: 59.4 us; the launch traced here: 58.9 us
  starting transfers between devices  39.5 us (66%)
  waiting for transfers between devices  10.6 us (18%)
  Pallas kernels  7.22 us (12%)
  between operations  0.84 us (1%)
  local copies, waits for them, and re-layouts  0.67 us (1%)
    all_to_all x1, starting transfers between devices, shards(): loads = lax.all_to_all(partial, ('core', 'z'), 0, 0, tiled=True)  12.7 us
    all_to_all x1, starting transfers between devices, shards(): offered = lax.all_to_all(offered, ('fx', 'sec'), 0, 0, tiled=True)  10.6 us
    all_to_all x1, waiting for transfers between devices, shards(): offered = lax.all_to_all(offered, ('fx', 'sec'), 0, 0, tiled=True)  5.54 us
    all_to_all x1, waiting for transfers between devices, shards(): walls = lax.all_to_all(walls, ('fx', 'core'), 0, 0, tiled=True)  4.95 us
    all_to_all x1, starting transfers between devices, shards(): walls = lax.all_to_all(walls, ('fx', 'core'), 0, 0, tiled=True)  3.6 us
    ppermute x1, starting transfers between devices, shards(): from_far = lax.ppermute(to_far, FY, far_y)  3.58 us
    ppermute x1, starting transfers between devices, shards(): other = lax.ppermute(own, FY, near_y)  3.17 us
    ppermute x1, starting transfers between devices, shards(): near = lax.ppermute(state, 'fx', near_x)  3.14 us
  transfers between devices with their start and end apart: 8, of which 3 were waited for; matrix products, arithmetic and copies ran while one was open for 0% of the time, Pallas kernels for 8%

profile of v9, /device:TPU:1, one launch (start us, length us, event | category | flops | bytes accessed | tf_op | source)
XLA Modules:
  0.0 58.9 jit_solution(15925886122960171262)
XLA Ops:
  0.6 1.8 %shard_map.112 = f32[32,8,128]{2,1,0:T(8,128)} custom-call(s32[2]{0:T(128)} %bitcast.19, s32[2]{0:T(128)} %bitcast.20, f32[2,1,128]{2,1,0:T(1,128)} %weight_ref.1, f32[5,2,32,128]{3,2,1,0:T(8,128)} %state_ref.3), custom_call_target="tpu_custom_call" | custom-call | flops 20000 | bytes 20000 | tf_op jit(solution)/shard_map/pallas_call | solution.py:114
  2.5 0.0 copy-start
  2.5 10.6 %all-to-all-start = ((f32[32,8,128]{2,1,0:T(8,128)}), f32[32,8,128]{2,1,0:T(8,128)S(1)}, u32[]{:S(2)}, u32[]{:S(2)}) async-start(f32[32,8,128]{2,1,0:T(8,128)} %shard_map.112), calls=%async_computation | async-start | bytes 262144 | tf_op jit(solution)/shard_map/all_to_all | solution.py:556
  13.1 0.0 copy-done
  13.2 3.1 %collective-permute-start = (f32[5,2,32,128]{3,2,1,0:T(8,128)S(1)}, f32[5,2,32,128]{3,2,1,0:T(8,128)S(1)}, u32[]{:S(2)}, u32[]{:S(2)}) collective-permute-start(f32[5,2,32,128]{3,2,1,0:T(8,128)S(1)} %copy-done), channel_id=1, source_target_pairs={{0,32},{32,0},{64,96},{96,64},{128,160},{160,128},{192,224},{224,1... | collective-permute-start | bytes 491528 | tf_op jit(solution)/shard_map/ppermute | solution.py:557
  16.3 0.7 %collective-permute-start.1 = (f32[5,2,32,128]{3,2,1,0:T(8,128)S(1)}, f32[5,2,32,128]{3,2,1,0:T(8,128)S(1)}, u32[]{:S(2)}, u32[]{:S(2)}) collective-permute-start(f32[5,2,32,128]{3,2,1,0:T(8,128)S(1)} %copy-done), channel_id=1, source_target_pairs={{32,64},{64,32},{96,128},{128,96},{160,192},{192,160},{224,256},{2... | collective-permute-start | bytes 491528 | tf_op jit(solution)/shard_map/ppermute | solution.py:558
  17.0 5.5 %all-to-all-done.offered_ref = f32[32,8,128]{2,1,0:T(8,128)S(1)} async-done(((f32[32,8,128]{2,1,0:T(8,128)}), f32[32,8,128]{2,1,0:T(8,128)S(1)}, u32[]{:S(2)}, u32[]{:S(2)}) %all-to-all-start) | async-done | bytes 131104 | tf_op jit(solution)/shard_map/all_to_all | solution.py:556
  22.5 0.9 %shard_map.113 = f32[16,16,128]{2,1,0:T(8,128)} custom-call(f32[32,8,128]{2,1,0:T(8,128)S(1)} %all-to-all-done.offered_ref), custom_call_target="tpu_custom_call" | custom-call | flops 20000 | bytes 20000 | tf_op jit(solution)/shard_map/pallas_call | solution.py:560
  23.4 12.7 %all-to-all-start.1 = ((f32[16,16,128]{2,1,0:T(8,128)}), f32[16,16,128]{2,1,0:T(8,128)S(1)}, u32[]{:S(2)}, u32[]{:S(2)}) async-start(f32[16,16,128]{2,1,0:T(8,128)} %shard_map.113), calls=%async_computation.1 | async-start | bytes 262144 | tf_op jit(solution)/shard_map/all_to_all | solution.py:561
  36.1 0.0 collective-permute-done.near_ref
  36.1 0.0 collective-permute-done.1.far_ref
  36.1 0.0 copy-start.1
  36.1 0.0 copy-start.2
  36.1 0.0 copy-start.3
  36.2 0.0 copy-start.5
  36.2 0.4 shard_map.114
  36.5 2.0 %collective-permute-start.2 = (f32[112,128]{1,0:T(8,128)S(1)}, f32[112,128]{1,0:T(8,128)S(1)}, u32[]{:S(2)}, u32[]{:S(2)}) collective-permute-start(f32[112,128]{1,0:T(8,128)S(1)} %get-tuple-element.18.to_near_ref), channel_id=1, source_target_pairs={{0,2},{2,0},{4,6},{6,4},{8,10},{10,8},{12,14},{14,12},{16,18},{18,... | collective-permute-start | bytes 172040 | tf_op jit(solution)/shard_map/ppermute | solution.py:582
  38.6 3.6 %collective-permute-start.3 = (f32[48,128]{1,0:T(8,128)S(1)}, f32[48,128]{1,0:T(8,128)S(1)}, u32[]{:S(2)}, u32[]{:S(2)}) collective-permute-start(f32[48,128]{1,0:T(8,128)S(1)} %get-tuple-element.25.to_far_ref), channel_id=1, source_target_pairs={{2,4},{4,2},{6,8},{8,6},{10,12},{12,10},{14,16},{16,14},{18,20},{2... | collective-permute-start | bytes 73736 | tf_op jit(solution)/shard_map/ppermute | solution.py:583
  42.2 0.0 copy-start.4
  42.2 0.0 copy-done.1
  42.2 0.0 copy-done.2
  42.2 0.0 copy-done.3
  42.2 0.0 copy-done.5
  42.2 0.6 %copy-done.4 = f32[2,1,128]{2,1,0:T(1,128)S(1)} copy-done((f32[2,1,128]{2,1,0:T(1,128)S(1)}, f32[2,1,128]{2,1,0:T(1,128)}, u32[]{:S(2)}) %copy-start.4) | copy-done | bytes 1048
  42.8 0.4 shard_map.115
  43.3 0.0 collective-permute-done.2.from_near_ref
  43.3 0.1 all-to-all-done.1.loads_ref
  43.4 1.0 %shard_map.116 = (f32[32,128]{1,0:T(8,128)S(1)}, f32[32,128]{1,0:T(8,128)}) custom-call(f32[16,16,128]{2,1,0:T(8,128)S(1)} %all-to-all-done.1.loads_ref, f32[64,128]{1,0:T(8,128)S(1)} %get-tuple-element.17.wanted_ref, f32[112,128]{1,0:T(8,128)S(1)} %collective-permute-done.2.from_near_ref, f32[32,32,128]{2,1,0:T(8,128)S(1)} %get-tuple-element.19.couple_ref, ...), custom_call_target="tpu_custom_call" | custom-call | flops 20000 | bytes 20000 | tf_op jit(solution)/shard_map/pallas_call | solution.py:585
  44.4 3.2 %collective-permute-start.4 = (f32[32,128]{1,0:T(8,128)S(1)}, f32[32,128]{1,0:T(8,128)S(1)}, u32[]{:S(2)}, u32[]{:S(2)}) collective-permute-start(f32[32,128]{1,0:T(8,128)S(1)} %get-tuple-element.26.own_ref), channel_id=1, source_target_pairs={{0,2},{2,0},{4,6},{6,4},{8,10},{10,8},{12,14},{14,12},{16,18},{18,... | collective-permute-start | bytes 49160 | tf_op jit(solution)/shard_map/ppermute | solution.py:589
  47.5 0.0 copy-start.6
  47.6 3.6 %all-to-all-start.2 = ((f32[32,1,128]{2,1,0:T(1,128)}), f32[32,1,128]{2,1,0:T(1,128)S(1)}, u32[]{:S(2)}, u32[]{:S(2)}) async-start(f32[32,1,128]{2,1,0:T(1,128)} %bitcast.8), calls=%async_computation.2 | async-start | bytes 32768 | tf_op jit(solution)/shard_map/all_to_all | solution.py:588
  51.2 0.0 collective-permute-done.3.from_far_ref
  51.2 0.0 collective-permute-done.4.other_ref
  51.2 0.0 copy-done.6
  51.2 2.1 %shard_map.117 = (f32[5,2,32,128]{3,2,1,0:T(8,128)}, f32[2,8,128]{2,1,0:T(8,128)S(1)}, f32[32,128]{1,0:T(8,128)}, f32[32,128]{1,0:T(8,128)}) custom-call(f32[5,5]{1,0:T(8,128)S(1)} %copy-done.6, f32[5,2,32,128]{3,2,1,0:T(8,128)S(1)} %collective-permute-done.near_ref, f32[5,2,32,128]{3,2,1,0:T(8,128)S(1)} %copy-done, ...), custom_call_target="tpu_custom_call" | custom-call | flops 3800000000 | bytes 3800000000 | tf_op jit(solution)/shard_map/pallas_call | solution.py:591
  53.3 4.9 %all-to-all-done.2 = f32[32,1,128]{2,1,0:T(1,128)S(1)} async-done(((f32[32,1,128]{2,1,0:T(1,128)}), f32[32,1,128]{2,1,0:T(1,128)S(1)}, u32[]{:S(2)}, u32[]{:S(2)}) %all-to-all-start.2) | async-done | bytes 16416 | tf_op jit(solution)/shard_map/all_to_all | solution.py:588
  58.2 0.7 %shard_map.118 = f32[5,2,32,128]{3,2,1,0:T(8,128)} custom-call(f32[32,128]{1,0:T(8,128)S(1)} %bitcast.14, f32[2,1,128]{2,1,0:T(1,128)S(1)} %get-tuple-element.23.weight_ref, f32[2,8,128]{2,1,0:T(8,128)S(1)} %get-tuple-element.27.part_ref, f32[5,2,32,128]{3,2,1,0:T(8,128)} %get-tuple-element.28._), custom_call_target="tpu_custom_call", output_to_operand_aliasing={{}: (3, {})} | custom-call | flops 4096 | bytes 65536 | tf_op jit(solution)/shard_map/pallas_call | solution.py:239
Async XLA Ops:
  2.5 10.7 %copy-start = (f32[5,2,32,128]{3,2,1,0:T(8,128)S(1)}, f32[5,2,32,128]{3,2,1,0:T(8,128)}, u32[]{:S(2)}) copy-start(f32[5,2,32,128]{3,2,1,0:T(8,128)} %state_ref.3) | copy-start | bytes 491524
  2.5 20.0 %all-to-all-start = ((f32[32,8,128]{2,1,0:T(8,128)}), f32[32,8,128]{2,1,0:T(8,128)S(1)}, u32[]{:S(2)}, u32[]{:S(2)}) async-start(f32[32,8,128]{2,1,0:T(8,128)} %shard_map.112), calls=%async_computation | async-start | bytes 262144 | tf_op jit(solution)/shard_map/all_to_all | solution.py:556
  13.2 23.0 %collective-permute-start = (f32[5,2,32,128]{3,2,1,0:T(8,128)S(1)}, f32[5,2,32,128]{3,2,1,0:T(8,128)S(1)}, u32[]{:S(2)}, u32[]{:S(2)}) collective-permute-start(f32[5,2,32,128]{3,2,1,0:T(8,128)S(1)} %copy-done), channel_id=1, source_target_pairs={{0,32},{32,0},{64,96},{96,64},{128,160},{160,128},{192,224},{224,1... | collective-permute-start | bytes 491528 | tf_op jit(solution)/shard_map/ppermute | solution.py:557
  16.3 19.8 %collective-permute-start.1 = (f32[5,2,32,128]{3,2,1,0:T(8,128)S(1)}, f32[5,2,32,128]{3,2,1,0:T(8,128)S(1)}, u32[]{:S(2)}, u32[]{:S(2)}) collective-permute-start(f32[5,2,32,128]{3,2,1,0:T(8,128)S(1)} %copy-done), channel_id=1, source_target_pairs={{32,64},{64,32},{96,128},{128,96},{160,192},{192,160},{224,256},{2... | collective-permute-start | bytes 491528 | tf_op jit(solution)/shard_map/ppermute | solution.py:558
  23.4 20.0 %all-to-all-start.1 = ((f32[16,16,128]{2,1,0:T(8,128)}), f32[16,16,128]{2,1,0:T(8,128)S(1)}, u32[]{:S(2)}, u32[]{:S(2)}) async-start(f32[16,16,128]{2,1,0:T(8,128)} %shard_map.113), calls=%async_computation.1 | async-start | bytes 262144 | tf_op jit(solution)/shard_map/all_to_all | solution.py:561
  36.1 6.0 %copy-start.1 = (f32[1,64,128]{2,1,0:T(8,128)S(1)}, f32[1,64,128]{2,1,0:T(8,128)}, u32[]{:S(2)}) copy-start(f32[1,64,128]{2,1,0:T(8,128)} %param.17) | copy-start | bytes 98308
  36.1 6.0 %copy-start.2 = (f32[1,4096]{1,0:T(1,128)S(1)}, f32[1,4096]{1,0:T(1,128)}, u32[]{:S(2)}) copy-start(f32[1,4096]{1,0:T(1,128)} %param.14) | copy-start | bytes 49156
  36.1 6.0 %copy-start.3 = (f32[1,4096]{1,0:T(1,128)S(1)}, f32[1,4096]{1,0:T(1,128)}, u32[]{:S(2)}) copy-start(f32[1,4096]{1,0:T(1,128)} %param.15) | copy-start | bytes 49156
  36.2 6.0 %copy-start.5 = (s32[1,64,2]{1,2,0:T(2,128)S(1)}, s32[1,64,2]{1,2,0:T(2,128)}, u32[]{:S(2)}) copy-start(s32[1,64,2]{1,2,0:T(2,128)} %param.16) | copy-start | bytes 1540
  36.5 6.7 %collective-permute-start.2 = (f32[112,128]{1,0:T(8,128)S(1)}, f32[112,128]{1,0:T(8,128)S(1)}, u32[]{:S(2)}, u32[]{:S(2)}) collective-permute-start(f32[112,128]{1,0:T(8,128)S(1)} %get-tuple-element.18.to_near_ref), channel_id=1, source_target_pairs={{0,2},{2,0},{4,6},{6,4},{8,10},{10,8},{12,14},{14,12},{16,18},{18,... | collective-permute-start | bytes 172040 | tf_op jit(solution)/shard_map/ppermute | solution.py:582
  38.6 12.6 %collective-permute-start.3 = (f32[48,128]{1,0:T(8,128)S(1)}, f32[48,128]{1,0:T(8,128)S(1)}, u32[]{:S(2)}, u32[]{:S(2)}) collective-permute-start(f32[48,128]{1,0:T(8,128)S(1)} %get-tuple-element.25.to_far_ref), channel_id=1, source_target_pairs={{2,4},{4,2},{6,8},{8,6},{10,12},{12,10},{14,16},{16,14},{18,20},{2... | collective-permute-start | bytes 73736 | tf_op jit(solution)/shard_map/ppermute | solution.py:583
  42.2 0.7 %copy-start.4 = (f32[2,1,128]{2,1,0:T(1,128)S(1)}, f32[2,1,128]{2,1,0:T(1,128)}, u32[]{:S(2)}) copy-start(f32[2,1,128]{2,1,0:T(1,128)} %weight_ref.1) | copy-start | bytes 3076
  44.4 6.8 %collective-permute-start.4 = (f32[32,128]{1,0:T(8,128)S(1)}, f32[32,128]{1,0:T(8,128)S(1)}, u32[]{:S(2)}, u32[]{:S(2)}) collective-permute-start(f32[32,128]{1,0:T(8,128)S(1)} %get-tuple-element.26.own_ref), channel_id=1, source_target_pairs={{0,2},{2,0},{4,6},{6,4},{8,10},{10,8},{12,14},{14,12},{16,18},{18,... | collective-permute-start | bytes 49160 | tf_op jit(solution)/shard_map/ppermute | solution.py:589
  47.5 3.6 %copy-start.6 = (f32[5,5]{1,0:T(8,128)S(1)}, f32[5,5]{1,0:T(8,128)}, u32[]{:S(2)}) copy-start(f32[5,5]{1,0:T(8,128)} %mixing_ref.1) | copy-start | bytes 304
  47.6 10.6 %all-to-all-start.2 = ((f32[32,1,128]{2,1,0:T(1,128)}), f32[32,1,128]{2,1,0:T(1,128)S(1)}, u32[]{:S(2)}, u32[]{:S(2)}) async-start(f32[32,1,128]{2,1,0:T(1,128)} %bitcast.8), calls=%async_computation.2 | async-start | bytes 32768 | tf_op jit(solution)/shard_map/all_to_all | solution.py:588
